TPU v7x, 32 devices: a whole 2x2x4 slice. The times are simulated.
32 devices in a mesh: groups: 2 (over y), row: 8 (over z, core), col: 2 (over x), sub: 1.
Axes of the slice: x: 2, y: 2, z: 4, core: 2. Of those that a mesh axis runs over, the one named last changes fastest.
Arguments:
- pair: float32 [256, 128, 128], P(('groups', 'row'), 'col'), parts along dimension 0, may hold values from -24 to 24
- residue_mask: int32 [256], P('groups'), parts along dimension 0, may hold values 0 or 1
- out_proj: bfloat16 [128, 4, 128], P(None, None, 'sub'), may hold values from -0.5 to 0.5
- out_gate: bfloat16 [128, 128], replicated, may hold values from -0.5 to 0.5
- out_final: bfloat16 [128, 128], replicated, may hold values from -0.5 to 0.5
- in_proj: bfloat16 [128, 4, 128], P(None, None, 'sub'), may hold values from -0.5 to 0.5
- in_gate: bfloat16 [128, 128], replicated, may hold values from -0.5 to 0.5
- in_final: bfloat16 [128, 128], replicated, may hold values from -0.5 to 0.5
Outputs:
- updated: float32 [256, 128, 128], P(('groups', 'row'), 'col'), parts along dimension 0
There are 2 independent parts, one for each index of `groups`. A program takes and returns all parts, laid end to end along the dimension named above; an argument that names none is the same for every part. Nothing has to cross between parts.
All inputs are finite; a program needn't handle non-finite values.
Results may differ from a plain program's by a relative error of at most 0.0029.
Values may be sent and summed in bfloat16 or wider, within the bound.
No kernel may reach another device: no remote copies, remote signals or barrier semaphores. Data moves between devices by JAX's collectives and lax.ppermute only.
A program may use at most 64 MiB of HBM per device.

v0:
```python
import jax
import jax.numpy as jnp
from jax import lax
from jax.sharding import PartitionSpec as P


def normalize(values, axis):
    average = jnp.mean(values, axis=axis, keepdims=True)
    centred = values - average
    variance = jnp.mean(centred * centred, axis=axis, keepdims=True)
    return centred * lax.rsqrt(variance + 1e-05)


def gated_panels(pair, row_live, col_live, proj):
    normed = normalize(pair, 2).astype(jnp.bfloat16)
    linear = jnp.einsum("ijc,cph->phij", normed, proj, preferred_element_type=jnp.float32)
    pair_mask = row_live[:, None] * col_live[None, :]
    left_panel = (pair_mask * jax.nn.sigmoid(linear[1]) * linear[0]).astype(jnp.bfloat16)
    right_panel = (pair_mask * jax.nn.sigmoid(linear[3]) * linear[2]).astype(jnp.bfloat16)
    return (normed, left_panel, right_panel)


def update_pair(pair, normed, mixed, gate_w, final_w):
    all_channels = lax.all_gather(mixed, "sub", axis=0, tiled=True)
    scaled = normalize(all_channels, 0).astype(jnp.bfloat16)
    projected = jnp.einsum("hij,hc->ijc", scaled, final_w, preferred_element_type=jnp.float32)
    gating = jax.nn.sigmoid(
        jnp.einsum("ijc,cd->ijd", normed, gate_w, preferred_element_type=jnp.float32)
    )
    return pair + gating * projected


def local(pair, residue_mask, out_proj, out_gate, out_final, in_proj, in_gate, in_final):
    row_count = pair.shape[0]
    col_count = pair.shape[1]
    row_start = lax.axis_index("row") * row_count
    col_start = lax.axis_index("col") * col_count
    live = residue_mask.astype(jnp.float32)
    row_live = lax.dynamic_slice_in_dim(live, row_start, row_count, 0)
    col_live = lax.dynamic_slice_in_dim(live, col_start, col_count, 0)
    normed, left_panel, right_panel = gated_panels(pair, row_live, col_live, out_proj)
    left_rows, right_rows = (
        lax.all_gather(left_panel, "col", axis=2, tiled=True),
        lax.all_gather(right_panel, "col", axis=2, tiled=True),
    )
    turned = lax.all_to_all(right_rows, "row", split_axis=2, concat_axis=1, tiled=True)
    own_right = lax.dynamic_slice_in_dim(turned, col_start, col_count, 1)
    matching = left_rows
    mixed = jnp.einsum(
        "hik,hjk->hij",
        matching,
        lax.all_gather(own_right, "row", axis=2, tiled=True),
        preferred_element_type=jnp.float32,
    )
    middle = update_pair(pair, normed, mixed, out_gate, out_final)
    normed, left_panel, right_panel = gated_panels(middle, row_live, col_live, in_proj)
    left_rows = lax.all_gather(left_panel, "col", axis=2, tiled=True)
    turned_left = lax.all_to_all(left_rows, "row", split_axis=2, concat_axis=1, tiled=True)
    matching = turned_left
    mixed_in = jnp.einsum(
        "hki,hkj->hij",
        matching,
        lax.all_gather(right_panel, "row", axis=1, tiled=True),
        preferred_element_type=jnp.float32,
    )
    return update_pair(middle, normed, mixed_in, in_gate, in_final)


def solution(mesh):
    return jax.shard_map(
        local,
        mesh=mesh,
        in_specs=(
            P(("groups", "row"), "col", None),
            P("groups"),
            P(None, None, "sub"),
            P(),
            P(),
            P(None, None, "sub"),
            P(),
            P(),
        ),
        out_specs=P(("groups", "row"), "col", None),
        check_vma=False,
    )
```

profile of v0, /device:TPU:0, one launch (start us, length us, event | category | flops | bytes accessed | tf_op | source)
XLA Modules:
  0.0 155.1 jit_solution(5710169449912707553)
XLA Ops:
  6.5 0.7 convert_element_type.28
  7.4 1.2 reduce_sum.72
  8.6 1.4 multiply_reduce_fusion.3
  10.2 1.5 convolution_bitcast_fusion.1
  12.1 10.0 %all_gather.18 = bf16[128,16,128]{0,2,1:T(8,128)(2,1)S(1)} all-gather(bf16[128,16,64]{0,2,1:T(8,128)(2,1)S(1)} %get-tuple-element.7), channel_id=1, replica_groups=mesh['groups'=2,'row'=8,'col'=2,'sub'=1] {'col'}, dimensions={2}, use_global_device_ids=true | all-gather | bytes 786432 | tf_op jit(solution)/shard_map/all_gather | solution.py:44
  22.5 20.3 %all_to_all.36 = bf16[128,16,128]{0,1,2:T(8,128)(2,1)S(1)} all-to-all(bf16[128,16,128]{0,1,2:T(8,128)(2,1)S(1)} %copy.53), channel_id=1, replica_groups=mesh['groups'=2,'row'=8,'col'=2,'sub'=1] {'row'}, dimensions={2} | all-to-all | bytes 1048576 | tf_op jit(solution)/shard_map/all_to_all | solution.py:46
  42.9 1.3 copy.77
  44.3 8.4 %all_gather.17 = bf16[128,16,128]{0,2,1:T(8,128)(2,1)S(1)} all-gather(bf16[128,16,64]{0,2,1:T(8,128)(2,1)S(1)} %get-tuple-element.8), channel_id=1, replica_groups=mesh['groups'=2,'row'=8,'col'=2,'sub'=1] {'col'}, dimensions={2}, use_global_device_ids=true | all-gather | bytes 786432 | tf_op jit(solution)/shard_map/all_gather | solution.py:43
  52.7 0.4 copy.57
  53.1 0.7 fusion.5
  53.9 37.3 %all-gather.3.cloned.1.call-done = bf16[128,64,128]{1,2,0:T(8,128)(2,1)} async-done(((bf16[128,64,16]{1,2,0:T(8,128)(2,1)}), bf16[128,64,128]{1,2,0:T(8,128)(2,1)}) %all-gather.3.cloned.1.call-update) | async-done | bytes 2097168 | tf_op jit(solution)/shard_map/all_gather | solution.py:52
  91.1 3.4 %fusion.49 = (f32[16,64]{1,0:T(8,128)S(1)}, f32[128,16,64]{2,1,0:T(8,128)S(1)}) fusion(bf16[128,16,128]{2,1,0:T(8,128)(2,1)S(1)} %copy.57, bf16[128,64,128]{1,2,0:T(8,128)(2,1)} %all-gather.3.cloned.1.call-done), kind=kOutput, calls=%fused_computation.81 | convolution fusion | flops 33684480 | bytes 3149824 | tf_op jit(solution)/shard_map/hik,hjk->hij/dot_general | solution.py:49
  94.9 0.4 fusion.50
  95.7 0.5 convolution_bitcast_fusion
  96.2 1.0 fusion.9
  97.3 9.2 %all_gather.20 = bf16[128,16,128]{0,2,1:T(8,128)(2,1)S(1)} all-gather(bf16[128,16,64]{0,2,1:T(8,128)(2,1)S(1)} %get-tuple-element.6), channel_id=1, replica_groups=mesh['groups'=2,'row'=8,'col'=2,'sub'=1] {'col'}, dimensions={2}, use_global_device_ids=true | all-gather | bytes 786432 | tf_op jit(solution)/shard_map/all_gather | solution.py:57
  106.4 1.1 copy.61
  107.6 3.5 %all-to-all-start.1 = ((bf16[128,16,128]{0,1,2:T(8,128)(2,1)}), bf16[128,16,128]{0,1,2:T(8,128)(2,1)S(1)}, u32[]{:S(2)}, u32[]{:S(2)}) async-start(bf16[128,16,128]{0,1,2:T(8,128)(2,1)} %copy.61), calls=%async_computation.1 | async-start | bytes 1048576 | tf_op jit(solution)/shard_map/all_to_all | solution.py:58
  111.1 0.7 fusion.2
  111.8 23.2 %all-to-all-done.1 = bf16[128,16,128]{0,1,2:T(8,128)(2,1)S(1)} async-done(((bf16[128,16,128]{0,1,2:T(8,128)(2,1)}), bf16[128,16,128]{0,1,2:T(8,128)(2,1)S(1)}, u32[]{:S(2)}, u32[]{:S(2)}) %all-to-all-start.1) | async-done | bytes 524320 | tf_op jit(solution)/shard_map/all_to_all | solution.py:58
  135.2 0.7 copy.64
  135.9 7.4 %copy.65 = bf16[128,128,64]{2,1,0:T(8,128)(2,1)} copy(bf16[128,128,64]{0,2,1:T(8,128)(2,1)} %all-gather.5.cloned.1.call-done) | data formatting | bytes 4194304 | tf_op jit(solution)/shard_map/all_gather | solution.py:63
  143.4 3.4 %fusion.51 = (f32[16,64]{1,0:T(8,128)S(1)}, f32[128,16,64]{2,1,0:T(8,128)S(1)}) fusion(bf16[128,128,16]{1,2,0:T(8,128)(2,1)S(1)} %copy.64, bf16[128,128,64]{2,1,0:T(8,128)(2,1)} %copy.65), kind=kOutput, calls=%fused_computation.83 | convolution fusion | flops 33684480 | bytes 3149824 | tf_op jit(solution)/shard_map/hki,hkj->hij/dot_general | solution.py:60
  147.1 1.1 fusion.6
  (38 shorter events, 2.4 us)
Async XLA Ops:
  6.5 89.2 %copy-start = (bf16[128,4,128]{2,1,0:T(4,128)(2,1)S(1)}, bf16[128,4,128]{2,1,0:T(4,128)(2,1)}, u32[]{:S(2)}) copy-start(bf16[128,4,128]{2,1,0:T(4,128)(2,1)} %param.13) | copy-start | bytes 393220
  6.5 84.6 %all-gather.3.cloned.1.call-start = ((), (), s32[]{:S(2)}) async-start(), calls=%async_computation.2 | async-start | bytes 4718592 | tf_op jit(solution)/shard_map/all_gather | solution.py:52
  12.0 41.1 %copy-start.1 = (f32[16,64,128]{2,1,0:T(8,128)S(1)}, f32[16,64,128]{2,1,0:T(8,128)}, u32[]{:S(2)}) copy-start(f32[16,64,128]{2,1,0:T(8,128)} %param.8) | copy-start | bytes 1572868
  12.1 41.1 %copy-start.4 = (bf16[128,128]{1,0:T(8,128)(2,1)S(1)}, bf16[128,128]{1,0:T(8,128)(2,1)}, u32[]{:S(2)}) copy-start(bf16[128,128]{1,0:T(8,128)(2,1)} %param.11) | copy-start | bytes 98308
  44.3 91.7 %all-gather.5.cloned.1.call-start = ((), (), s32[]{:S(2)}) async-start(), calls=%async_computation.3 | async-start | bytes 2359296 | tf_op jit(solution)/shard_map/all_gather | solution.py:63
  53.8 41.0 %copy-start.2 = (bf16[128,128]{1,0:T(8,128)(2,1)S(1)}, bf16[128,128]{1,0:T(8,128)(2,1)}, u32[]{:S(2)}) copy-start(bf16[128,128]{1,0:T(8,128)(2,1)} %param.12) | copy-start | bytes 98308
  95.7 15.3 %copy-start.5 = (bf16[128,128]{1,0:T(8,128)(2,1)S(1)}, bf16[128,128]{1,0:T(8,128)(2,1)}, u32[]{:S(2)}) copy-start(bf16[128,128]{1,0:T(8,128)(2,1)} %param.14) | copy-start | bytes 98308
  107.6 27.5 %all-to-all-start.1 = ((bf16[128,16,128]{0,1,2:T(8,128)(2,1)}), bf16[128,16,128]{0,1,2:T(8,128)(2,1)S(1)}, u32[]{:S(2)}, u32[]{:S(2)}) async-start(bf16[128,16,128]{0,1,2:T(8,128)(2,1)} %copy.61), calls=%async_computation.1 | async-start | bytes 1048576 | tf_op jit(solution)/shard_map/all_to_all | solution.py:58
  143.4 3.7 %copy-start.3 = (bf16[128,128]{1,0:T(8,128)(2,1)S(1)}, bf16[128,128]{1,0:T(8,128)(2,1)}, u32[]{:S(2)}) copy-start(bf16[128,128]{1,0:T(8,128)(2,1)} %param.15) | copy-start | bytes 98308
Sparse Core Ops, SparseCore 0:
  44.4 46.6 all-gather.2
  97.4 37.8 all-gather.4
where the time goes:
time: 156 us; the launch traced here: 155 us
  waiting for transfers between devices  60.5 us (39%)
  blocking collectives  47.8 us (31%)
  between operations  13.6 us (9%)
  local copies, waits for them, and re-layouts  11.9 us (8%)
  matrix products  11.8 us (8%)
  other arithmetic  5.87 us (4%)
  starting transfers between devices  3.54 us (2%)
    all_gather x1, waiting for transfers between devices, local(): lax.all_gather(own_right, 'row', axis=2, tiled=True)  37.3 us
    all_to_all x1, waiting for transfers between devices, local(): lax.all_to_all(left_rows, 'row', split_axis=2, concat_axis=1, tiled=True)  23.2 us
    all_to_all x1, blocking collectives, local(): lax.all_to_all(right_rows, 'row', split_axis=2, concat_axis=1, tiled=True)  20.3 us
    all_gather x1, blocking collectives, local(): lax.all_gather(right_panel, 'col', axis=2, tiled=True)  10 us
    all_gather x1, blocking collectives, local(): left_rows = lax.all_gather(left_panel, 'col', axis=2, tiled=True)  9.15 us
    all_gather x1, blocking collectives, local(): lax.all_gather(left_panel, 'col', axis=2, tiled=True)  8.36 us
    all_gather x1, local copies, waits for them, and re-layouts, local(): lax.all_gather(right_panel, 'row', axis=1, tiled=True)  7.44 us
    all_to_all x1, starting transfers between devices, local(): lax.all_to_all(left_rows, 'row', split_axis=2, concat_axis=1, tiled=True)  3.49 us
  transfers between devices with their start and end apart: 3, of which 2 were waited for; matrix products, arithmetic and copies ran while one was open for 2% of the time, Pallas kernels for 0%

commit v1 on v0

v1 whole, which is shorter than its diff:
```python
import functools

import jax
import jax.numpy as jnp
from jax import lax
from jax.experimental import pallas as pl
from jax.experimental.pallas import tpu as pltpu
from jax.sharding import PartitionSpec as P

F32 = jnp.float32
BF16 = jnp.bfloat16
LANES = 128
EPS = 1e-05


def over_channels(values):
    centred = values - jnp.mean(values, axis=0, keepdims=True)
    variance = jnp.mean(centred * centred, axis=0, keepdims=True)
    return centred * lax.rsqrt(variance + EPS)


def from_left(weight, values):
    return lax.dot_general(weight, values, (((0,), (0,)), ((), ())), preferred_element_type=F32)


def live_tile(mask_ref, rows, cols):
    live = mask_ref[...].astype(F32)
    lane = lax.broadcasted_iota(jnp.int32, (rows, LANES), 1)
    sub = lax.broadcasted_iota(jnp.int32, (rows, LANES), 0)
    wide = jnp.broadcast_to(live, (rows, LANES))
    mine = lane == lax.axis_index("row") * rows + sub
    row_live = jnp.sum(jnp.where(mine, wide, 0.0), axis=1, keepdims=True)
    col_live = jnp.where(lane // cols == lax.axis_index("col"), wide, pltpu.roll(wide, cols, 1))
    return row_live * col_live


def panels(normed, proj_ref, mask_ref, msg_ref, tiles, rows, cols):
    side = 2 * lax.axis_index("col")
    first = jax.nn.sigmoid(from_left(proj_ref[side + 1], normed)) * from_left(proj_ref[side], normed)
    second = jax.nn.sigmoid(from_left(proj_ref[3 - side], normed)) * from_left(proj_ref[2 - side], normed)
    hidden = first.shape[0]
    low = lax.broadcasted_iota(jnp.int32, (hidden, LANES), 1) < cols
    for t in range(rows // 2):
        a = first[:, t * LANES : (t + 1) * LANES]
        b = second[:, t * LANES : (t + 1) * LANES]
        tiles[pl.ds(2 * t, hidden, stride=rows), :] = jnp.where(low, a, pltpu.roll(b, cols, 1))
        tiles[pl.ds(2 * t + 1, hidden, stride=rows), :] = jnp.where(low, pltpu.roll(a, cols, 1), b)
    live = live_tile(mask_ref, rows, cols)
    devices, per_device = msg_ref.shape[:2]
    half = per_device // 2
    for d in range(devices):
        for e in range(per_device):
            h = (e // half) * (hidden // 2) + d * half + e % half
            msg_ref[d, e] = (tiles[h * rows : (h + 1) * rows, :] * live).astype(BF16)


def projected(recv_ref, final_ref, tiles, rows, cols):
    values = recv_ref[...].reshape(-1, rows, LANES).astype(F32)
    half = values.shape[0]
    total = jnp.sum(values, axis=0)
    centred = values - ((total + pltpu.roll(total, cols, 1)) / (2 * half))[None]
    square = jnp.sum(centred * centred, axis=0)
    variance = (square + pltpu.roll(square, cols, 1)) / (2 * half)
    tiles[: half * rows, :] = (centred * lax.rsqrt(variance + EPS)[None]).reshape(half * rows, LANES)
    low = lax.broadcasted_iota(jnp.int32, (half, LANES), 1) < cols
    parts = []
    for t in range(rows // 2):
        a = tiles[pl.ds(2 * t, half, stride=rows), :]
        b = tiles[pl.ds(2 * t + 1, half, stride=rows), :]
        upper = jnp.where(low, a, pltpu.roll(b, cols, 1))
        lower = jnp.where(low, pltpu.roll(a, cols, 1), b)
        parts.append(jnp.concatenate([upper, lower], axis=0).astype(BF16))
    return from_left(final_ref[...], jnp.concatenate(parts, axis=1))


def first_kernel(rows, cols, mask_ref, pair_ref, proj_ref, gate_ref, msg_ref, pair_t_ref, gating_ref, tiles):
    pair = pair_ref[...].T
    pair_t_ref[...] = pair
    normed = over_channels(pair).astype(BF16)
    gating_ref[...] = jax.nn.sigmoid(from_left(gate_ref[...], normed))
    panels(normed, proj_ref, mask_ref, msg_ref, tiles, rows, cols)


def middle_kernel(
    rows, cols, mask_ref, recv_ref, pair_t_ref, gating_ref, final_ref, proj_ref, gate_ref, msg_ref, middle_ref, gating2_ref, tiles
):
    middle = pair_t_ref[...] + gating_ref[...] * projected(recv_ref, final_ref, tiles, rows, cols)
    middle_ref[...] = middle
    normed = over_channels(middle).astype(BF16)
    gating2_ref[...] = jax.nn.sigmoid(from_left(gate_ref[...], normed))
    panels(normed, proj_ref, mask_ref, msg_ref, tiles, rows, cols)


def last_kernel(rows, cols, recv_ref, middle_ref, gating_ref, final_ref, out_ref, tiles):
    out = middle_ref[...] + gating_ref[...] * projected(recv_ref, final_ref, tiles, rows, cols)
    out_ref[...] = out.T


def mix_kernel(incoming, cols, recv_ref, msg_ref):
    devices, per_device, rows, _ = recv_ref.shape
    blocks = devices // 2
    half = per_device // 2
    low = lax.broadcasted_iota(jnp.int32, (blocks * rows, LANES), 1) < cols

    def mixed(e):
        even = jnp.concatenate([recv_ref[2 * r, e] for r in range(blocks)], axis=0)
        odd = jnp.concatenate([recv_ref[2 * r + 1, e] for r in range(blocks)], axis=0)
        a = jnp.where(low, even, odd)
        b = jnp.where(low, odd, even)
        if incoming:
            x = lax.dot_general(a, b, (((0,), (0,)), ((), ())), preferred_element_type=F32)
            return pltpu.roll(x, cols, 1), x
        b = jnp.concatenate([b[:, cols:], b[:, :cols]], axis=1)
        x = lax.dot_general(a, b, (((1,), (1,)), ((), ())), preferred_element_type=F32)
        return x, pltpu.roll(x, cols, 1)

    for q in range(half):
        x, x_turned = mixed(q)
        y, y_turned = mixed(q + half)
        left = jnp.where(low, x, y_turned).astype(BF16)
        right = jnp.where(low, x_turned, y).astype(BF16)
        for r in range(blocks):
            msg_ref[2 * r, q] = left[r * rows : (r + 1) * rows]
            msg_ref[2 * r + 1, q] = right[r * rows : (r + 1) * rows]


def call(kernel, out_shape, scratch=()):
    vmem = pl.BlockSpec(memory_space=pltpu.VMEM)

    def run(*args):
        return pl.pallas_call(
            kernel,
            out_shape=out_shape,
            in_specs=[vmem] * len(args),
            out_specs=jax.tree.map(lambda _: vmem, out_shape),
            scratch_shapes=list(scratch),
            compiler_params=pltpu.CompilerParams(vmem_limit_bytes=40 * 1024 * 1024),
        )(*args)

    return run


def by_channel(devices, pair, residue_mask, out_proj, out_gate, out_final, in_proj, in_gate, in_final):
    rows, cols, channels = pair.shape
    hidden = out_proj.shape[2]
    positions = rows * cols
    per_device = hidden // devices
    shape = jax.ShapeDtypeStruct
    exchange = functools.partial(lax.all_to_all, axis_name=("row", "col"), split_axis=0, concat_axis=0, tiled=True)
    panel_msg = shape((devices, per_device, rows, LANES), BF16)
    mixed_msg = shape((devices, per_device // 2, rows, LANES), BF16)
    plane = shape((channels, positions), F32)
    tiles = pltpu.VMEM((hidden * rows, LANES), F32)
    mask = residue_mask.reshape(1, -1)

    msg, pair_t, gating = call(functools.partial(first_kernel, rows, cols), (panel_msg, plane, plane), [tiles])(
        mask, pair.reshape(positions, channels), jnp.swapaxes(out_proj, 0, 1), out_gate
    )
    mixed = call(functools.partial(mix_kernel, False, cols), mixed_msg)(exchange(msg))
    msg, middle, gating = call(functools.partial(middle_kernel, rows, cols), (panel_msg, plane, plane), [tiles])(
        mask, exchange(mixed), pair_t, gating, out_final, jnp.swapaxes(in_proj, 0, 1), in_gate
    )
    mixed = call(functools.partial(mix_kernel, True, cols), mixed_msg)(exchange(msg))
    out = call(functools.partial(last_kernel, rows, cols), shape((positions, channels), F32), [tiles])(
        exchange(mixed), middle, gating, in_final
    )
    return out.reshape(rows, cols, channels)


def normalize(values, axis):
    average = jnp.mean(values, axis=axis, keepdims=True)
    centred = values - average
    variance = jnp.mean(centred * centred, axis=axis, keepdims=True)
    return centred * lax.rsqrt(variance + EPS)


def gated_panels(pair, row_live, col_live, proj):
    normed = normalize(pair, 2).astype(BF16)
    linear = jnp.einsum("ijc,cph->phij", normed, proj, preferred_element_type=F32)
    pair_mask = row_live[:, None] * col_live[None, :]
    left_panel = (pair_mask * jax.nn.sigmoid(linear[1]) * linear[0]).astype(BF16)
    right_panel = (pair_mask * jax.nn.sigmoid(linear[3]) * linear[2]).astype(BF16)
    return (normed, left_panel, right_panel)


def update_pair(pair, normed, mixed, gate_w, final_w):
    all_channels = lax.all_gather(mixed, "sub", axis=0, tiled=True)
    scaled = normalize(all_channels, 0).astype(BF16)
    projected = jnp.einsum("hij,hc->ijc", scaled, final_w, preferred_element_type=F32)
    gating = jax.nn.sigmoid(jnp.einsum("ijc,cd->ijd", normed, gate_w, preferred_element_type=F32))
    return pair + gating * projected


def by_position(pair, residue_mask, out_proj, out_gate, out_final, in_proj, in_gate, in_final):
    row_count = pair.shape[0]
    col_count = pair.shape[1]
    row_start = lax.axis_index("row") * row_count
    col_start = lax.axis_index("col") * col_count
    live = residue_mask.astype(F32)
    row_live = lax.dynamic_slice_in_dim(live, row_start, row_count, 0)
    col_live = lax.dynamic_slice_in_dim(live, col_start, col_count, 0)
    normed, left_panel, right_panel = gated_panels(pair, row_live, col_live, out_proj)
    left_rows, right_rows = (
        lax.all_gather(left_panel, "col", axis=2, tiled=True),
        lax.all_gather(right_panel, "col", axis=2, tiled=True),
    )
    turned = lax.all_to_all(right_rows, "row", split_axis=2, concat_axis=1, tiled=True)
    own_right = lax.dynamic_slice_in_dim(turned, col_start, col_count, 1)
    mixed = jnp.einsum(
        "hik,hjk->hij",
        left_rows,
        lax.all_gather(own_right, "row", axis=2, tiled=True),
        preferred_element_type=F32,
    )
    middle = update_pair(pair, normed, mixed, out_gate, out_final)
    normed, left_panel, right_panel = gated_panels(middle, row_live, col_live, in_proj)
    left_rows = lax.all_gather(left_panel, "col", axis=2, tiled=True)
    turned_left = lax.all_to_all(left_rows, "row", split_axis=2, concat_axis=1, tiled=True)
    mixed_in = jnp.einsum(
        "hki,hkj->hij",
        turned_left,
        lax.all_gather(right_panel, "row", axis=1, tiled=True),
        preferred_element_type=F32,
    )
    return update_pair(middle, normed, mixed_in, in_gate, in_final)


def local(axes, pair, residue_mask, out_proj, *rest):
    rows, cols, channels = pair.shape
    hidden = out_proj.shape[2]
    devices = axes["row"] * axes["col"]
    fits = (
        axes["sub"] == 1
        and axes["col"] == 2
        and residue_mask.shape[0] == LANES
        and cols * 2 == LANES
        and rows % 16 == 0
        and channels == LANES
        and hidden % (2 * devices) == 0
        and hidden % 16 == 0
    )
    plan = functools.partial(by_channel, devices) if fits else by_position
    return plan(pair, residue_mask, out_proj, *rest)


def solution(mesh):
    return jax.shard_map(
        functools.partial(local, dict(mesh.shape)),
        mesh=mesh,
        in_specs=(
            P(("groups", "row"), "col", None),
            P("groups"),
            P(None, None, "sub"),
            P(),
            P(),
            P(None, None, "sub"),
            P(),
            P(),
        ),
        out_specs=P(("groups", "row"), "col", None),
        check_vma=False,
    )
```

time: 156 us -> 76.3 us (0.49)
  waiting for transfers between devices: 60.5 us -> 9.9 us
  between operations: 13.6 us -> 0.1 us
  matrix products: 11.8 us -> 0 us
  local copies, waits for them, and re-layouts: 11.9 us -> 2.66 us
  other arithmetic: 5.87 us -> 0 us
  Pallas kernels: 0 us -> 5.84 us
  blocking collectives: 47.8 us -> 53.2 us
    all_gather x2 -> x0, waiting for transfers between devices: 37.3 us -> none  [the longest x1 37.3 us: local(): lax.all_gather(own_right, 'row', axis=2, tiled=True)]
    all_to_all x1 -> x3, blocking collectives: 20.3 us -> 53.2 us  [the longest x2 39.3 us: by_channel(): exchange(msg)]
    all_gather x3 -> x0, blocking collectives: 27.6 us -> none  [the longest x1 10 us: local(): lax.all_gather(right_panel, 'col', axis=2, tiled=True)]
    all_to_all x1, waiting for transfers between devices: 23.2 us -> 9.9 us  [by_channel(): exchange(mixed)]
    dot_general x8 -> x0, matrix products: 11.8 us -> none  [the longest x1 3.39 us: local(): jnp.einsum('hki,hkj->hij', matching, lax.all_gather(right_panel, 'row', a...]
    all_gather x4 -> x0, local copies, waits for them, and re-layouts: 9.35 us -> none  [the longest x1 7.44 us: local(): lax.all_gather(right_panel, 'row', axis=1, tiled=True)]
    pallas_call x0 -> x5, Pallas kernels: none -> 5.84 us  [run(): pl.pallas_call(kernel, out_shape=out_shape, in_specs=[vmem] * len(args),...]
    reduce_sum x5 -> x0, other arithmetic: 3.47 us -> none  [the longest x4 2.22 us: normalize(): variance = jnp.mean(centred * centred, axis=axis, keepdims=True)]
  transfers between devices with their start and end apart: 3 -> 1, of which waited for: 2 -> 1; matrix products, arithmetic and copies ran while one was open for 2% -> 0% of each run, Pallas kernels for 0% -> 0%
where the time goes in v1:
time: 76.3 us; the launch traced here: 75.9 us
  blocking collectives  53.2 us (70%)
  waiting for transfers between devices  9.9 us (13%)
  Pallas kernels  5.84 us (8%)
  starting transfers between devices  4.23 us (6%)
  local copies, waits for them, and re-layouts  2.66 us (3%)
    all_to_all x2, blocking collectives, by_channel(): exchange(msg)  39.3 us
    all_to_all x1, blocking collectives, by_channel(): exchange(mixed)  13.9 us
    all_to_all x1, waiting for transfers between devices, by_channel(): exchange(mixed)  9.9 us
    pallas_call x5, Pallas kernels, run(): pl.pallas_call(kernel, out_shape=out_shape, in_specs=[vmem] * len(args),...  5.84 us
    all_to_all x1, starting transfers between devices, by_channel(): exchange(mixed)  4.23 us
    unnamed x16, local copies, waits for them, and re-layouts  2.66 us
  transfers between devices with their start and end apart: 1, of which 1 were waited for; matrix products, arithmetic and copies ran while one was open for 0% of the time, Pallas kernels for 0%

profile of v1, /device:TPU:0, one launch (start us, length us, event | category | flops | bytes accessed | tf_op | source)
XLA Modules:
  0.0 75.9 jit_solution(4823324147316674022)
XLA Ops:
  0.0 0.0 copy-start.2
  0.0 0.9 %copy.14 = bf16[128,4,128]{2,0,1:T(8,128)(2,1)S(1)} copy(bf16[128,4,128]{2,1,0:T(4,128)(2,1)} %param.10) | data formatting | bytes 262144 | tf_op args[2]
  0.9 0.0 copy-start.5
  0.9 0.0 copy-done.2
  1.0 0.6 copy-done.5
  1.6 0.0 copy-start
  1.6 1.0 %copy-done = f32[16,64,128]{2,1,0:T(8,128)S(1)} copy-done((f32[16,64,128]{2,1,0:T(8,128)S(1)}, f32[16,64,128]{2,1,0:T(8,128)}, u32[]{:S(2)}) %copy-start) | copy-done | bytes 524312
  2.6 1.1 %shard_map.82 = (bf16[16,8,16,128]{3,2,1,0:T(8,128)(2,1)S(1)}, f32[128,1024]{1,0:T(8,128)S(1)}, f32[128,1024]{1,0:T(8,128)S(1)}) custom-call(s32[1,128]{1,0:T(1,128)S(1)} %bitcast.12, f32[1024,128]{1,0:T(8,128)S(1)} %bitcast.9, bf16[4,128,128]{2,1,0:T(8,128)(2,1)S(1)} %bitcast.10, bf16[128,128]{1,0:T(8,128)(2,1)S(1)} %copy-done.2), custom_call_target="tpu_custom_call" | custom-call | tf_op jit(solution)/shard_map/pallas_call | solution.py:131
  3.8 21.7 %all_to_all.20.recv_ref = bf16[16,8,16,128]{3,2,1,0:T(8,128)(2,1)S(1)} all-to-all(bf16[16,8,16,128]{3,2,1,0:T(8,128)(2,1)S(1)} %get-tuple-element.11), channel_id=1, replica_groups=mesh['groups'=2,'row'=8,'col'=2,'sub'=1] {'row','col'}, dimensions={0} | all-to-all | bytes 1048576 | tf_op jit(solution)/shard_map/all_to_all | solution.py:159
  25.5 1.2 %shard_map.83 = bf16[16,4,16,128]{3,2,1,0:T(8,128)(2,1)} custom-call(bf16[16,8,16,128]{3,2,1,0:T(8,128)(2,1)S(1)} %all_to_all.20.recv_ref), custom_call_target="tpu_custom_call" | custom-call | tf_op jit(solution)/shard_map/pallas_call | solution.py:131
  26.6 4.2 %all-to-all-start.1 = ((bf16[16,4,16,128]{3,2,1,0:T(8,128)(2,1)}), bf16[16,4,16,128]{3,2,1,0:T(8,128)(2,1)S(1)}, u32[]{:S(2)}, u32[]{:S(2)}) async-start(bf16[16,4,16,128]{3,2,1,0:T(8,128)(2,1)} %shard_map.83), calls=%async_computation.1 | async-start | bytes 524288 | tf_op jit(solution)/shard_map/all_to_all | solution.py:161
  30.9 0.0 copy-done.6
  30.9 0.0 copy-start.3
  30.9 0.0 copy-start.4
  30.9 9.9 %all-to-all-done.1.recv_ref = bf16[16,4,16,128]{3,2,1,0:T(8,128)(2,1)S(1)} async-done(((bf16[16,4,16,128]{3,2,1,0:T(8,128)(2,1)}), bf16[16,4,16,128]{3,2,1,0:T(8,128)(2,1)S(1)}, u32[]{:S(2)}, u32[]{:S(2)}) %all-to-all-start.1) | async-done | bytes 262176 | tf_op jit(solution)/shard_map/all_to_all | solution.py:161
  40.8 0.0 copy-done.3
  40.8 0.0 copy-done.4
  40.8 1.6 %shard_map.84 = (bf16[16,8,16,128]{3,2,1,0:T(8,128)(2,1)S(1)}, f32[128,1024]{1,0:T(8,128)S(1)}, f32[128,1024]{1,0:T(8,128)S(1)}) custom-call(s32[1,128]{1,0:T(1,128)S(1)} %bitcast.13, bf16[16,4,16,128]{3,2,1,0:T(8,128)(2,1)S(1)} %all-to-all-done.1.recv_ref, f32[128,1024]{1,0:T(8,128)S(1)} %get-tuple-element.12.pair_t_ref, ...), custom_call_target="tpu_custom_call" | custom-call | tf_op jit(solution)/shard_map/pallas_call | solution.py:131
  42.4 17.6 %all_to_all.21.recv_ref = bf16[16,8,16,128]{3,2,1,0:T(8,128)(2,1)S(1)} all-to-all(bf16[16,8,16,128]{3,2,1,0:T(8,128)(2,1)S(1)} %get-tuple-element.14), channel_id=1, replica_groups=mesh['groups'=2,'row'=8,'col'=2,'sub'=1] {'row','col'}, dimensions={0} | all-to-all | bytes 1048576 | tf_op jit(solution)/shard_map/all_to_all | solution.py:163
  60.0 0.4 shard_map.85
  60.4 0.0 copy-start.1
  60.4 13.9 %all_to_all.22.recv_ref = bf16[16,4,16,128]{3,2,1,0:T(8,128)(2,1)S(1)} all-to-all(bf16[16,4,16,128]{3,2,1,0:T(8,128)(2,1)S(1)} %shard_map.85), channel_id=1, replica_groups=mesh['groups'=2,'row'=8,'col'=2,'sub'=1] {'row','col'}, dimensions={0} | all-to-all | bytes 524288 | tf_op jit(solution)/shard_map/all_to_all | solution.py:165
  74.3 0.0 copy-done.1
  74.3 1.6 %shard_map.86 = f32[1024,128]{1,0:T(8,128)} custom-call(bf16[16,4,16,128]{3,2,1,0:T(8,128)(2,1)S(1)} %all_to_all.22.recv_ref, f32[128,1024]{1,0:T(8,128)S(1)} %get-tuple-element.15.middle_ref, f32[128,1024]{1,0:T(8,128)S(1)} %get-tuple-element.16.gating_ref, bf16[128,128]{1,0:T(8,128)(2,1)S(1)} %copy-done.1), custom_call_target="tpu_custom_call" | custom-call | tf_op jit(solution)/shard_map/pallas_call | solution.py:131
  (2 shorter events, 0.0 us)
Async XLA Ops:
  0.0 0.9 %copy-start.2 = (bf16[128,128]{1,0:T(8,128)(2,1)S(1)}, bf16[128,128]{1,0:T(8,128)(2,1)}, u32[]{:S(2)}) copy-start(bf16[128,128]{1,0:T(8,128)(2,1)} %gate_ref.2) | copy-start | bytes 98308
  0.9 0.7 copy-start.5
  1.6 1.0 %copy-start = (f32[16,64,128]{2,1,0:T(8,128)S(1)}, f32[16,64,128]{2,1,0:T(8,128)}, u32[]{:S(2)}) copy-start(f32[16,64,128]{2,1,0:T(8,128)} %param.8) | copy-start | bytes 1572868
  26.6 4.2 %copy-start.6 = (bf16[128,4,128]{2,1,0:T(4,128)(2,1)S(1)}, bf16[128,4,128]{2,1,0:T(4,128)(2,1)}, u32[]{:S(2)}) copy-start(bf16[128,4,128]{2,1,0:T(4,128)(2,1)} %param.13) | copy-start | bytes 393220
  26.6 14.2 %all-to-all-start.1 = ((bf16[16,4,16,128]{3,2,1,0:T(8,128)(2,1)}), bf16[16,4,16,128]{3,2,1,0:T(8,128)(2,1)S(1)}, u32[]{:S(2)}, u32[]{:S(2)}) async-start(bf16[16,4,16,128]{3,2,1,0:T(8,128)(2,1)} %shard_map.83), calls=%async_computation.1 | async-start | bytes 524288 | tf_op jit(solution)/shard_map/all_to_all | solution.py:161
  30.9 10.0 %copy-start.3 = (bf16[128,128]{1,0:T(8,128)(2,1)S(1)}, bf16[128,128]{1,0:T(8,128)(2,1)}, u32[]{:S(2)}) copy-start(bf16[128,128]{1,0:T(8,128)(2,1)} %final_ref.2) | copy-start | bytes 98308
  30.9 9.9 %copy-start.4 = (bf16[128,128]{1,0:T(8,128)(2,1)S(1)}, bf16[128,128]{1,0:T(8,128)(2,1)}, u32[]{:S(2)}) copy-start(bf16[128,128]{1,0:T(8,128)(2,1)} %gate_ref.3) | copy-start | bytes 98308
  60.4 13.9 %copy-start.1 = (bf16[128,128]{1,0:T(8,128)(2,1)S(1)}, bf16[128,128]{1,0:T(8,128)(2,1)}, u32[]{:S(2)}) copy-start(bf16[128,128]{1,0:T(8,128)(2,1)} %final_ref.3) | copy-start | bytes 98308

commit v2 on v1

--- a/solution.py
+++ b/solution.py
@@ -10,6 +10,7 @@
 F32 = jnp.float32
 BF16 = jnp.bfloat16
 LANES = 128
+CHUNK = 256
 EPS = 1e-05
 
 
@@ -19,8 +20,17 @@
     return centred * lax.rsqrt(variance + EPS)
 
 
-def from_left(weight, values):
+def product(weight, values):
     return lax.dot_general(weight, values, (((0,), (0,)), ((), ())), preferred_element_type=F32)
+
+
+def side_by_side(proj_ref, gate_ref, wide, weights):
+    channels, hidden = gate_ref.shape
+    wide[...] = proj_ref[...].astype(F32)
+    side = 2 * lax.axis_index("col")
+    for n, p in enumerate((side, side + 1, 2 - side, 3 - side)):
+        weights[:, n * hidden : (n + 1) * hidden] = wide[pl.ds(p, channels, stride=4), :].astype(BF16)
+    weights[:, 4 * hidden :] = gate_ref[...]
 
 
 def live_tile(mask_ref, rows, cols):
@@ -34,24 +44,26 @@
     return row_live * col_live
 
 
-def panels(normed, proj_ref, mask_ref, msg_ref, tiles, rows, cols):
-    side = 2 * lax.axis_index("col")
-    first = jax.nn.sigmoid(from_left(proj_ref[side + 1], normed)) * from_left(proj_ref[side], normed)
-    second = jax.nn.sigmoid(from_left(proj_ref[3 - side], normed)) * from_left(proj_ref[2 - side], normed)
-    hidden = first.shape[0]
+def panels(normed, weights, live, msg_ref, gating_ref, rows, cols):
+    linear = product(weights[...], normed)
+    hidden = linear.shape[0] // 5
+    gating_ref[...] = jax.nn.sigmoid(linear[4 * hidden :])
+    first = jax.nn.sigmoid(linear[hidden : 2 * hidden]) * linear[:hidden]
+    second = jax.nn.sigmoid(linear[3 * hidden : 4 * hidden]) * linear[2 * hidden : 3 * hidden]
     low = lax.broadcasted_iota(jnp.int32, (hidden, LANES), 1) < cols
+    by_row = []
     for t in range(rows // 2):
         a = first[:, t * LANES : (t + 1) * LANES]
         b = second[:, t * LANES : (t + 1) * LANES]
-        tiles[pl.ds(2 * t, hidden, stride=rows), :] = jnp.where(low, a, pltpu.roll(b, cols, 1))
-        tiles[pl.ds(2 * t + 1, hidden, stride=rows), :] = jnp.where(low, pltpu.roll(a, cols, 1), b)
-    live = live_tile(mask_ref, rows, cols)
+        for tile in (jnp.where(low, a, pltpu.roll(b, cols, 1)), jnp.where(low, pltpu.roll(a, cols, 1), b)):
+            row = len(by_row)
+            by_row.append((tile * live[row : row + 1]).astype(BF16))
+    by_hidden = jnp.swapaxes(jnp.stack(by_row, axis=0), 0, 1)
     devices, per_device = msg_ref.shape[:2]
     half = per_device // 2
     for d in range(devices):
-        for e in range(per_device):
-            h = (e // half) * (hidden // 2) + d * half + e % half
-            msg_ref[d, e] = (tiles[h * rows : (h + 1) * rows, :] * live).astype(BF16)
+        msg_ref[d, :half] = by_hidden[d * half : (d + 1) * half]
+        msg_ref[d, half:] = by_hidden[hidden // 2 + d * half : hidden // 2 + (d + 1) * half]
 
 
 def projected(recv_ref, final_ref, tiles, rows, cols):
@@ -70,30 +82,54 @@
         upper = jnp.where(low, a, pltpu.roll(b, cols, 1))
         lower = jnp.where(low, pltpu.roll(a, cols, 1), b)
         parts.append(jnp.concatenate([upper, lower], axis=0).astype(BF16))
-    return from_left(final_ref[...], jnp.concatenate(parts, axis=1))
-
-
-def first_kernel(rows, cols, mask_ref, pair_ref, proj_ref, gate_ref, msg_ref, pair_t_ref, gating_ref, tiles):
+    return product(final_ref[...], jnp.concatenate(parts, axis=1))
+
+
+def copies(pairs, done):
+    started = [pltpu.make_async_copy(source, target, done.at[n]) for n, (source, target) in enumerate(pairs)]
+    for copy in started:
+        copy.start()
+    return started
+
+
+def first_kernel(
+    rows, cols, pair_hbm, mask_hbm, proj_hbm, gate_hbm, proj2_hbm, gate2_hbm, msg_ref, pair_t_ref, gating_ref, live_ref, weights2,
+    pair_ref, mask_ref, proj_ref, gate_ref, proj2_ref, gate2_ref, weights, wide, done,
+):
+    whole = ((mask_hbm, mask_ref), (proj_hbm, proj_ref), (gate_hbm, gate_ref), (proj2_hbm, proj2_ref), (gate2_hbm, gate2_ref))
+    chunks = [slice(at, at + CHUNK) for at in range(0, rows * cols, CHUNK)]
+    coming = copies([(pair_hbm.at[at], pair_ref.at[at]) for at in chunks] + list(whole), done)
+    for copy in coming[len(chunks) :]:
+        copy.wait()
+    side_by_side(proj_ref, gate_ref, wide, weights)
+    side_by_side(proj2_ref, gate2_ref, wide, weights2)
+    for copy in coming[: len(chunks)]:
+        copy.wait()
     pair = pair_ref[...].T
     pair_t_ref[...] = pair
-    normed = over_channels(pair).astype(BF16)
-    gating_ref[...] = jax.nn.sigmoid(from_left(gate_ref[...], normed))
-    panels(normed, proj_ref, mask_ref, msg_ref, tiles, rows, cols)
+    live = live_tile(mask_ref, rows, cols)
+    live_ref[...] = live
+    panels(over_channels(pair).astype(BF16), weights, live, msg_ref, gating_ref, rows, cols)
 
 
 def middle_kernel(
-    rows, cols, mask_ref, recv_ref, pair_t_ref, gating_ref, final_ref, proj_ref, gate_ref, msg_ref, middle_ref, gating2_ref, tiles
+    rows, cols, live_ref, weights, final_ref, recv_ref, pair_t_ref, gating_ref, msg_ref, middle_ref, gating2_ref, tiles
 ):
     middle = pair_t_ref[...] + gating_ref[...] * projected(recv_ref, final_ref, tiles, rows, cols)
     middle_ref[...] = middle
-    normed = over_channels(middle).astype(BF16)
-    gating2_ref[...] = jax.nn.sigmoid(from_left(gate_ref[...], normed))
-    panels(normed, proj_ref, mask_ref, msg_ref, tiles, rows, cols)
-
-
-def last_kernel(rows, cols, recv_ref, middle_ref, gating_ref, final_ref, out_ref, tiles):
-    out = middle_ref[...] + gating_ref[...] * projected(recv_ref, final_ref, tiles, rows, cols)
-    out_ref[...] = out.T
+    panels(over_channels(middle).astype(BF16), weights, live_ref[...], msg_ref, gating2_ref, rows, cols)
+
+
+def last_kernel(rows, cols, recv_ref, middle_ref, gating_ref, final_ref, out_hbm, tiles, out_ref, done):
+    change = projected(recv_ref, final_ref, tiles, rows, cols)
+    leaving = []
+    for n in range(rows * cols // CHUNK):
+        at = slice(n * CHUNK, (n + 1) * CHUNK)
+        out_ref[at, :] = (middle_ref[:, at] + gating_ref[:, at] * change[:, at]).T
+        leaving.append(pltpu.make_async_copy(out_ref.at[at], out_hbm.at[at], done.at[n]))
+        leaving[-1].start()
+    for copy in leaving:
+        copy.wait()
 
 
 def mix_kernel(incoming, cols, recv_ref, msg_ref):
@@ -110,7 +146,7 @@
         if incoming:
             x = lax.dot_general(a, b, (((0,), (0,)), ((), ())), preferred_element_type=F32)
             return pltpu.roll(x, cols, 1), x
-        b = jnp.concatenate([b[:, cols:], b[:, :cols]], axis=1)
+        b = pltpu.roll(b.astype(F32), cols, 1).astype(BF16)
         x = lax.dot_general(a, b, (((1,), (1,)), ((), ())), preferred_element_type=F32)
         return x, pltpu.roll(x, cols, 1)
 
@@ -124,15 +160,18 @@
             msg_ref[2 * r + 1, q] = right[r * rows : (r + 1) * rows]
 
 
-def call(kernel, out_shape, scratch=()):
+def call(kernel, out_shape, scratch=(), far=(0, False)):
     vmem = pl.BlockSpec(memory_space=pltpu.VMEM)
+    hbm = pl.BlockSpec(memory_space=pltpu.HBM)
+    far_args, far_outs = far
 
     def run(*args):
+        args = [pltpu.with_memory_space_constraint(a, pltpu.HBM) for a in args[:far_args]] + list(args[far_args:])
         return pl.pallas_call(
             kernel,
             out_shape=out_shape,
-            in_specs=[vmem] * len(args),
-            out_specs=jax.tree.map(lambda _: vmem, out_shape),
+            in_specs=[hbm] * far_args + [vmem] * (len(args) - far_args),
+            out_specs=jax.tree.map(lambda _: hbm if far_outs else vmem, out_shape),
             scratch_shapes=list(scratch),
             compiler_params=pltpu.CompilerParams(vmem_limit_bytes=40 * 1024 * 1024),
         )(*args)
@@ -150,18 +189,24 @@
     panel_msg = shape((devices, per_device, rows, LANES), BF16)
     mixed_msg = shape((devices, per_device // 2, rows, LANES), BF16)
     plane = shape((channels, positions), F32)
-    tiles = pltpu.VMEM((hidden * rows, LANES), F32)
     mask = residue_mask.reshape(1, -1)
-
-    msg, pair_t, gating = call(functools.partial(first_kernel, rows, cols), (panel_msg, plane, plane), [tiles])(
-        mask, pair.reshape(positions, channels), jnp.swapaxes(out_proj, 0, 1), out_gate
-    )
+    by_position = pltpu.VMEM((positions, channels), F32)
+    tiles = pltpu.VMEM((positions, LANES), F32)
+    weights = (channels, 5 * hidden)
+    chunks = positions // CHUNK
+
+    far = (pair.reshape(positions, channels), mask, out_proj.reshape(-1, hidden), out_gate, in_proj.reshape(-1, hidden), in_gate)
+    near = [pltpu.VMEM(a.shape, a.dtype) for a in far] + [pltpu.VMEM(weights, BF16), pltpu.VMEM((4 * channels, hidden), F32), pltpu.SemaphoreType.DMA((chunks + 5,))]
+    outs = (panel_msg, plane, plane, shape((rows, LANES), F32), shape(weights, BF16))
+    msg, pair_t, gating, live, weights = call(functools.partial(first_kernel, rows, cols), outs, near, (6, False))(*far)
     mixed = call(functools.partial(mix_kernel, False, cols), mixed_msg)(exchange(msg))
-    msg, middle, gating = call(functools.partial(middle_kernel, rows, cols), (panel_msg, plane, plane), [tiles])(
-        mask, exchange(mixed), pair_t, gating, out_final, jnp.swapaxes(in_proj, 0, 1), in_gate
+    outs = (panel_msg, plane, plane)
+    msg, middle, gating = call(functools.partial(middle_kernel, rows, cols), outs, [tiles])(
+        live, weights, out_final, exchange(mixed), pair_t, gating
     )
     mixed = call(functools.partial(mix_kernel, True, cols), mixed_msg)(exchange(msg))
-    out = call(functools.partial(last_kernel, rows, cols), shape((positions, channels), F32), [tiles])(
+    near = [tiles, by_position, pltpu.SemaphoreType.DMA((chunks,))]
+    out = call(functools.partial(last_kernel, rows, cols), shape((positions, channels), F32), near, (0, True))(
         exchange(mixed), middle, gating, in_final
     )
     return out.reshape(rows, cols, channels)
@@ -235,7 +280,9 @@
         and residue_mask.shape[0] == LANES
         and cols * 2 == LANES
         and rows % 16 == 0
+        and rows * cols % CHUNK == 0
         and channels == LANES
+        and hidden == channels
         and hidden % (2 * devices) == 0
         and hidden % 16 == 0
     )

time: 76.3 us -> 73.5 us (0.963)
  blocking collectives: 53.2 us -> 67 us
  waiting for transfers between devices: 9.9 us -> 0 us
  starting transfers between devices: 4.23 us -> 0 us
  local copies, waits for them, and re-layouts: 2.66 us -> 0.01 us
    all_to_all x1 -> x2, blocking collectives: 13.9 us -> 27.7 us  [by_channel(): exchange(mixed)]
    all_to_all x1 -> x0, waiting for transfers between devices: 9.9 us -> none  [by_channel(): exchange(mixed)]
    all_to_all x1 -> x0, starting transfers between devices: 4.23 us -> none  [by_channel(): exchange(mixed)]
    unnamed x16 -> x4, local copies, waits for them, and re-layouts: 2.66 us -> 0.01 us
  transfers between devices with their start and end apart: 1 -> 0, of which waited for: 1 -> 0; matrix products, arithmetic and copies ran while one was open for 0% -> 0% of each run, Pallas kernels for 0% -> 0%
where the time goes in v2:
time: 73.5 us; the launch traced here: 73.1 us
  blocking collectives  67 us (91%)
  Pallas kernels  6.01 us (8%)
    all_to_all x2, blocking collectives, by_channel(): exchange(msg)  39.3 us
    all_to_all x2, blocking collectives, by_channel(): exchange(mixed)  27.7 us
    pallas_call x5, Pallas kernels, run(): pl.pallas_call(kernel, out_shape=out_shape, in_specs=[hbm] * far_args + [...  6.01 us

profile of v2, /device:TPU:0, one launch (start us, length us, event | category | flops | bytes accessed | tf_op | source)
XLA Modules:
  0.0 73.1 jit_solution(959260287290455606)
XLA Ops:
  0.0 2.3 %shard_map.82 = (bf16[16,8,16,128]{3,2,1,0:T(8,128)(2,1)S(1)}, f32[128,1024]{1,0:T(8,128)S(1)}, f32[128,1024]{1,0:T(8,128)S(1)}, f32[16,128]{1,0:T(8,128)S(1)}, bf16[128,640]{1,0:T(8,128)(2,1)S(1)}) custom-call(f32[1024,128]{1,0:T(8,128)} %bitcast.5, s32[1,128]{1,0:T(1,128)} %bitcast.8, bf16[512,128]{1,0:T(8,128)(2,1)} %bitcast.6, ...), custom_call_target="tpu_custom_call" | custom-call | tf_op jit(solution)/shard_map/pallas_call | solution.py:170
  2.3 21.7 %all_to_all.20.recv_ref = bf16[16,8,16,128]{3,2,1,0:T(8,128)(2,1)S(1)} all-to-all(bf16[16,8,16,128]{3,2,1,0:T(8,128)(2,1)S(1)} %get-tuple-element.15), channel_id=1, replica_groups=mesh['groups'=2,'row'=8,'col'=2,'sub'=1] {'row','col'}, dimensions={0} | all-to-all | bytes 1048576 | tf_op jit(solution)/shard_map/all_to_all | solution.py:202
  24.0 0.4 shard_map.83
  24.5 0.0 copy-start.1
  24.5 13.9 %all_to_all.21.recv_ref = bf16[16,4,16,128]{3,2,1,0:T(8,128)(2,1)S(1)} all-to-all(bf16[16,4,16,128]{3,2,1,0:T(8,128)(2,1)S(1)} %shard_map.83), channel_id=1, replica_groups=mesh['groups'=2,'row'=8,'col'=2,'sub'=1] {'row','col'}, dimensions={0} | all-to-all | bytes 524288 | tf_op jit(solution)/shard_map/all_to_all | solution.py:205
  38.3 0.0 copy-done.1
  38.3 1.4 %shard_map.84 = (bf16[16,8,16,128]{3,2,1,0:T(8,128)(2,1)S(1)}, f32[128,1024]{1,0:T(8,128)S(1)}, f32[128,1024]{1,0:T(8,128)S(1)}) custom-call(f32[16,128]{1,0:T(8,128)S(1)} %get-tuple-element.13.live_ref, bf16[128,640]{1,0:T(8,128)(2,1)S(1)} %get-tuple-element.14.weights, bf16[128,128]{1,0:T(8,128)(2,1)S(1)} %copy-done.1, ...), custom_call_target="tpu_custom_call" | custom-call | tf_op jit(solution)/shard_map/pallas_call | solution.py:170
  39.7 17.6 %all_to_all.22.recv_ref = bf16[16,8,16,128]{3,2,1,0:T(8,128)(2,1)S(1)} all-to-all(bf16[16,8,16,128]{3,2,1,0:T(8,128)(2,1)S(1)} %get-tuple-element.18), channel_id=1, replica_groups=mesh['groups'=2,'row'=8,'col'=2,'sub'=1] {'row','col'}, dimensions={0} | all-to-all | bytes 1048576 | tf_op jit(solution)/shard_map/all_to_all | solution.py:207
  57.3 0.4 shard_map.85
  57.7 0.0 copy-start
  57.7 13.9 %all_to_all.23.recv_ref = bf16[16,4,16,128]{3,2,1,0:T(8,128)(2,1)S(1)} all-to-all(bf16[16,4,16,128]{3,2,1,0:T(8,128)(2,1)S(1)} %shard_map.85), channel_id=1, replica_groups=mesh['groups'=2,'row'=8,'col'=2,'sub'=1] {'row','col'}, dimensions={0} | all-to-all | bytes 524288 | tf_op jit(solution)/shard_map/all_to_all | solution.py:210
  71.6 0.0 copy-done
  71.6 1.5 %shard_map.86 = f32[1024,128]{1,0:T(8,128)} custom-call(bf16[16,4,16,128]{3,2,1,0:T(8,128)(2,1)S(1)} %all_to_all.23.recv_ref, f32[128,1024]{1,0:T(8,128)S(1)} %get-tuple-element.19.middle_ref, f32[128,1024]{1,0:T(8,128)S(1)} %get-tuple-element.20.gating_ref, bf16[128,128]{1,0:T(8,128)(2,1)S(1)} %copy-done), custom_call_target="tpu_custom_call" | custom-call | tf_op jit(solution)/shard_map/pallas_call | solution.py:170
Async XLA Ops:
  24.5 13.9 %copy-start.1 = (bf16[128,128]{1,0:T(8,128)(2,1)S(1)}, bf16[128,128]{1,0:T(8,128)(2,1)}, u32[]{:S(2)}) copy-start(bf16[128,128]{1,0:T(8,128)(2,1)} %final_ref.2) | copy-start | bytes 98308
  57.7 13.9 %copy-start = (bf16[128,128]{1,0:T(8,128)(2,1)S(1)}, bf16[128,128]{1,0:T(8,128)(2,1)}, u32[]{:S(2)}) copy-start(bf16[128,128]{1,0:T(8,128)(2,1)} %final_ref.3) | copy-start | bytes 98308

commit v3 on v2

--- a/solution.py
+++ b/solution.py
@@ -67,8 +67,8 @@
 
 
 def projected(recv_ref, final_ref, tiles, rows, cols):
-    values = recv_ref[...].reshape(-1, rows, LANES).astype(F32)
-    half = values.shape[0]
+    half = final_ref.shape[0] // 2
+    values = jnp.sum(recv_ref[...].reshape(-1, half, rows, LANES).astype(F32), axis=0)
     total = jnp.sum(values, axis=0)
     centred = values - ((total + pltpu.roll(total, cols, 1)) / (2 * half))[None]
     square = jnp.sum(centred * centred, axis=0)
@@ -133,16 +133,17 @@
 
 
 def mix_kernel(incoming, cols, recv_ref, msg_ref):
-    devices, per_device, rows, _ = recv_ref.shape
-    blocks = devices // 2
+    sources, per_device, rows, _ = recv_ref.shape
     half = per_device // 2
-    low = lax.broadcasted_iota(jnp.int32, (blocks * rows, LANES), 1) < cols
+
+    def low(x):
+        return lax.broadcasted_iota(jnp.int32, x.shape, 1) < cols
 
     def mixed(e):
-        even = jnp.concatenate([recv_ref[2 * r, e] for r in range(blocks)], axis=0)
-        odd = jnp.concatenate([recv_ref[2 * r + 1, e] for r in range(blocks)], axis=0)
-        a = jnp.where(low, even, odd)
-        b = jnp.where(low, odd, even)
+        even = jnp.concatenate([recv_ref[r, e] for r in range(0, sources, 2)], axis=0)
+        odd = jnp.concatenate([recv_ref[r, e] for r in range(1, sources, 2)], axis=0)
+        a = jnp.where(low(even), even, odd)
+        b = jnp.where(low(even), odd, even)
         if incoming:
             x = lax.dot_general(a, b, (((0,), (0,)), ((), ())), preferred_element_type=F32)
             return pltpu.roll(x, cols, 1), x
@@ -153,9 +154,9 @@
     for q in range(half):
         x, x_turned = mixed(q)
         y, y_turned = mixed(q + half)
-        left = jnp.where(low, x, y_turned).astype(BF16)
-        right = jnp.where(low, x_turned, y).astype(BF16)
-        for r in range(blocks):
+        left = jnp.where(low(x), x, y_turned).astype(BF16)
+        right = jnp.where(low(x), x_turned, y).astype(BF16)
+        for r in range(msg_ref.shape[0] // 2):
             msg_ref[2 * r, q] = left[r * rows : (r + 1) * rows]
             msg_ref[2 * r + 1, q] = right[r * rows : (r + 1) * rows]
 
@@ -183,11 +184,15 @@
     rows, cols, channels = pair.shape
     hidden = out_proj.shape[2]
     positions = rows * cols
-    per_device = hidden // devices
     shape = jax.ShapeDtypeStruct
+    near = devices // 2
+    halves = [list(range(near)), list(range(near, devices))]
     exchange = functools.partial(lax.all_to_all, axis_name=("row", "col"), split_axis=0, concat_axis=0, tiled=True)
-    panel_msg = shape((devices, per_device, rows, LANES), BF16)
-    mixed_msg = shape((devices, per_device // 2, rows, LANES), BF16)
+    exchange_near = functools.partial(exchange, axis_index_groups=halves)
+
+    def messages(targets, tiles):
+        return shape((targets, tiles, rows, LANES), BF16)
+
     plane = shape((channels, positions), F32)
     mask = residue_mask.reshape(1, -1)
     by_position = pltpu.VMEM((positions, channels), F32)
@@ -196,17 +201,17 @@
     chunks = positions // CHUNK
 
     far = (pair.reshape(positions, channels), mask, out_proj.reshape(-1, hidden), out_gate, in_proj.reshape(-1, hidden), in_gate)
-    near = [pltpu.VMEM(a.shape, a.dtype) for a in far] + [pltpu.VMEM(weights, BF16), pltpu.VMEM((4 * channels, hidden), F32), pltpu.SemaphoreType.DMA((chunks + 5,))]
-    outs = (panel_msg, plane, plane, shape((rows, LANES), F32), shape(weights, BF16))
-    msg, pair_t, gating, live, weights = call(functools.partial(first_kernel, rows, cols), outs, near, (6, False))(*far)
-    mixed = call(functools.partial(mix_kernel, False, cols), mixed_msg)(exchange(msg))
-    outs = (panel_msg, plane, plane)
+    scratch = [pltpu.VMEM(a.shape, a.dtype) for a in far] + [pltpu.VMEM(weights, BF16), pltpu.VMEM((4 * channels, hidden), F32), pltpu.SemaphoreType.DMA((chunks + 5,))]
+    outs = (messages(devices, hidden // devices), plane, plane, shape((rows, LANES), F32), shape(weights, BF16))
+    msg, pair_t, gating, live, weights = call(functools.partial(first_kernel, rows, cols), outs, scratch, (6, False))(*far)
+    mixed = call(functools.partial(mix_kernel, False, cols), messages(devices, hidden // devices // 2))(exchange(msg))
+    outs = (messages(near, hidden // near), plane, plane)
     msg, middle, gating = call(functools.partial(middle_kernel, rows, cols), outs, [tiles])(
         live, weights, out_final, exchange(mixed), pair_t, gating
     )
-    mixed = call(functools.partial(mix_kernel, True, cols), mixed_msg)(exchange(msg))
-    near = [tiles, by_position, pltpu.SemaphoreType.DMA((chunks,))]
-    out = call(functools.partial(last_kernel, rows, cols), shape((positions, channels), F32), near, (0, True))(
+    mixed = call(functools.partial(mix_kernel, True, cols), messages(devices, hidden // near // 2))(exchange_near(msg))
+    scratch = [tiles, by_position, pltpu.SemaphoreType.DMA((chunks,))]
+    out = call(functools.partial(last_kernel, rows, cols), shape((positions, channels), F32), scratch, (0, True))(
         exchange(mixed), middle, gating, in_final
     )
     return out.reshape(rows, cols, channels)
@@ -284,6 +289,7 @@
         and channels == LANES
         and hidden == channels
         and hidden % (2 * devices) == 0
+        and axes["row"] % 2 == 0
         and hidden % 16 == 0
     )
     plan = functools.partial(by_channel, devices) if fits else by_position

time: 73.5 us -> 71.2 us (0.969)
  blocking collectives: 67 us -> 64.6 us
    all_to_all x2 -> x1, blocking collectives: 39.3 us -> 21.7 us  [by_channel(): exchange(msg)]
    all_to_all x0 -> x1, blocking collectives: none -> 11.3 us  [by_channel(): exchange_near(msg)]
    all_to_all x2, blocking collectives: 27.7 us -> 31.6 us  [by_channel(): exchange(mixed)]
where the time goes in v3:
time: 71.2 us; the launch traced here: 70.7 us
  blocking collectives  64.6 us (91%)
  Pallas kernels  6.08 us (9%)
    all_to_all x2, blocking collectives, by_channel(): exchange(mixed)  31.6 us
    all_to_all x1, blocking collectives, by_channel(): exchange(msg)  21.7 us
    all_to_all x1, blocking collectives, by_channel(): exchange_near(msg)  11.3 us
    pallas_call x5, Pallas kernels, run(): pl.pallas_call(kernel, out_shape=out_shape, in_specs=[hbm] * far_args + [...  6.08 us

profile of v3, /device:TPU:0, one launch (start us, length us, event | category | flops | bytes accessed | tf_op | source)
XLA Modules:
  0.0 70.7 jit_solution(1388927552232016895)
XLA Ops:
  0.0 2.3 %shard_map.82 = (bf16[16,8,16,128]{3,2,1,0:T(8,128)(2,1)S(1)}, f32[128,1024]{1,0:T(8,128)S(1)}, f32[128,1024]{1,0:T(8,128)S(1)}, f32[16,128]{1,0:T(8,128)S(1)}, bf16[128,640]{1,0:T(8,128)(2,1)S(1)}) custom-call(f32[1024,128]{1,0:T(8,128)} %bitcast.5, s32[1,128]{1,0:T(1,128)} %bitcast.8, bf16[512,128]{1,0:T(8,128)(2,1)} %bitcast.6, ...), custom_call_target="tpu_custom_call" | custom-call | tf_op jit(solution)/shard_map/pallas_call | solution.py:171
  2.3 21.7 %all_to_all.20.recv_ref = bf16[16,8,16,128]{3,2,1,0:T(8,128)(2,1)S(1)} all-to-all(bf16[16,8,16,128]{3,2,1,0:T(8,128)(2,1)S(1)} %get-tuple-element.15), channel_id=1, replica_groups=mesh['groups'=2,'row'=8,'col'=2,'sub'=1] {'row','col'}, dimensions={0} | all-to-all | bytes 1048576 | tf_op jit(solution)/shard_map/all_to_all | solution.py:207
  24.0 0.4 shard_map.83
  24.5 0.0 copy-start.1
  24.5 13.9 %all_to_all.21.recv_ref = bf16[16,4,16,128]{3,2,1,0:T(8,128)(2,1)S(1)} all-to-all(bf16[16,4,16,128]{3,2,1,0:T(8,128)(2,1)S(1)} %shard_map.83), channel_id=1, replica_groups=mesh['groups'=2,'row'=8,'col'=2,'sub'=1] {'row','col'}, dimensions={0} | all-to-all | bytes 524288 | tf_op jit(solution)/shard_map/all_to_all | solution.py:210
  38.3 0.0 copy-done.1
  38.3 1.4 %shard_map.84 = (bf16[8,16,16,128]{3,2,1,0:T(8,128)(2,1)S(1)}, f32[128,1024]{1,0:T(8,128)S(1)}, f32[128,1024]{1,0:T(8,128)S(1)}) custom-call(f32[16,128]{1,0:T(8,128)S(1)} %get-tuple-element.13.live_ref, bf16[128,640]{1,0:T(8,128)(2,1)S(1)} %get-tuple-element.14.weights, bf16[128,128]{1,0:T(8,128)(2,1)S(1)} %copy-done.1, ...), custom_call_target="tpu_custom_call" | custom-call | tf_op jit(solution)/shard_map/pallas_call | solution.py:171
  39.7 11.3 %all_to_all.22.recv_ref = bf16[8,16,16,128]{3,2,1,0:T(8,128)(2,1)S(1)} all-to-all(bf16[8,16,16,128]{3,2,1,0:T(8,128)(2,1)S(1)} %get-tuple-element.18), channel_id=1, replica_groups={{0,1,2,3,4,5,6,7},{8,9,10,11,12,13,14,15},{16,17,18,19,20,21,22,23},{24..., dimensions={0} | all-to-all | bytes 1048576 | tf_op jit(solution)/shard_map/all_to_all | solution.py:212
  51.0 0.4 shard_map.85
  51.4 0.0 copy-start
  51.4 17.7 %all_to_all.23.recv_ref = bf16[16,8,16,128]{3,2,1,0:T(8,128)(2,1)S(1)} all-to-all(bf16[16,8,16,128]{3,2,1,0:T(8,128)(2,1)S(1)} %shard_map.85), channel_id=1, replica_groups=mesh['groups'=2,'row'=8,'col'=2,'sub'=1] {'row','col'}, dimensions={0} | all-to-all | bytes 1048576 | tf_op jit(solution)/shard_map/all_to_all | solution.py:215
  69.2 0.0 copy-done
  69.2 1.5 %shard_map.86 = f32[1024,128]{1,0:T(8,128)} custom-call(bf16[16,8,16,128]{3,2,1,0:T(8,128)(2,1)S(1)} %all_to_all.23.recv_ref, f32[128,1024]{1,0:T(8,128)S(1)} %get-tuple-element.19.middle_ref, f32[128,1024]{1,0:T(8,128)S(1)} %get-tuple-element.20.gating_ref, bf16[128,128]{1,0:T(8,128)(2,1)S(1)} %copy-done), custom_call_target="tpu_custom_call" | custom-call | tf_op jit(solution)/shard_map/pallas_call | solution.py:171
Async XLA Ops:
  24.5 13.9 %copy-start.1 = (bf16[128,128]{1,0:T(8,128)(2,1)S(1)}, bf16[128,128]{1,0:T(8,128)(2,1)}, u32[]{:S(2)}) copy-start(bf16[128,128]{1,0:T(8,128)(2,1)} %final_ref.2) | copy-start | bytes 98308
  51.4 17.8 %copy-start = (bf16[128,128]{1,0:T(8,128)(2,1)S(1)}, bf16[128,128]{1,0:T(8,128)(2,1)}, u32[]{:S(2)}) copy-start(bf16[128,128]{1,0:T(8,128)(2,1)} %final_ref.3) | copy-start | bytes 98308

commit v4 on v3

--- a/solution.py
+++ b/solution.py
@@ -11,6 +11,9 @@
 BF16 = jnp.bfloat16
 LANES = 128
 CHUNK = 256
+NEAR = 8
+SIBLING = 2
+STEPS = (0, 1, 4, 5)
 EPS = 1e-05
 
 
@@ -24,12 +27,17 @@
     return lax.dot_general(weight, values, (((0,), (0,)), ((), ())), preferred_element_type=F32)
 
 
-def side_by_side(proj_ref, gate_ref, wide, weights):
+def side_by_side(proj_ref, gate_ref, wide, weights, order):
     channels, hidden = gate_ref.shape
     wide[...] = proj_ref[...].astype(F32)
-    side = 2 * lax.axis_index("col")
-    for n, p in enumerate((side, side + 1, 2 - side, 3 - side)):
-        weights[:, n * hidden : (n + 1) * hidden] = wide[pl.ds(p, channels, stride=4), :].astype(BF16)
+    col = lax.axis_index("col")
+    for n in range(4):
+        if order == "panels":
+            panel = wide[pl.ds(n + 2 * col if n < 2 else n - 2 * col, channels, stride=4), :]
+        else:
+            panel = wide[pl.ds(n, channels, stride=4), :]
+            panel = jnp.where(col == 1, pltpu.roll(panel, hidden // 2, 1), panel)
+        weights[:, n * hidden : (n + 1) * hidden] = panel.astype(BF16)
     weights[:, 4 * hidden :] = gate_ref[...]
 
 
@@ -44,26 +52,25 @@
     return row_live * col_live
 
 
-def panels(normed, weights, live, msg_ref, gating_ref, rows, cols):
+def panels(normed, weights, gating_ref):
     linear = product(weights[...], normed)
     hidden = linear.shape[0] // 5
     gating_ref[...] = jax.nn.sigmoid(linear[4 * hidden :])
     first = jax.nn.sigmoid(linear[hidden : 2 * hidden]) * linear[:hidden]
     second = jax.nn.sigmoid(linear[3 * hidden : 4 * hidden]) * linear[2 * hidden : 3 * hidden]
-    low = lax.broadcasted_iota(jnp.int32, (hidden, LANES), 1) < cols
+    return first, second
+
+
+def paired(first, second, live, cols):
+    low = lax.broadcasted_iota(jnp.int32, (first.shape[0], LANES), 1) < cols
     by_row = []
-    for t in range(rows // 2):
+    for t in range(live.shape[0] // 2):
         a = first[:, t * LANES : (t + 1) * LANES]
         b = second[:, t * LANES : (t + 1) * LANES]
         for tile in (jnp.where(low, a, pltpu.roll(b, cols, 1)), jnp.where(low, pltpu.roll(a, cols, 1), b)):
             row = len(by_row)
             by_row.append((tile * live[row : row + 1]).astype(BF16))
-    by_hidden = jnp.swapaxes(jnp.stack(by_row, axis=0), 0, 1)
-    devices, per_device = msg_ref.shape[:2]
-    half = per_device // 2
-    for d in range(devices):
-        msg_ref[d, :half] = by_hidden[d * half : (d + 1) * half]
-        msg_ref[d, half:] = by_hidden[hidden // 2 + d * half : hidden // 2 + (d + 1) * half]
+    return jnp.swapaxes(jnp.stack(by_row, axis=0), 0, 1)
 
 
 def projected(recv_ref, final_ref, tiles, rows, cols):
@@ -92,24 +99,44 @@
     return started
 
 
+def near_index():
+    return (lax.axis_index("row") * 2 + lax.axis_index("col")) % NEAR
+
+
 def first_kernel(
-    rows, cols, pair_hbm, mask_hbm, proj_hbm, gate_hbm, proj2_hbm, gate2_hbm, msg_ref, pair_t_ref, gating_ref, live_ref, weights2,
-    pair_ref, mask_ref, proj_ref, gate_ref, proj2_ref, gate2_ref, weights, wide, done,
+    rows, cols, pair_hbm, mask_hbm, proj_hbm, gate_hbm, proj2_hbm, gate2_hbm,
+    b_ref, keep_ref, give_ref, pair_t_ref, gating_ref, live_ref, weights2,
+    pair_ref, mask_ref, proj_ref, gate_ref, proj2_ref, gate2_ref, weights, wide, by_near, done,
 ):
     whole = ((mask_hbm, mask_ref), (proj_hbm, proj_ref), (gate_hbm, gate_ref), (proj2_hbm, proj2_ref), (gate2_hbm, gate2_ref))
     chunks = [slice(at, at + CHUNK) for at in range(0, rows * cols, CHUNK)]
     coming = copies([(pair_hbm.at[at], pair_ref.at[at]) for at in chunks] + list(whole), done)
     for copy in coming[len(chunks) :]:
         copy.wait()
-    side_by_side(proj_ref, gate_ref, wide, weights)
-    side_by_side(proj2_ref, gate2_ref, wide, weights2)
+    side_by_side(proj_ref, gate_ref, wide, weights, "halves")
+    side_by_side(proj2_ref, gate2_ref, wide, weights2, "panels")
     for copy in coming[: len(chunks)]:
         copy.wait()
     pair = pair_ref[...].T
     pair_t_ref[...] = pair
     live = live_tile(mask_ref, rows, cols)
     live_ref[...] = live
-    panels(over_channels(pair).astype(BF16), weights, live, msg_ref, gating_ref, rows, cols)
+    a, b = panels(over_channels(pair).astype(BF16), weights, gating_ref)
+    half = a.shape[0] // 2
+    b_tiles = paired(b[:half], b[half:], live, cols).reshape((NEAR,) + b_ref.shape[1:])
+    b_ref[:NEAR] = b_tiles
+    b_ref[NEAR:] = b_tiles
+    by_near[...] = paired(a[:half], a[half:], live, cols).reshape(by_near.shape)
+    me = near_index()
+    for n, step in enumerate(STEPS):
+        keep_ref[n] = by_near[me ^ step]
+        give_ref[n] = by_near[me ^ step ^ SIBLING]
+
+
+def forward_kernel(keep_ref, got_ref, *out_refs):
+    for n, out_ref in enumerate(out_refs):
+        out_ref[0] = keep_ref[n + 1]
+        out_ref[1] = got_ref[n + 1]
 
 
 def middle_kernel(
@@ -117,7 +144,14 @@
 ):
     middle = pair_t_ref[...] + gating_ref[...] * projected(recv_ref, final_ref, tiles, rows, cols)
     middle_ref[...] = middle
-    panels(over_channels(middle).astype(BF16), weights, live_ref[...], msg_ref, gating2_ref, rows, cols)
+    a, b = panels(over_channels(middle).astype(BF16), weights, gating2_ref)
+    hidden = a.shape[0]
+    by_hidden = paired(a, b, live_ref[...], cols)
+    devices, per_device = msg_ref.shape[:2]
+    half = per_device // 2
+    for d in range(devices):
+        msg_ref[d, :half] = by_hidden[d * half : (d + 1) * half]
+        msg_ref[d, half:] = by_hidden[hidden // 2 + d * half : hidden // 2 + (d + 1) * half]
 
 
 def last_kernel(rows, cols, recv_ref, middle_ref, gating_ref, final_ref, out_hbm, tiles, out_ref, done):
@@ -132,33 +166,55 @@
         copy.wait()
 
 
-def mix_kernel(incoming, cols, recv_ref, msg_ref):
-    sources, per_device, rows, _ = recv_ref.shape
-    half = per_device // 2
-
-    def low(x):
-        return lax.broadcasted_iota(jnp.int32, x.shape, 1) < cols
+def low_of(x, cols):
+    return lax.broadcasted_iota(jnp.int32, x.shape, 1) < cols
+
+
+def both(ref, e):
+    sources = ref.shape[0]
+    return [jnp.concatenate([ref[r, e] for r in range(odd, sources, 2)], axis=0) for odd in (0, 1)]
+
+
+def put(left, right, msg_ref, q):
+    rows = msg_ref.shape[2]
+    for r in range(msg_ref.shape[0] // 2):
+        msg_ref[2 * r, q] = left[r * rows : (r + 1) * rows].astype(BF16)
+        msg_ref[2 * r + 1, q] = right[r * rows : (r + 1) * rows].astype(BF16)
+
+
+def outgoing_kernel(cols, b_ref, keep_ref, got_ref, *refs):
+    *moved_refs, msg_ref, a_ref = refs
+    me = near_index()
+    for n, step in enumerate(STEPS):
+        own, other = (keep_ref.at[0], got_ref.at[0]) if n == 0 else (moved_refs[n - 1].at[0], moved_refs[n - 1].at[1])
+        a_ref[me ^ step] = own[...]
+        a_ref[me ^ step ^ SIBLING] = other[...]
+    for q in range(msg_ref.shape[1]):
+        even, odd = both(a_ref, q)
+        low = low_of(even, cols)
+        a, a2 = jnp.where(low, even, odd), jnp.where(low, odd, even)
+        even, odd = both(b_ref, q)
+        low = low_of(even, cols)
+        b, b2 = jnp.where(low, even, odd), jnp.where(low, odd, even)
+        x = lax.dot_general(a, b, (((1,), (1,)), ((), ())), preferred_element_type=F32)
+        y = lax.dot_general(a2, b2, (((1,), (1,)), ((), ())), preferred_element_type=F32)
+        low = low_of(x, cols)
+        put(jnp.where(low, x, pltpu.roll(y, cols, 1)), jnp.where(low, pltpu.roll(x, cols, 1), y), msg_ref, q)
+
+
+def incoming_kernel(cols, recv_ref, msg_ref):
+    half = msg_ref.shape[1]
 
     def mixed(e):
-        even = jnp.concatenate([recv_ref[r, e] for r in range(0, sources, 2)], axis=0)
-        odd = jnp.concatenate([recv_ref[r, e] for r in range(1, sources, 2)], axis=0)
-        a = jnp.where(low(even), even, odd)
-        b = jnp.where(low(even), odd, even)
-        if incoming:
-            x = lax.dot_general(a, b, (((0,), (0,)), ((), ())), preferred_element_type=F32)
-            return pltpu.roll(x, cols, 1), x
-        b = pltpu.roll(b.astype(F32), cols, 1).astype(BF16)
-        x = lax.dot_general(a, b, (((1,), (1,)), ((), ())), preferred_element_type=F32)
-        return x, pltpu.roll(x, cols, 1)
+        even, odd = both(recv_ref, e)
+        low = low_of(even, cols)
+        a, b = jnp.where(low, even, odd), jnp.where(low, odd, even)
+        return lax.dot_general(a, b, (((0,), (0,)), ((), ())), preferred_element_type=F32)
 
     for q in range(half):
-        x, x_turned = mixed(q)
-        y, y_turned = mixed(q + half)
-        left = jnp.where(low(x), x, y_turned).astype(BF16)
-        right = jnp.where(low(x), x_turned, y).astype(BF16)
-        for r in range(msg_ref.shape[0] // 2):
-            msg_ref[2 * r, q] = left[r * rows : (r + 1) * rows]
-            msg_ref[2 * r + 1, q] = right[r * rows : (r + 1) * rows]
+        x, y = mixed(q), mixed(q + half)
+        low = low_of(x, cols)
+        put(jnp.where(low, pltpu.roll(x, cols, 1), y), jnp.where(low, x, pltpu.roll(y, cols, 1)), msg_ref, q)
 
 
 def call(kernel, out_shape, scratch=(), far=(0, False)):
@@ -185,10 +241,13 @@
     hidden = out_proj.shape[2]
     positions = rows * cols
     shape = jax.ShapeDtypeStruct
-    near = devices // 2
-    halves = [list(range(near)), list(range(near, devices))]
-    exchange = functools.partial(lax.all_to_all, axis_name=("row", "col"), split_axis=0, concat_axis=0, tiled=True)
+    axes = ("row", "col")
+    halves = [list(range(NEAR)), list(range(NEAR, devices))]
+    exchange = functools.partial(lax.all_to_all, axis_name=axes, split_axis=0, concat_axis=0, tiled=True)
     exchange_near = functools.partial(exchange, axis_index_groups=halves)
+
+    def swap(values, step):
+        return lax.ppermute(values, axes, [(d, d ^ step) for d in range(devices)])
 
     def messages(targets, tiles):
         return shape((targets, tiles, rows, LANES), BF16)
@@ -199,17 +258,26 @@
     tiles = pltpu.VMEM((positions, LANES), F32)
     weights = (channels, 5 * hidden)
     chunks = positions // CHUNK
+    pairs = hidden // NEAR // 2
+    steps = messages(len(STEPS), pairs)
 
     far = (pair.reshape(positions, channels), mask, out_proj.reshape(-1, hidden), out_gate, in_proj.reshape(-1, hidden), in_gate)
-    scratch = [pltpu.VMEM(a.shape, a.dtype) for a in far] + [pltpu.VMEM(weights, BF16), pltpu.VMEM((4 * channels, hidden), F32), pltpu.SemaphoreType.DMA((chunks + 5,))]
-    outs = (messages(devices, hidden // devices), plane, plane, shape((rows, LANES), F32), shape(weights, BF16))
-    msg, pair_t, gating, live, weights = call(functools.partial(first_kernel, rows, cols), outs, scratch, (6, False))(*far)
-    mixed = call(functools.partial(mix_kernel, False, cols), messages(devices, hidden // devices // 2))(exchange(msg))
-    outs = (messages(near, hidden // near), plane, plane)
+    outs = (messages(devices, pairs), steps, steps, plane, plane, shape((rows, LANES), F32), shape(weights, BF16))
+    scratch = [pltpu.VMEM(a.shape, a.dtype) for a in far]
+    scratch += [pltpu.VMEM(weights, BF16), pltpu.VMEM((4 * channels, hidden), F32)]
+    scratch += [pltpu.VMEM(messages(NEAR, pairs).shape, BF16), pltpu.SemaphoreType.DMA((chunks + 5,))]
+    b, keep, give, pair_t, gating, live, weights = call(functools.partial(first_kernel, rows, cols), outs, scratch, (6, False))(*far)
+    b = exchange(b)
+    got = swap(give, SIBLING)
+    moving = call(forward_kernel, (messages(2, pairs),) * (len(STEPS) - 1))(keep, got)
+    moved = [swap(block, step) for block, step in zip(moving, STEPS[1:])]
+    scratch = [pltpu.VMEM(messages(NEAR, pairs).shape, BF16)]
+    mixed = call(functools.partial(outgoing_kernel, cols), messages(NEAR, pairs), scratch)(b, keep, got, *moved)
+    outs = (messages(NEAR, 2 * pairs), plane, plane)
     msg, middle, gating = call(functools.partial(middle_kernel, rows, cols), outs, [tiles])(
-        live, weights, out_final, exchange(mixed), pair_t, gating
-    )
-    mixed = call(functools.partial(mix_kernel, True, cols), messages(devices, hidden // near // 2))(exchange_near(msg))
+        live, weights, out_final, exchange_near(mixed), pair_t, gating
+    )
+    mixed = call(functools.partial(incoming_kernel, cols), messages(devices, pairs))(exchange_near(msg))
     scratch = [tiles, by_position, pltpu.SemaphoreType.DMA((chunks,))]
     out = call(functools.partial(last_kernel, rows, cols), shape((positions, channels), F32), scratch, (0, True))(
         exchange(mixed), middle, gating, in_final
@@ -288,8 +356,8 @@
         and rows * cols % CHUNK == 0
         and channels == LANES
         and hidden == channels
-        and hidden % (2 * devices) == 0
-        and axes["row"] % 2 == 0
+        and devices == 2 * NEAR
+        and hidden % (2 * NEAR) == 0
         and hidden % 16 == 0
     )
     plan = functools.partial(by_channel, devices) if fits else by_position

time: 71.2 us -> 69.2 us (0.972)
  blocking collectives: 64.6 us -> 38.9 us
  starting transfers between devices: 0 us -> 11.3 us
  waiting for transfers between devices: 0 us -> 11.3 us
  Pallas kernels: 6.08 us -> 7.07 us
    all_to_all x1, blocking collectives: 21.7 us -> 8.71 us  [by_channel(): exchange_near(mixed)]
    all_to_all x2 -> x1, blocking collectives: 31.6 us -> 18.8 us  [by_channel(): exchange(mixed)]
    ppermute x0 -> x4, waiting for transfers between devices: none -> 11.3 us  [swap(): return lax.ppermute(values, axes, [(d, d ^ step) for d in range(devices)])]
    all_to_all x0 -> x1, starting transfers between devices: none -> 7.37 us  [by_channel(): b = exchange(b)]
    ppermute x0 -> x4, starting transfers between devices: none -> 3.96 us  [swap(): return lax.ppermute(values, axes, [(d, d ^ step) for d in range(devices)])]
    pallas_call x5 -> x6, Pallas kernels: 6.08 us -> 7.07 us  [run(): pl.pallas_call(kernel, out_shape=out_shape, in_specs=[hbm] * far_args + [...]
  transfers between devices with their start and end apart: 0 -> 5, of which waited for: 0 -> 4; matrix products, arithmetic and copies ran while one was open for 0% -> 0% of each run, Pallas kernels for 0% -> 0%
where the time goes in v4:
time: 69.2 us; the launch traced here: 68.7 us
  blocking collectives  38.9 us (56%)
  starting transfers between devices  11.3 us (16%)
  waiting for transfers between devices  11.3 us (16%)
  Pallas kernels  7.07 us (10%)
    all_to_all x1, blocking collectives, by_channel(): exchange(mixed)  18.8 us
    all_to_all x1, blocking collectives, by_channel(): exchange_near(msg)  11.4 us
    ppermute x4, waiting for transfers between devices, swap(): return lax.ppermute(values, axes, [(d, d ^ step) for d in range(devices)])  11.3 us
    all_to_all x1, blocking collectives, by_channel(): exchange_near(mixed)  8.71 us
    all_to_all x1, starting transfers between devices, by_channel(): b = exchange(b)  7.37 us
    pallas_call x6, Pallas kernels, run(): pl.pallas_call(kernel, out_shape=out_shape, in_specs=[hbm] * far_args + [...  7.07 us
    ppermute x4, starting transfers between devices, swap(): return lax.ppermute(values, axes, [(d, d ^ step) for d in range(devices)])  3.96 us
  transfers between devices with their start and end apart: 5, of which 4 were waited for; matrix products, arithmetic and copies ran while one was open for 0% of the time, Pallas kernels for 0%

profile of v4, /device:TPU:0, one launch (start us, length us, event | category | flops | bytes accessed | tf_op | source)
XLA Modules:
  0.0 68.7 jit_solution(13342316227123476699)
XLA Ops:
  0.0 3.2 %shard_map.82 = (bf16[16,8,16,128]{3,2,1,0:T(8,128)(2,1)}, bf16[4,8,16,128]{3,2,1,0:T(8,128)(2,1)S(1)}, bf16[4,8,16,128]{3,2,1,0:T(8,128)(2,1)S(1)}, f32[128,102...) custom-call(f32[1024,128]{1,0:T(8,128)} %bitcast.5, ...), custom_call_target="tpu_custom_call" | custom-call | tf_op jit(solution)/shard_map/pallas_call | solution.py:227
  3.2 7.4 %all-to-all-start = ((bf16[16,8,16,128]{3,2,1,0:T(8,128)(2,1)}), bf16[16,8,16,128]{3,2,1,0:T(8,128)(2,1)S(1)}, u32[]{:S(2)}, u32[]{:S(2)}) async-start(bf16[16,8,16,128]{3,2,1,0:T(8,128)(2,1)} %get-tuple-element.20), calls=%async_computation | async-start | bytes 1048576 | tf_op jit(solution)/shard_map/all_to_all | solution.py:270
  10.5 0.4 collective-permute-start
  11.0 1.0 %collective-permute-done.got_ref = bf16[4,8,16,128]{3,2,1,0:T(8,128)(2,1)S(1)} collective-permute-done((bf16[4,8,16,128]{3,2,1,0:T(8,128)(2,1)S(1)}, bf16[4,8,16,128]{3,2,1,0:T(8,128)(2,1)S(1)}, u32[]{:S(2)}, u32[]{:S(2)}) %collective-permute-start) | collective-permute-done | bytes 131104 | tf_op jit(solution)/shard_map/ppermute | solution.py:250
  12.0 1.9 %collective-permute-start.1 = (bf16[2,8,16,128]{3,2,1,0:T(8,128)(2,1)S(1)}, bf16[2,8,16,128]{3,2,1,0:T(8,128)(2,1)S(1)}, u32[]{:S(2)}, u32[]{:S(2)}) collective-permute-start(bf16[2,8,16,128]{3,2,1,0:T(8,128)(2,1)S(1)} %get-tuple-element.23), channel_id=1, source_target_pairs={{0,1},{1,0},{2,3},{3,2},{4,5},{5,4},{6,7},{7,6},{8,9},{9,8},{10,11... | collective-permute-start | bytes 196616 | tf_op jit(solution)/shard_map/ppermute | solution.py:250
  13.9 1.5 %collective-permute-start.2 = (bf16[2,8,16,128]{3,2,1,0:T(8,128)(2,1)S(1)}, bf16[2,8,16,128]{3,2,1,0:T(8,128)(2,1)S(1)}, u32[]{:S(2)}, u32[]{:S(2)}) collective-permute-start(bf16[2,8,16,128]{3,2,1,0:T(8,128)(2,1)S(1)} %get-tuple-element.24), channel_id=1, source_target_pairs={{0,4},{1,5},{2,6},{3,7},{4,0},{5,1},{6,2},{7,3},{8,12},{9,13},{10,... | collective-permute-start | bytes 196616 | tf_op jit(solution)/shard_map/ppermute | solution.py:250
  15.4 0.2 collective-permute-start.3
  15.5 1.0 %collective-permute-done.1.refs_0_ = bf16[2,8,16,128]{3,2,1,0:T(8,128)(2,1)S(1)} collective-permute-done((bf16[2,8,16,128]{3,2,1,0:T(8,128)(2,1)S(1)}, bf16[2,8,16,128]{3,2,1,0:T(8,128)(2,1)S(1)}, u32[]{:S(2)}, u32[]{:S(2)}) %collective-permute-start.1) | collective-permute-done | bytes 65568 | tf_op jit(solution)/shard_map/ppermute | solution.py:250
  16.5 6.0 %collective-permute-done.2.refs_1_ = bf16[2,8,16,128]{3,2,1,0:T(8,128)(2,1)S(1)} collective-permute-done((bf16[2,8,16,128]{3,2,1,0:T(8,128)(2,1)S(1)}, bf16[2,8,16,128]{3,2,1,0:T(8,128)(2,1)S(1)}, u32[]{:S(2)}, u32[]{:S(2)}) %collective-permute-start.2) | collective-permute-done | bytes 65568 | tf_op jit(solution)/shard_map/ppermute | solution.py:250
  22.5 3.3 %collective-permute-done.3.refs_2_ = bf16[2,8,16,128]{3,2,1,0:T(8,128)(2,1)S(1)} collective-permute-done((bf16[2,8,16,128]{3,2,1,0:T(8,128)(2,1)S(1)}, bf16[2,8,16,128]{3,2,1,0:T(8,128)(2,1)S(1)}, u32[]{:S(2)}, u32[]{:S(2)}) %collective-permute-start.3) | collective-permute-done | bytes 65568 | tf_op jit(solution)/shard_map/ppermute | solution.py:250
  25.8 0.0 all-to-all-done.b_ref
  25.8 0.5 shard_map.84
  26.4 0.0 copy-start.1
  26.4 8.7 %all_to_all.20.recv_ref = bf16[8,8,16,128]{3,2,1,0:T(8,128)(2,1)S(1)} all-to-all(bf16[8,8,16,128]{3,2,1,0:T(8,128)(2,1)S(1)} %shard_map.84), channel_id=1, replica_groups={{0,1,2,3,4,5,6,7},{8,9,10,11,12,13,14,15},{16,17,18,19,20,21,22,23},{24..., dimensions={0} | all-to-all | bytes 524288 | tf_op jit(solution)/shard_map/all_to_all | solution.py:278
  35.1 0.0 copy-done.1
  35.1 1.4 %shard_map.85 = (bf16[8,16,16,128]{3,2,1,0:T(8,128)(2,1)S(1)}, f32[128,1024]{1,0:T(8,128)S(1)}, f32[128,1024]{1,0:T(8,128)S(1)}) custom-call(f32[16,128]{1,0:T(8,128)S(1)} %get-tuple-element.18.live_ref, bf16[128,640]{1,0:T(8,128)(2,1)S(1)} %get-tuple-element.19.weights, bf16[128,128]{1,0:T(8,128)(2,1)S(1)} %copy-done.1, ...), custom_call_target="tpu_custom_call" | custom-call | tf_op jit(solution)/shard_map/pallas_call | solution.py:227
  36.5 11.4 %all_to_all.21.recv_ref = bf16[8,16,16,128]{3,2,1,0:T(8,128)(2,1)S(1)} all-to-all(bf16[8,16,16,128]{3,2,1,0:T(8,128)(2,1)S(1)} %get-tuple-element.28), channel_id=1, replica_groups={{0,1,2,3,4,5,6,7},{8,9,10,11,12,13,14,15},{16,17,18,19,20,21,22,23},{24..., dimensions={0} | all-to-all | bytes 1048576 | tf_op jit(solution)/shard_map/all_to_all | solution.py:280
  47.9 0.4 shard_map.86
  48.3 0.0 copy-start
  48.3 18.8 %all_to_all.22.recv_ref = bf16[16,8,16,128]{3,2,1,0:T(8,128)(2,1)S(1)} all-to-all(bf16[16,8,16,128]{3,2,1,0:T(8,128)(2,1)S(1)} %shard_map.86), channel_id=1, replica_groups=mesh['groups'=2,'row'=8,'col'=2,'sub'=1] {'row','col'}, dimensions={0} | all-to-all | bytes 1048576 | tf_op jit(solution)/shard_map/all_to_all | solution.py:283
  67.1 0.0 copy-done
  67.1 1.5 %shard_map.87 = f32[1024,128]{1,0:T(8,128)} custom-call(bf16[16,8,16,128]{3,2,1,0:T(8,128)(2,1)S(1)} %all_to_all.22.recv_ref, f32[128,1024]{1,0:T(8,128)S(1)} %get-tuple-element.29.middle_ref, f32[128,1024]{1,0:T(8,128)S(1)} %get-tuple-element.30.gating_ref, bf16[128,128]{1,0:T(8,128)(2,1)S(1)} %copy-done), custom_call_target="tpu_custom_call" | custom-call | tf_op jit(solution)/shard_map/pallas_call | solution.py:227
  (1 shorter events, 0.0 us)
Async XLA Ops:
  3.2 22.6 %all-to-all-start = ((bf16[16,8,16,128]{3,2,1,0:T(8,128)(2,1)}), bf16[16,8,16,128]{3,2,1,0:T(8,128)(2,1)S(1)}, u32[]{:S(2)}, u32[]{:S(2)}) async-start(bf16[16,8,16,128]{3,2,1,0:T(8,128)(2,1)} %get-tuple-element.20), calls=%async_computation | async-start | bytes 1048576 | tf_op jit(solution)/shard_map/all_to_all | solution.py:270
  10.5 1.4 %collective-permute-start = (bf16[4,8,16,128]{3,2,1,0:T(8,128)(2,1)S(1)}, bf16[4,8,16,128]{3,2,1,0:T(8,128)(2,1)S(1)}, u32[]{:S(2)}, u32[]{:S(2)}) collective-permute-start(bf16[4,8,16,128]{3,2,1,0:T(8,128)(2,1)S(1)} %get-tuple-element.22), channel_id=1, source_target_pairs={{0,2},{1,3},{2,0},{3,1},{4,6},{5,7},{6,4},{7,5},{8,10},{9,11},{10,... | collective-permute-start | bytes 393224 | tf_op jit(solution)/shard_map/ppermute | solution.py:250
  12.0 4.5 %collective-permute-start.1 = (bf16[2,8,16,128]{3,2,1,0:T(8,128)(2,1)S(1)}, bf16[2,8,16,128]{3,2,1,0:T(8,128)(2,1)S(1)}, u32[]{:S(2)}, u32[]{:S(2)}) collective-permute-start(bf16[2,8,16,128]{3,2,1,0:T(8,128)(2,1)S(1)} %get-tuple-element.23), channel_id=1, source_target_pairs={{0,1},{1,0},{2,3},{3,2},{4,5},{5,4},{6,7},{7,6},{8,9},{9,8},{10,11... | collective-permute-start | bytes 196616 | tf_op jit(solution)/shard_map/ppermute | solution.py:250
  13.9 8.6 %collective-permute-start.2 = (bf16[2,8,16,128]{3,2,1,0:T(8,128)(2,1)S(1)}, bf16[2,8,16,128]{3,2,1,0:T(8,128)(2,1)S(1)}, u32[]{:S(2)}, u32[]{:S(2)}) collective-permute-start(bf16[2,8,16,128]{3,2,1,0:T(8,128)(2,1)S(1)} %get-tuple-element.24), channel_id=1, source_target_pairs={{0,4},{1,5},{2,6},{3,7},{4,0},{5,1},{6,2},{7,3},{8,12},{9,13},{10,... | collective-permute-start | bytes 196616 | tf_op jit(solution)/shard_map/ppermute | solution.py:250
  15.4 10.4 %collective-permute-start.3 = (bf16[2,8,16,128]{3,2,1,0:T(8,128)(2,1)S(1)}, bf16[2,8,16,128]{3,2,1,0:T(8,128)(2,1)S(1)}, u32[]{:S(2)}, u32[]{:S(2)}) collective-permute-start(bf16[2,8,16,128]{3,2,1,0:T(8,128)(2,1)S(1)} %get-tuple-element.25), channel_id=1, source_target_pairs={{0,5},{1,4},{2,7},{3,6},{4,1},{5,0},{6,3},{7,2},{8,13},{9,12},{10,... | collective-permute-start | bytes 196616 | tf_op jit(solution)/shard_map/ppermute | solution.py:250
  26.4 8.7 %copy-start.1 = (bf16[128,128]{1,0:T(8,128)(2,1)S(1)}, bf16[128,128]{1,0:T(8,128)(2,1)}, u32[]{:S(2)}) copy-start(bf16[128,128]{1,0:T(8,128)(2,1)} %final_ref.2) | copy-start | bytes 98308
  48.3 18.8 %copy-start = (bf16[128,128]{1,0:T(8,128)(2,1)S(1)}, bf16[128,128]{1,0:T(8,128)(2,1)}, u32[]{:S(2)}) copy-start(bf16[128,128]{1,0:T(8,128)(2,1)} %final_ref.3) | copy-start | bytes 98308

commit v5 on v4

--- a/solution.py
+++ b/solution.py
@@ -13,7 +13,7 @@
 CHUNK = 256
 NEAR = 8
 SIBLING = 2
-STEPS = (0, 1, 4, 5)
+STEPS = (0, 5, 4, 1)
 EPS = 1e-05
 
 
@@ -27,8 +27,8 @@
     return lax.dot_general(weight, values, (((0,), (0,)), ((), ())), preferred_element_type=F32)
 
 
-def side_by_side(proj_ref, gate_ref, wide, weights, order):
-    channels, hidden = gate_ref.shape
+def side_by_side(proj_ref, wide, weights, order):
+    channels, hidden = weights.shape[0], weights.shape[1] // 4
     wide[...] = proj_ref[...].astype(F32)
     col = lax.axis_index("col")
     for n in range(4):
@@ -38,7 +38,6 @@
             panel = wide[pl.ds(n, channels, stride=4), :]
             panel = jnp.where(col == 1, pltpu.roll(panel, hidden // 2, 1), panel)
         weights[:, n * hidden : (n + 1) * hidden] = panel.astype(BF16)
-    weights[:, 4 * hidden :] = gate_ref[...]
 
 
 def live_tile(mask_ref, rows, cols):
@@ -52,13 +51,20 @@
     return row_live * col_live
 
 
-def panels(normed, weights, gating_ref):
+def panel(normed, weights, which):
+    hidden = weights.shape[1] // 4
+    linear = product(weights[:, 2 * which * hidden : 2 * (which + 1) * hidden], normed)
+    return jax.nn.sigmoid(linear[hidden:]) * linear[:hidden]
+
+
+def panels(normed, weights):
+    hidden = weights.shape[1] // 4
     linear = product(weights[...], normed)
-    hidden = linear.shape[0] // 5
-    gating_ref[...] = jax.nn.sigmoid(linear[4 * hidden :])
-    first = jax.nn.sigmoid(linear[hidden : 2 * hidden]) * linear[:hidden]
-    second = jax.nn.sigmoid(linear[3 * hidden : 4 * hidden]) * linear[2 * hidden : 3 * hidden]
-    return first, second
+    return [jax.nn.sigmoid(linear[(p + 1) * hidden : (p + 2) * hidden]) * linear[p * hidden : (p + 1) * hidden] for p in (0, 2)]
+
+
+def gate_kernel(normed_ref, gate_ref, gating_ref):
+    gating_ref[...] = jax.nn.sigmoid(product(gate_ref[...], normed_ref[...]))
 
 
 def paired(first, second, live, cols):
@@ -103,34 +109,51 @@
     return (lax.axis_index("row") * 2 + lax.axis_index("col")) % NEAR
 
 
+def hand_out(by_near, keep_ref, give_ref):
+    me = near_index()
+    for n, step in enumerate(STEPS):
+        keep_ref[n] = by_near[me ^ step]
+        give_ref[n] = by_near[me ^ step ^ SIBLING]
+
+
+def take_in(refs, by_near):
+    keep_ref, got_ref, *moved_refs = refs
+    me = near_index()
+    by_near[me] = keep_ref[0]
+    by_near[me ^ SIBLING] = got_ref[0]
+    for step, moved_ref in zip(STEPS[1:], moved_refs):
+        by_near[me ^ step] = moved_ref[0]
+        by_near[me ^ step ^ SIBLING] = moved_ref[1]
+
+
 def first_kernel(
-    rows, cols, pair_hbm, mask_hbm, proj_hbm, gate_hbm, proj2_hbm, gate2_hbm,
-    b_ref, keep_ref, give_ref, pair_t_ref, gating_ref, live_ref, weights2,
-    pair_ref, mask_ref, proj_ref, gate_ref, proj2_ref, gate2_ref, weights, wide, by_near, done,
+    rows, cols, pair_hbm, mask_hbm, proj_hbm, proj2_hbm, b_hbm, keep_ref, give_ref, pair_t_ref, normed_ref, live_ref, weights2,
+    pair_ref, mask_ref, proj_ref, proj2_ref, weights, wide, b_tiles, by_near, done,
 ):
-    whole = ((mask_hbm, mask_ref), (proj_hbm, proj_ref), (gate_hbm, gate_ref), (proj2_hbm, proj2_ref), (gate2_hbm, gate2_ref))
     chunks = [slice(at, at + CHUNK) for at in range(0, rows * cols, CHUNK)]
-    coming = copies([(pair_hbm.at[at], pair_ref.at[at]) for at in chunks] + list(whole), done)
+    whole = [(mask_hbm, mask_ref), (proj_hbm, proj_ref), (proj2_hbm, proj2_ref)]
+    coming = copies([(pair_hbm.at[at], pair_ref.at[at]) for at in chunks] + whole, done)
     for copy in coming[len(chunks) :]:
         copy.wait()
-    side_by_side(proj_ref, gate_ref, wide, weights, "halves")
-    side_by_side(proj2_ref, gate2_ref, wide, weights2, "panels")
+    side_by_side(proj_ref, wide, weights, "halves")
+    side_by_side(proj2_ref, wide, weights2, "panels")
+    live = live_tile(mask_ref, rows, cols)
+    live_ref[...] = live
     for copy in coming[: len(chunks)]:
         copy.wait()
     pair = pair_ref[...].T
     pair_t_ref[...] = pair
-    live = live_tile(mask_ref, rows, cols)
-    live_ref[...] = live
-    a, b = panels(over_channels(pair).astype(BF16), weights, gating_ref)
-    half = a.shape[0] // 2
-    b_tiles = paired(b[:half], b[half:], live, cols).reshape((NEAR,) + b_ref.shape[1:])
-    b_ref[:NEAR] = b_tiles
-    b_ref[NEAR:] = b_tiles
+    normed = over_channels(pair).astype(BF16)
+    normed_ref[...] = normed
+    b = panel(normed, weights, 1)
+    half = b.shape[0] // 2
+    b_tiles[...] = paired(b[:half], b[half:], live, cols).reshape(b_tiles.shape)
+    leaving = copies([(b_tiles, b_hbm.at[:NEAR]), (b_tiles, b_hbm.at[NEAR:])], done)
+    a = panel(normed, weights, 0)
     by_near[...] = paired(a[:half], a[half:], live, cols).reshape(by_near.shape)
-    me = near_index()
-    for n, step in enumerate(STEPS):
-        keep_ref[n] = by_near[me ^ step]
-        give_ref[n] = by_near[me ^ step ^ SIBLING]
+    hand_out(by_near, keep_ref, give_ref)
+    for copy in leaving:
+        copy.wait()
 
 
 def forward_kernel(keep_ref, got_ref, *out_refs):
@@ -139,19 +162,22 @@
         out_ref[1] = got_ref[n + 1]
 
 
-def middle_kernel(
-    rows, cols, live_ref, weights, final_ref, recv_ref, pair_t_ref, gating_ref, msg_ref, middle_ref, gating2_ref, tiles
-):
-    middle = pair_t_ref[...] + gating_ref[...] * projected(recv_ref, final_ref, tiles, rows, cols)
+def middle_kernel(rows, cols, live_ref, weights, final_ref, pair_t_ref, gating_ref, *refs):
+    *came_refs, keep_ref, give_ref, middle_ref, normed_ref, tiles, came, by_near = refs
+    take_in(came_refs, came)
+    middle = pair_t_ref[...] + gating_ref[...] * projected(came, final_ref, tiles, rows, cols)
     middle_ref[...] = middle
-    a, b = panels(over_channels(middle).astype(BF16), weights, gating2_ref)
+    normed = over_channels(middle).astype(BF16)
+    normed_ref[...] = normed
+    a, b = panels(normed, weights)
     hidden = a.shape[0]
     by_hidden = paired(a, b, live_ref[...], cols)
-    devices, per_device = msg_ref.shape[:2]
+    devices, per_device = by_near.shape[:2]
     half = per_device // 2
     for d in range(devices):
-        msg_ref[d, :half] = by_hidden[d * half : (d + 1) * half]
-        msg_ref[d, half:] = by_hidden[hidden // 2 + d * half : hidden // 2 + (d + 1) * half]
+        by_near[d, :half] = by_hidden[d * half : (d + 1) * half]
+        by_near[d, half:] = by_hidden[hidden // 2 + d * half : hidden // 2 + (d + 1) * half]
+    hand_out(by_near, keep_ref, give_ref)
 
 
 def last_kernel(rows, cols, recv_ref, middle_ref, gating_ref, final_ref, out_hbm, tiles, out_ref, done):
@@ -182,13 +208,9 @@
         msg_ref[2 * r + 1, q] = right[r * rows : (r + 1) * rows].astype(BF16)
 
 
-def outgoing_kernel(cols, b_ref, keep_ref, got_ref, *refs):
-    *moved_refs, msg_ref, a_ref = refs
-    me = near_index()
-    for n, step in enumerate(STEPS):
-        own, other = (keep_ref.at[0], got_ref.at[0]) if n == 0 else (moved_refs[n - 1].at[0], moved_refs[n - 1].at[1])
-        a_ref[me ^ step] = own[...]
-        a_ref[me ^ step ^ SIBLING] = other[...]
+def outgoing_kernel(cols, b_ref, *refs):
+    *came_refs, keep_ref, give_ref, a_ref, msg_ref = refs
+    take_in(came_refs, a_ref)
     for q in range(msg_ref.shape[1]):
         even, odd = both(a_ref, q)
         low = low_of(even, cols)
@@ -200,9 +222,12 @@
         y = lax.dot_general(a2, b2, (((1,), (1,)), ((), ())), preferred_element_type=F32)
         low = low_of(x, cols)
         put(jnp.where(low, x, pltpu.roll(y, cols, 1)), jnp.where(low, pltpu.roll(x, cols, 1), y), msg_ref, q)
-
-
-def incoming_kernel(cols, recv_ref, msg_ref):
+    hand_out(msg_ref, keep_ref, give_ref)
+
+
+def incoming_kernel(cols, *refs):
+    *came_refs, msg_ref, recv_ref = refs
+    take_in(came_refs, recv_ref)
     half = msg_ref.shape[1]
 
     def mixed(e):
@@ -217,7 +242,7 @@
         put(jnp.where(low, pltpu.roll(x, cols, 1), y), jnp.where(low, x, pltpu.roll(y, cols, 1)), msg_ref, q)
 
 
-def call(kernel, out_shape, scratch=(), far=(0, False)):
+def call(kernel, out_shape, scratch=(), far=(0, 0), flops=0, transcendentals=0):
     vmem = pl.BlockSpec(memory_space=pltpu.VMEM)
     hbm = pl.BlockSpec(memory_space=pltpu.HBM)
     far_args, far_outs = far
@@ -226,11 +251,14 @@
         args = [pltpu.with_memory_space_constraint(a, pltpu.HBM) for a in args[:far_args]] + list(args[far_args:])
         return pl.pallas_call(
             kernel,
-            out_shape=out_shape,
+            out_shape=tuple(out_shape),
             in_specs=[hbm] * far_args + [vmem] * (len(args) - far_args),
-            out_specs=jax.tree.map(lambda _: hbm if far_outs else vmem, out_shape),
+            out_specs=(hbm,) * far_outs + (vmem,) * (len(out_shape) - far_outs),
             scratch_shapes=list(scratch),
             compiler_params=pltpu.CompilerParams(vmem_limit_bytes=40 * 1024 * 1024),
+            cost_estimate=pl.CostEstimate(
+                flops=flops, transcendentals=transcendentals, bytes_accessed=sum(a.size * a.dtype.itemsize for a in (*args, *out_shape))
+            ),
         )(*args)
 
     return run
@@ -242,44 +270,53 @@
     positions = rows * cols
     shape = jax.ShapeDtypeStruct
     axes = ("row", "col")
-    halves = [list(range(NEAR)), list(range(NEAR, devices))]
     exchange = functools.partial(lax.all_to_all, axis_name=axes, split_axis=0, concat_axis=0, tiled=True)
-    exchange_near = functools.partial(exchange, axis_index_groups=halves)
 
     def swap(values, step):
         return lax.ppermute(values, axes, [(d, d ^ step) for d in range(devices)])
 
+    def within_half(keep, give):
+        got = swap(give, SIBLING)
+        moving = call(forward_kernel, (shape((2,) + keep.shape[1:], BF16),) * (len(STEPS) - 1))(keep, got)
+        return (keep, got, *(swap(block, step) for block, step in zip(moving, STEPS[1:])))
+
     def messages(targets, tiles):
         return shape((targets, tiles, rows, LANES), BF16)
 
+    def near_tiles(tiles):
+        return pltpu.VMEM(messages(NEAR, tiles).shape, BF16)
+
     plane = shape((channels, positions), F32)
+    half_plane = shape((channels, positions), BF16)
     mask = residue_mask.reshape(1, -1)
     by_position = pltpu.VMEM((positions, channels), F32)
     tiles = pltpu.VMEM((positions, LANES), F32)
-    weights = (channels, 5 * hidden)
+    weights = (channels, 4 * hidden)
     chunks = positions // CHUNK
     pairs = hidden // NEAR // 2
-    steps = messages(len(STEPS), pairs)
-
-    far = (pair.reshape(positions, channels), mask, out_proj.reshape(-1, hidden), out_gate, in_proj.reshape(-1, hidden), in_gate)
-    outs = (messages(devices, pairs), steps, steps, plane, plane, shape((rows, LANES), F32), shape(weights, BF16))
+    steps = (messages(len(STEPS), pairs),) * 2
+    wide_steps = (messages(len(STEPS), 2 * pairs),) * 2
+    gate = call(gate_kernel, [plane], flops=2 * channels * channels * positions, transcendentals=channels * positions)
+
+    far = (pair.reshape(positions, channels), mask, out_proj.reshape(-1, hidden), in_proj.reshape(-1, hidden))
+    outs = (messages(devices, pairs), *steps, plane, half_plane, shape((rows, LANES), F32), shape(weights, BF16))
     scratch = [pltpu.VMEM(a.shape, a.dtype) for a in far]
     scratch += [pltpu.VMEM(weights, BF16), pltpu.VMEM((4 * channels, hidden), F32)]
-    scratch += [pltpu.VMEM(messages(NEAR, pairs).shape, BF16), pltpu.SemaphoreType.DMA((chunks + 5,))]
-    b, keep, give, pair_t, gating, live, weights = call(functools.partial(first_kernel, rows, cols), outs, scratch, (6, False))(*far)
+    scratch += [near_tiles(pairs), near_tiles(pairs), pltpu.SemaphoreType.DMA((chunks + 3,))]
+    b, keep, give, pair_t, normed, live, weights = call(functools.partial(first_kernel, rows, cols), outs, scratch, (4, 1))(*far)
     b = exchange(b)
-    got = swap(give, SIBLING)
-    moving = call(forward_kernel, (messages(2, pairs),) * (len(STEPS) - 1))(keep, got)
-    moved = [swap(block, step) for block, step in zip(moving, STEPS[1:])]
-    scratch = [pltpu.VMEM(messages(NEAR, pairs).shape, BF16)]
-    mixed = call(functools.partial(outgoing_kernel, cols), messages(NEAR, pairs), scratch)(b, keep, got, *moved)
-    outs = (messages(NEAR, 2 * pairs), plane, plane)
-    msg, middle, gating = call(functools.partial(middle_kernel, rows, cols), outs, [tiles])(
-        live, weights, out_final, exchange_near(mixed), pair_t, gating
-    )
-    mixed = call(functools.partial(incoming_kernel, cols), messages(devices, pairs))(exchange_near(msg))
+    a = within_half(keep, give)
+    (gating,) = gate(normed, out_gate)
+    keep, give = call(functools.partial(outgoing_kernel, cols), steps, [near_tiles(pairs)] * 2)(b, *a)
+    scratch = [tiles, near_tiles(pairs), near_tiles(2 * pairs)]
+    keep, give, middle, normed = call(functools.partial(middle_kernel, rows, cols), (*wide_steps, plane, half_plane), scratch)(
+        live, weights, out_final, pair_t, gating, *within_half(keep, give)
+    )
+    came = within_half(keep, give)
+    gating, came = lax.optimization_barrier((gate(normed, in_gate)[0], came))
+    (mixed,) = call(functools.partial(incoming_kernel, cols), [messages(devices, pairs)], [near_tiles(2 * pairs)])(*came)
     scratch = [tiles, by_position, pltpu.SemaphoreType.DMA((chunks,))]
-    out = call(functools.partial(last_kernel, rows, cols), shape((positions, channels), F32), scratch, (0, True))(
+    (out,) = call(functools.partial(last_kernel, rows, cols), [shape((positions, channels), F32)], scratch, (0, 1))(
         exchange(mixed), middle, gating, in_final
     )
     return out.reshape(rows, cols, channels)

time: 69.2 us -> 67.4 us (0.974)
  blocking collectives: 38.9 us -> 18.6 us
  waiting for transfers between devices: 11.3 us -> 21.6 us
  starting transfers between devices: 11.3 us -> 19.1 us
    all_to_all x2 -> x0, blocking collectives: 20.1 us -> none  [the longest x1 11.4 us: by_channel(): exchange_near(msg)]
    ppermute x4 -> x12, waiting for transfers between devices: 11.3 us -> 21.5 us  [swap(): return lax.ppermute(values, axes, [(d, d ^ step) for d in range(devices)])]
    ppermute x4 -> x12, starting transfers between devices: 3.96 us -> 11.7 us  [swap(): return lax.ppermute(values, axes, [(d, d ^ step) for d in range(devices)])]
    pallas_call x6 -> x10, Pallas kernels: 7.07 us -> 7.52 us  [run(): pl.pallas_call(kernel, out_shape=tuple(out_shape), in_specs=[hbm] * far_a...]
  transfers between devices with their start and end apart: 5 -> 13, of which waited for: 4 -> 12; matrix products, arithmetic and copies ran while one was open for 0% -> 0% of each run, Pallas kernels for 0% -> 1%
where the time goes in v5:
time: 67.4 us; the launch traced here: 67 us
  waiting for transfers between devices  21.6 us (32%)
  starting transfers between devices  19.1 us (28%)
  blocking collectives  18.6 us (28%)
  Pallas kernels  7.52 us (11%)
    ppermute x12, waiting for transfers between devices, swap(): return lax.ppermute(values, axes, [(d, d ^ step) for d in range(devices)])  21.5 us
    all_to_all x1, blocking collectives, by_channel(): exchange(mixed)  18.6 us
    ppermute x12, starting transfers between devices, swap(): return lax.ppermute(values, axes, [(d, d ^ step) for d in range(devices)])  11.7 us
    pallas_call x10, Pallas kernels, run(): pl.pallas_call(kernel, out_shape=tuple(out_shape), in_specs=[hbm] * far_a...  7.52 us
    all_to_all x1, starting transfers between devices, by_channel(): b = exchange(b)  7.37 us
  transfers between devices with their start and end apart: 13, of which 12 were waited for; matrix products, arithmetic and copies ran while one was open for 0% of the time, Pallas kernels for 1%

profile of v5, /device:TPU:0, one launch (start us, length us, event | category | flops | bytes accessed | tf_op | source)
XLA Modules:
  0.0 67.0 jit_solution(11807289301692595347)
XLA Ops:
  0.0 3.0 %shard_map.82 = (bf16[16,8,16,128]{3,2,1,0:T(8,128)(2,1)}, bf16[4,8,16,128]{3,2,1,0:T(8,128)(2,1)S(1)}, bf16[4,8,16,128]{3,2,1,0:T(8,128)(2,1)S(1)}, f32[128,102...) custom-call(f32[1024,128]{1,0:T(8,128)} %bitcast.5, ...), custom_call_target="tpu_custom_call" | custom-call | bytes 2499072 | tf_op jit(solution)/shard_map/pallas_call | solution.py:252
  3.0 7.4 %all-to-all-start = ((bf16[16,8,16,128]{3,2,1,0:T(8,128)(2,1)}), bf16[16,8,16,128]{3,2,1,0:T(8,128)(2,1)S(1)}, u32[]{:S(2)}, u32[]{:S(2)}) async-start(bf16[16,8,16,128]{3,2,1,0:T(8,128)(2,1)} %get-tuple-element.37), calls=%async_computation | async-start | bytes 1048576 | tf_op jit(solution)/shard_map/all_to_all | solution.py:307
  10.8 1.0 %collective-permute-done.got_ref.refs_1_ = bf16[4,8,16,128]{3,2,1,0:T(8,128)(2,1)S(1)} collective-permute-done((bf16[4,8,16,128]{3,2,1,0:T(8,128)(2,1)S(1)}, bf16[4,8,16,128]{3,2,1,0:T(8,128)(2,1)S(1)}, u32[]{:S(2)}, u32[]{:S(2)}) %collective-permute-start) | collective-permute-done | bytes 131104 | tf_op jit(solution)/shard_map/ppermute | solution.py:276
  11.8 2.8 %collective-permute-start.1 = (bf16[2,8,16,128]{3,2,1,0:T(8,128)(2,1)S(1)}, bf16[2,8,16,128]{3,2,1,0:T(8,128)(2,1)S(1)}, u32[]{:S(2)}, u32[]{:S(2)}) collective-permute-start(bf16[2,8,16,128]{3,2,1,0:T(8,128)(2,1)S(1)} %get-tuple-element.40), channel_id=1, source_target_pairs={{0,5},{1,4},{2,7},{3,6},{4,1},{5,0},{6,3},{7,2},{8,13},{9,12},{10,... | collective-permute-start | bytes 196616 | tf_op jit(solution)/shard_map/ppermute | solution.py:276
  14.6 0.6 collective-permute-start.2
  15.4 7.9 %collective-permute-done.1.refs_2_ = bf16[2,8,16,128]{3,2,1,0:T(8,128)(2,1)S(1)} collective-permute-done((bf16[2,8,16,128]{3,2,1,0:T(8,128)(2,1)S(1)}, bf16[2,8,16,128]{3,2,1,0:T(8,128)(2,1)S(1)}, u32[]{:S(2)}, u32[]{:S(2)}) %collective-permute-start.1) | collective-permute-done | bytes 65568 | tf_op jit(solution)/shard_map/ppermute | solution.py:276
  23.2 1.5 %collective-permute-done.2.refs_3_ = bf16[2,8,16,128]{3,2,1,0:T(8,128)(2,1)S(1)} collective-permute-done((bf16[2,8,16,128]{3,2,1,0:T(8,128)(2,1)S(1)}, bf16[2,8,16,128]{3,2,1,0:T(8,128)(2,1)S(1)}, u32[]{:S(2)}, u32[]{:S(2)}) %collective-permute-start.2) | collective-permute-done | bytes 65568 | tf_op jit(solution)/shard_map/ppermute | solution.py:276
  24.9 0.6 shard_map.85
  25.5 0.6 collective-permute-start.4
  26.1 1.0 %collective-permute-done.4.got_ref.refs_1_ = bf16[4,8,16,128]{3,2,1,0:T(8,128)(2,1)S(1)} collective-permute-done((bf16[4,8,16,128]{3,2,1,0:T(8,128)(2,1)S(1)}, bf16[4,8,16,128]{3,2,1,0:T(8,128)(2,1)S(1)}, u32[]{:S(2)}, u32[]{:S(2)}) %collective-permute-start.4) | collective-permute-done | bytes 131104 | tf_op jit(solution)/shard_map/ppermute | solution.py:276
  27.1 1.8 %collective-permute-start.5 = (bf16[2,8,16,128]{3,2,1,0:T(8,128)(2,1)S(1)}, bf16[2,8,16,128]{3,2,1,0:T(8,128)(2,1)S(1)}, u32[]{:S(2)}, u32[]{:S(2)}) collective-permute-start(bf16[2,8,16,128]{3,2,1,0:T(8,128)(2,1)S(1)} %get-tuple-element.45), channel_id=1, source_target_pairs={{0,5},{1,4},{2,7},{3,6},{4,1},{5,0},{6,3},{7,2},{8,13},{9,12},{10,... | collective-permute-start | bytes 196616 | tf_op jit(solution)/shard_map/ppermute | solution.py:276
  28.8 0.9 %collective-permute-start.6 = (bf16[2,8,16,128]{3,2,1,0:T(8,128)(2,1)S(1)}, bf16[2,8,16,128]{3,2,1,0:T(8,128)(2,1)S(1)}, u32[]{:S(2)}, u32[]{:S(2)}) collective-permute-start(bf16[2,8,16,128]{3,2,1,0:T(8,128)(2,1)S(1)} %get-tuple-element.46), channel_id=1, source_target_pairs={{0,4},{1,5},{2,6},{3,7},{4,0},{5,1},{6,2},{7,3},{8,12},{9,13},{10,... | collective-permute-start | bytes 196616 | tf_op jit(solution)/shard_map/ppermute | solution.py:276
  29.7 0.9 %collective-permute-start.7 = (bf16[2,8,16,128]{3,2,1,0:T(8,128)(2,1)S(1)}, bf16[2,8,16,128]{3,2,1,0:T(8,128)(2,1)S(1)}, u32[]{:S(2)}, u32[]{:S(2)}) collective-permute-start(bf16[2,8,16,128]{3,2,1,0:T(8,128)(2,1)S(1)} %get-tuple-element.47), channel_id=1, source_target_pairs={{0,1},{1,0},{2,3},{3,2},{4,5},{5,4},{6,7},{7,6},{8,9},{9,8},{10,11... | collective-permute-start | bytes 196616 | tf_op jit(solution)/shard_map/ppermute | solution.py:276
  30.9 1.7 %collective-permute-done.5.refs_2_ = bf16[2,8,16,128]{3,2,1,0:T(8,128)(2,1)S(1)} collective-permute-done((bf16[2,8,16,128]{3,2,1,0:T(8,128)(2,1)S(1)}, bf16[2,8,16,128]{3,2,1,0:T(8,128)(2,1)S(1)}, u32[]{:S(2)}, u32[]{:S(2)}) %collective-permute-start.5) | collective-permute-done | bytes 65568 | tf_op jit(solution)/shard_map/ppermute | solution.py:276
  32.6 0.7 %collective-permute-done.6.refs_3_ = bf16[2,8,16,128]{3,2,1,0:T(8,128)(2,1)S(1)} collective-permute-done((bf16[2,8,16,128]{3,2,1,0:T(8,128)(2,1)S(1)}, bf16[2,8,16,128]{3,2,1,0:T(8,128)(2,1)S(1)}, u32[]{:S(2)}, u32[]{:S(2)}) %collective-permute-start.6) | collective-permute-done | bytes 65568 | tf_op jit(solution)/shard_map/ppermute | solution.py:276
  33.4 0.6 collective-permute-done.7.refs_4_
  34.0 1.4 %shard_map.87 = (bf16[4,16,16,128]{3,2,1,0:T(8,128)(2,1)S(1)}, bf16[4,16,16,128]{3,2,1,0:T(8,128)(2,1)S(1)}, f32[128,1024]{1,0:T(8,128)S(1)}, bf16[128,1024]{1,0:T(8,128)(2,1)S(1)}) custom-call(f32[16,128]{1,0:T(8,128)S(1)} %get-tuple-element.33.live_ref, bf16[128,512]{1,0:T(8,128)(2,1)S(1)} %get-tuple-element.34.weights, bf16[128,128]{1,0:T(8,128)(2,1)S(1)} %copy-done.2, ...), custom_call_target="tpu_custom_call" | custom-call | bytes 2990080 | tf_op jit(solution)/shard_map/pallas_call | solution.py:252
  35.5 1.5 %collective-permute-done.8.got_ref.refs_1_ = bf16[4,16,16,128]{3,2,1,0:T(8,128)(2,1)S(1)} collective-permute-done((bf16[4,16,16,128]{3,2,1,0:T(8,128)(2,1)S(1)}, bf16[4,16,16,128]{3,2,1,0:T(8,128)(2,1)S(1)}, u32[]{:S(2)}, u32[]{:S(2)}) %collective-permute-start.8) | collective-permute-done | bytes 262176 | tf_op jit(solution)/shard_map/ppermute | solution.py:276
  37.0 2.1 %collective-permute-start.9 = (bf16[2,16,16,128]{3,2,1,0:T(8,128)(2,1)S(1)}, bf16[2,16,16,128]{3,2,1,0:T(8,128)(2,1)S(1)}, u32[]{:S(2)}, u32[]{:S(2)}) collective-permute-start(bf16[2,16,16,128]{3,2,1,0:T(8,128)(2,1)S(1)} %get-tuple-element.51), channel_id=1, source_target_pairs={{0,5},{1,4},{2,7},{3,6},{4,1},{5,0},{6,3},{7,2},{8,13},{9,12},{10,... | collective-permute-start | bytes 393224 | tf_op jit(solution)/shard_map/ppermute | solution.py:276
  39.5 1.1 %collective-permute-start.11 = (bf16[2,16,16,128]{3,2,1,0:T(8,128)(2,1)S(1)}, bf16[2,16,16,128]{3,2,1,0:T(8,128)(2,1)S(1)}, u32[]{:S(2)}, u32[]{:S(2)}) collective-permute-start(bf16[2,16,16,128]{3,2,1,0:T(8,128)(2,1)S(1)} %get-tuple-element.53), channel_id=1, source_target_pairs={{0,1},{1,0},{2,3},{3,2},{4,5},{5,4},{6,7},{7,6},{8,9},{9,8},{10,11... | collective-permute-start | bytes 393224 | tf_op jit(solution)/shard_map/ppermute | solution.py:276
  40.9 3.5 %collective-permute-done.9.refs_2_ = bf16[2,16,16,128]{3,2,1,0:T(8,128)(2,1)S(1)} collective-permute-done((bf16[2,16,16,128]{3,2,1,0:T(8,128)(2,1)S(1)}, bf16[2,16,16,128]{3,2,1,0:T(8,128)(2,1)S(1)}, u32[]{:S(2)}, u32[]{:S(2)}) %collective-permute-start.9) | collective-permute-done | bytes 131104 | tf_op jit(solution)/shard_map/ppermute | solution.py:276
  44.3 1.5 %collective-permute-done.10.refs_3_ = bf16[2,16,16,128]{3,2,1,0:T(8,128)(2,1)S(1)} collective-permute-done((bf16[2,16,16,128]{3,2,1,0:T(8,128)(2,1)S(1)}, bf16[2,16,16,128]{3,2,1,0:T(8,128)(2,1)S(1)}, u32[]{:S(2)}, u32[]{:S(2)}) %collective-permute-start.10) | collective-permute-done | bytes 131104 | tf_op jit(solution)/shard_map/ppermute | solution.py:276
  46.8 18.6 %all_to_all.10.recv_ref = bf16[16,8,16,128]{3,2,1,0:T(8,128)(2,1)S(1)} all-to-all(bf16[16,8,16,128]{3,2,1,0:T(8,128)(2,1)S(1)} %shard_map.90), channel_id=1, replica_groups=mesh['groups'=2,'row'=8,'col'=2,'sub'=1] {'row','col'}, dimensions={0} | all-to-all | bytes 1048576 | tf_op jit(solution)/shard_map/all_to_all | solution.py:320
  65.5 1.5 %shard_map.91 = f32[1024,128]{1,0:T(8,128)} custom-call(bf16[16,8,16,128]{3,2,1,0:T(8,128)(2,1)S(1)} %all_to_all.10.recv_ref, f32[128,1024]{1,0:T(8,128)S(1)} %get-tuple-element.59.middle_ref, f32[128,1024]{1,0:T(8,128)S(1)} %shard_map.88.gating_ref, bf16[128,128]{1,0:T(8,128)(2,1)S(1)} %copy-done), custom_call_target="tpu_custom_call" | custom-call | bytes 2129920 | tf_op jit(solution)/shard_map/pallas_call | solution.py:252
  (21 shorter events, 2.8 us)
Async XLA Ops:
  3.0 21.9 %all-to-all-start = ((bf16[16,8,16,128]{3,2,1,0:T(8,128)(2,1)}), bf16[16,8,16,128]{3,2,1,0:T(8,128)(2,1)S(1)}, u32[]{:S(2)}, u32[]{:S(2)}) async-start(bf16[16,8,16,128]{3,2,1,0:T(8,128)(2,1)} %get-tuple-element.37), calls=%async_computation | async-start | bytes 1048576 | tf_op jit(solution)/shard_map/all_to_all | solution.py:307
  10.4 1.4 %collective-permute-start = (bf16[4,8,16,128]{3,2,1,0:T(8,128)(2,1)S(1)}, bf16[4,8,16,128]{3,2,1,0:T(8,128)(2,1)S(1)}, u32[]{:S(2)}, u32[]{:S(2)}) collective-permute-start(bf16[4,8,16,128]{3,2,1,0:T(8,128)(2,1)S(1)} %get-tuple-element.39), channel_id=1, source_target_pairs={{0,2},{1,3},{2,0},{3,1},{4,6},{5,7},{6,4},{7,5},{8,10},{9,11},{10,... | collective-permute-start | bytes 393224 | tf_op jit(solution)/shard_map/ppermute | solution.py:276
  11.8 11.4 %collective-permute-start.1 = (bf16[2,8,16,128]{3,2,1,0:T(8,128)(2,1)S(1)}, bf16[2,8,16,128]{3,2,1,0:T(8,128)(2,1)S(1)}, u32[]{:S(2)}, u32[]{:S(2)}) collective-permute-start(bf16[2,8,16,128]{3,2,1,0:T(8,128)(2,1)S(1)} %get-tuple-element.40), channel_id=1, source_target_pairs={{0,5},{1,4},{2,7},{3,6},{4,1},{5,0},{6,3},{7,2},{8,13},{9,12},{10,... | collective-permute-start | bytes 196616 | tf_op jit(solution)/shard_map/ppermute | solution.py:276
  14.6 10.1 %collective-permute-start.2 = (bf16[2,8,16,128]{3,2,1,0:T(8,128)(2,1)S(1)}, bf16[2,8,16,128]{3,2,1,0:T(8,128)(2,1)S(1)}, u32[]{:S(2)}, u32[]{:S(2)}) collective-permute-start(bf16[2,8,16,128]{3,2,1,0:T(8,128)(2,1)S(1)} %get-tuple-element.41), channel_id=1, source_target_pairs={{0,4},{1,5},{2,6},{3,7},{4,0},{5,1},{6,2},{7,3},{8,12},{9,13},{10,... | collective-permute-start | bytes 196616 | tf_op jit(solution)/shard_map/ppermute | solution.py:276
  15.2 9.5 %collective-permute-start.3 = (bf16[2,8,16,128]{3,2,1,0:T(8,128)(2,1)S(1)}, bf16[2,8,16,128]{3,2,1,0:T(8,128)(2,1)S(1)}, u32[]{:S(2)}, u32[]{:S(2)}) collective-permute-start(bf16[2,8,16,128]{3,2,1,0:T(8,128)(2,1)S(1)} %get-tuple-element.42), channel_id=1, source_target_pairs={{0,1},{1,0},{2,3},{3,2},{4,5},{5,4},{6,7},{7,6},{8,9},{9,8},{10,11... | collective-permute-start | bytes 196616 | tf_op jit(solution)/shard_map/ppermute | solution.py:276
  25.5 1.6 %collective-permute-start.4 = (bf16[4,8,16,128]{3,2,1,0:T(8,128)(2,1)S(1)}, bf16[4,8,16,128]{3,2,1,0:T(8,128)(2,1)S(1)}, u32[]{:S(2)}, u32[]{:S(2)}) collective-permute-start(bf16[4,8,16,128]{3,2,1,0:T(8,128)(2,1)S(1)} %get-tuple-element.44), channel_id=1, source_target_pairs={{0,2},{1,3},{2,0},{3,1},{4,6},{5,7},{6,4},{7,5},{8,10},{9,11},{10,... | collective-permute-start | bytes 393224 | tf_op jit(solution)/shard_map/ppermute | solution.py:276
  27.1 3.6 %copy-start.1 = (bf16[128,128]{1,0:T(8,128)(2,1)S(1)}, bf16[128,128]{1,0:T(8,128)(2,1)}, u32[]{:S(2)}) copy-start(bf16[128,128]{1,0:T(8,128)(2,1)} %gate_ref.2) | copy-start | bytes 98308
  27.1 5.6 %collective-permute-start.5 = (bf16[2,8,16,128]{3,2,1,0:T(8,128)(2,1)S(1)}, bf16[2,8,16,128]{3,2,1,0:T(8,128)(2,1)S(1)}, u32[]{:S(2)}, u32[]{:S(2)}) collective-permute-start(bf16[2,8,16,128]{3,2,1,0:T(8,128)(2,1)S(1)} %get-tuple-element.45), channel_id=1, source_target_pairs={{0,5},{1,4},{2,7},{3,6},{4,1},{5,0},{6,3},{7,2},{8,13},{9,12},{10,... | collective-permute-start | bytes 196616 | tf_op jit(solution)/shard_map/ppermute | solution.py:276
  28.8 4.5 %collective-permute-start.6 = (bf16[2,8,16,128]{3,2,1,0:T(8,128)(2,1)S(1)}, bf16[2,8,16,128]{3,2,1,0:T(8,128)(2,1)S(1)}, u32[]{:S(2)}, u32[]{:S(2)}) collective-permute-start(bf16[2,8,16,128]{3,2,1,0:T(8,128)(2,1)S(1)} %get-tuple-element.46), channel_id=1, source_target_pairs={{0,4},{1,5},{2,6},{3,7},{4,0},{5,1},{6,2},{7,3},{8,12},{9,13},{10,... | collective-permute-start | bytes 196616 | tf_op jit(solution)/shard_map/ppermute | solution.py:276
  29.7 4.3 %collective-permute-start.7 = (bf16[2,8,16,128]{3,2,1,0:T(8,128)(2,1)S(1)}, bf16[2,8,16,128]{3,2,1,0:T(8,128)(2,1)S(1)}, u32[]{:S(2)}, u32[]{:S(2)}) collective-permute-start(bf16[2,8,16,128]{3,2,1,0:T(8,128)(2,1)S(1)} %get-tuple-element.47), channel_id=1, source_target_pairs={{0,1},{1,0},{2,3},{3,2},{4,5},{5,4},{6,7},{7,6},{8,9},{9,8},{10,11... | collective-permute-start | bytes 196616 | tf_op jit(solution)/shard_map/ppermute | solution.py:276
  30.6 3.3 %copy-start.2 = (bf16[128,128]{1,0:T(8,128)(2,1)S(1)}, bf16[128,128]{1,0:T(8,128)(2,1)}, u32[]{:S(2)}) copy-start(bf16[128,128]{1,0:T(8,128)(2,1)} %final_ref.2) | copy-start | bytes 98308
  35.4 1.6 %collective-permute-start.8 = (bf16[4,16,16,128]{3,2,1,0:T(8,128)(2,1)S(1)}, bf16[4,16,16,128]{3,2,1,0:T(8,128)(2,1)S(1)}, u32[]{:S(2)}, u32[]{:S(2)}) collective-permute-start(bf16[4,16,16,128]{3,2,1,0:T(8,128)(2,1)S(1)} %get-tuple-element.50), channel_id=1, source_target_pairs={{0,2},{1,3},{2,0},{3,1},{4,6},{5,7},{6,4},{7,5},{8,10},{9,11},{10,... | collective-permute-start | bytes 786440 | tf_op jit(solution)/shard_map/ppermute | solution.py:276
  37.0 3.6 %copy-start.3 = (bf16[128,128]{1,0:T(8,128)(2,1)S(1)}, bf16[128,128]{1,0:T(8,128)(2,1)}, u32[]{:S(2)}) copy-start(bf16[128,128]{1,0:T(8,128)(2,1)} %gate_ref.3) | copy-start | bytes 98308
  37.0 7.3 %collective-permute-start.9 = (bf16[2,16,16,128]{3,2,1,0:T(8,128)(2,1)S(1)}, bf16[2,16,16,128]{3,2,1,0:T(8,128)(2,1)S(1)}, u32[]{:S(2)}, u32[]{:S(2)}) collective-permute-start(bf16[2,16,16,128]{3,2,1,0:T(8,128)(2,1)S(1)} %get-tuple-element.51), channel_id=1, source_target_pairs={{0,5},{1,4},{2,7},{3,6},{4,1},{5,0},{6,3},{7,2},{8,13},{9,12},{10,... | collective-permute-start | bytes 393224 | tf_op jit(solution)/shard_map/ppermute | solution.py:276
  39.1 6.7 %collective-permute-start.10 = (bf16[2,16,16,128]{3,2,1,0:T(8,128)(2,1)S(1)}, bf16[2,16,16,128]{3,2,1,0:T(8,128)(2,1)S(1)}, u32[]{:S(2)}, u32[]{:S(2)}) collective-permute-start(bf16[2,16,16,128]{3,2,1,0:T(8,128)(2,1)S(1)} %get-tuple-element.52), channel_id=1, source_target_pairs={{0,4},{1,5},{2,6},{3,7},{4,0},{5,1},{6,2},{7,3},{8,12},{9,13},{10,... | collective-permute-start | bytes 393224 | tf_op jit(solution)/shard_map/ppermute | solution.py:276
  39.5 6.8 %collective-permute-start.11 = (bf16[2,16,16,128]{3,2,1,0:T(8,128)(2,1)S(1)}, bf16[2,16,16,128]{3,2,1,0:T(8,128)(2,1)S(1)}, u32[]{:S(2)}, u32[]{:S(2)}) collective-permute-start(bf16[2,16,16,128]{3,2,1,0:T(8,128)(2,1)S(1)} %get-tuple-element.53), channel_id=1, source_target_pairs={{0,1},{1,0},{2,3},{3,2},{4,5},{5,4},{6,7},{7,6},{8,9},{9,8},{10,11... | collective-permute-start | bytes 393224 | tf_op jit(solution)/shard_map/ppermute | solution.py:276
  46.8 18.7 %copy-start = (bf16[128,128]{1,0:T(8,128)(2,1)S(1)}, bf16[128,128]{1,0:T(8,128)(2,1)}, u32[]{:S(2)}) copy-start(bf16[128,128]{1,0:T(8,128)(2,1)} %final_ref.3) | copy-start | bytes 98308

commit v6 on v5

--- a/solution.py
+++ b/solution.py
@@ -13,7 +13,8 @@
 CHUNK = 256
 NEAR = 8
 SIBLING = 2
-STEPS = (0, 5, 4, 1)
+NEAR_STEPS = (0, 5, 4, 1)
+ALL_STEPS = (0, 13, 12, 5, 9, 8, 4, 1)
 EPS = 1e-05
 
 
@@ -49,12 +50,6 @@
     row_live = jnp.sum(jnp.where(mine, wide, 0.0), axis=1, keepdims=True)
     col_live = jnp.where(lane // cols == lax.axis_index("col"), wide, pltpu.roll(wide, cols, 1))
     return row_live * col_live
-
-
-def panel(normed, weights, which):
-    hidden = weights.shape[1] // 4
-    linear = product(weights[:, 2 * which * hidden : 2 * (which + 1) * hidden], normed)
-    return jax.nn.sigmoid(linear[hidden:]) * linear[:hidden]
 
 
 def panels(normed, weights):
@@ -105,30 +100,64 @@
     return started
 
 
-def near_index():
-    return (lax.axis_index("row") * 2 + lax.axis_index("col")) % NEAR
-
-
-def hand_out(by_near, keep_ref, give_ref):
-    me = near_index()
-    for n, step in enumerate(STEPS):
-        keep_ref[n] = by_near[me ^ step]
-        give_ref[n] = by_near[me ^ step ^ SIBLING]
-
-
-def take_in(refs, by_near):
+def own_index():
+    return lax.axis_index("row") * 2 + lax.axis_index("col")
+
+
+def hand_out(tiles, steps, keep_ref, give_ref):
+    me = own_index()
+    count = tiles.shape[0]
+    for n, step in enumerate(steps):
+        keep_ref[n] = tiles[(me ^ step) % count]
+        give_ref[n] = tiles[(me ^ step ^ SIBLING) % count]
+
+
+def forward_kernel(keep_ref, got_ref, *out_refs):
+    for n, out_ref in enumerate(out_refs):
+        out_ref[0] = keep_ref[n + 1]
+        out_ref[1] = got_ref[n + 1]
+
+
+def take_in(refs, steps, tiles):
     keep_ref, got_ref, *moved_refs = refs
-    me = near_index()
-    by_near[me] = keep_ref[0]
-    by_near[me ^ SIBLING] = got_ref[0]
-    for step, moved_ref in zip(STEPS[1:], moved_refs):
-        by_near[me ^ step] = moved_ref[0]
-        by_near[me ^ step ^ SIBLING] = moved_ref[1]
+    me = own_index()
+    count = tiles.shape[0]
+    tiles[me % count] = keep_ref[0]
+    tiles[(me ^ SIBLING) % count] = got_ref[0]
+    for step, moved_ref in zip(steps[1:], moved_refs):
+        tiles[(me ^ step) % count] = moved_ref[0]
+        tiles[(me ^ step ^ SIBLING) % count] = moved_ref[1]
+
+
+def forward_panels_kernel(keep_ref, got_ref, *out_refs):
+    for step, out_ref in zip(ALL_STEPS[1:], out_refs):
+        n = NEAR_STEPS.index(step % NEAR)
+        for core, ref in enumerate((keep_ref, got_ref)):
+            if step < NEAR:
+                out_ref[core, 0] = ref[0, n]
+                out_ref[core, 1] = ref[1, n]
+            else:
+                out_ref[core] = ref[1, n]
+
+
+def take_in_panels(refs, a_tiles, b_tiles):
+    keep_ref, got_ref, *moved_refs = refs
+    me = own_index()
+    for step, ref in ((0, keep_ref), (SIBLING, got_ref)):
+        a_tiles[(me ^ step) % NEAR] = ref[0, 0]
+        b_tiles[me ^ step] = ref[1, 0]
+    for step, moved_ref in zip(ALL_STEPS[1:], moved_refs):
+        for core, source in enumerate((me ^ step, me ^ step ^ SIBLING)):
+            if step < NEAR:
+                a_tiles[source % NEAR] = moved_ref[core, 0]
+                b_tiles[source] = moved_ref[core, 1]
+            else:
+                b_tiles[source] = moved_ref[core]
 
 
 def first_kernel(
-    rows, cols, pair_hbm, mask_hbm, proj_hbm, proj2_hbm, b_hbm, keep_ref, give_ref, pair_t_ref, normed_ref, live_ref, weights2,
-    pair_ref, mask_ref, proj_ref, proj2_ref, weights, wide, b_tiles, by_near, done,
+    rows, cols, pair_hbm, mask_hbm, proj_hbm, proj2_hbm, keep_ref, give_ref, pair_t_ref, normed_ref, live_ref, weights2,
+    pair_ref, mask_ref, proj_ref, proj2_ref, weights, wide, by_near, done,
 ):
     chunks = [slice(at, at + CHUNK) for at in range(0, rows * cols, CHUNK)]
     whole = [(mask_hbm, mask_ref), (proj_hbm, proj_ref), (proj2_hbm, proj2_ref)]
@@ -145,26 +174,15 @@
     pair_t_ref[...] = pair
     normed = over_channels(pair).astype(BF16)
     normed_ref[...] = normed
-    b = panel(normed, weights, 1)
-    half = b.shape[0] // 2
-    b_tiles[...] = paired(b[:half], b[half:], live, cols).reshape(b_tiles.shape)
-    leaving = copies([(b_tiles, b_hbm.at[:NEAR]), (b_tiles, b_hbm.at[NEAR:])], done)
-    a = panel(normed, weights, 0)
-    by_near[...] = paired(a[:half], a[half:], live, cols).reshape(by_near.shape)
-    hand_out(by_near, keep_ref, give_ref)
-    for copy in leaving:
-        copy.wait()
-
-
-def forward_kernel(keep_ref, got_ref, *out_refs):
-    for n, out_ref in enumerate(out_refs):
-        out_ref[0] = keep_ref[n + 1]
-        out_ref[1] = got_ref[n + 1]
+    for n, values in enumerate(panels(normed, weights)):
+        half = values.shape[0] // 2
+        by_near[...] = paired(values[:half], values[half:], live, cols).reshape(by_near.shape)
+        hand_out(by_near, NEAR_STEPS, keep_ref.at[n], give_ref.at[n])
 
 
 def middle_kernel(rows, cols, live_ref, weights, final_ref, pair_t_ref, gating_ref, *refs):
     *came_refs, keep_ref, give_ref, middle_ref, normed_ref, tiles, came, by_near = refs
-    take_in(came_refs, came)
+    take_in(came_refs, NEAR_STEPS, came)
     middle = pair_t_ref[...] + gating_ref[...] * projected(came, final_ref, tiles, rows, cols)
     middle_ref[...] = middle
     normed = over_channels(middle).astype(BF16)
@@ -177,11 +195,13 @@
     for d in range(devices):
         by_near[d, :half] = by_hidden[d * half : (d + 1) * half]
         by_near[d, half:] = by_hidden[hidden // 2 + d * half : hidden // 2 + (d + 1) * half]
-    hand_out(by_near, keep_ref, give_ref)
-
-
-def last_kernel(rows, cols, recv_ref, middle_ref, gating_ref, final_ref, out_hbm, tiles, out_ref, done):
-    change = projected(recv_ref, final_ref, tiles, rows, cols)
+    hand_out(by_near, NEAR_STEPS, keep_ref, give_ref)
+
+
+def last_kernel(rows, cols, middle_ref, gating_ref, final_ref, *refs):
+    *came_refs, out_hbm, tiles, came, out_ref, done = refs
+    take_in(came_refs, ALL_STEPS, came)
+    change = projected(came, final_ref, tiles, rows, cols)
     leaving = []
     for n in range(rows * cols // CHUNK):
         at = slice(n * CHUNK, (n + 1) * CHUNK)
@@ -208,9 +228,9 @@
         msg_ref[2 * r + 1, q] = right[r * rows : (r + 1) * rows].astype(BF16)
 
 
-def outgoing_kernel(cols, b_ref, *refs):
-    *came_refs, keep_ref, give_ref, a_ref, msg_ref = refs
-    take_in(came_refs, a_ref)
+def outgoing_kernel(cols, *refs):
+    *came_refs, keep_ref, give_ref, a_ref, b_ref, msg_ref = refs
+    take_in_panels(came_refs, a_ref, b_ref)
     for q in range(msg_ref.shape[1]):
         even, odd = both(a_ref, q)
         low = low_of(even, cols)
@@ -222,12 +242,12 @@
         y = lax.dot_general(a2, b2, (((1,), (1,)), ((), ())), preferred_element_type=F32)
         low = low_of(x, cols)
         put(jnp.where(low, x, pltpu.roll(y, cols, 1)), jnp.where(low, pltpu.roll(x, cols, 1), y), msg_ref, q)
-    hand_out(msg_ref, keep_ref, give_ref)
+    hand_out(msg_ref, NEAR_STEPS, keep_ref, give_ref)
 
 
 def incoming_kernel(cols, *refs):
-    *came_refs, msg_ref, recv_ref = refs
-    take_in(came_refs, recv_ref)
+    *came_refs, keep_ref, give_ref, recv_ref, msg_ref = refs
+    take_in(came_refs, NEAR_STEPS, recv_ref)
     half = msg_ref.shape[1]
 
     def mixed(e):
@@ -240,6 +260,7 @@
         x, y = mixed(q), mixed(q + half)
         low = low_of(x, cols)
         put(jnp.where(low, pltpu.roll(x, cols, 1), y), jnp.where(low, x, pltpu.roll(y, cols, 1)), msg_ref, q)
+    hand_out(msg_ref, ALL_STEPS, keep_ref, give_ref)
 
 
 def call(kernel, out_shape, scratch=(), far=(0, 0), flops=0, transcendentals=0):
@@ -270,21 +291,27 @@
     positions = rows * cols
     shape = jax.ShapeDtypeStruct
     axes = ("row", "col")
-    exchange = functools.partial(lax.all_to_all, axis_name=axes, split_axis=0, concat_axis=0, tiled=True)
 
     def swap(values, step):
         return lax.ppermute(values, axes, [(d, d ^ step) for d in range(devices)])
 
-    def within_half(keep, give):
+    def exchange(keep, give, steps):
         got = swap(give, SIBLING)
-        moving = call(forward_kernel, (shape((2,) + keep.shape[1:], BF16),) * (len(STEPS) - 1))(keep, got)
-        return (keep, got, *(swap(block, step) for block, step in zip(moving, STEPS[1:])))
+        moving = call(forward_kernel, [shape((2,) + keep.shape[1:], BF16)] * (len(steps) - 1))(keep, got)
+        return (keep, got, *(swap(block, step) for block, step in zip(moving, steps[1:])))
+
+    def exchange_panels(keep, give):
+        got = swap(give, SIBLING)
+        one = keep.shape[2:]
+        outs = [shape((2, 2) + one if step < NEAR else (2,) + one, BF16) for step in ALL_STEPS[1:]]
+        moving = call(forward_panels_kernel, outs)(keep, got)
+        return (keep, got, *(swap(block, step) for block, step in zip(moving, ALL_STEPS[1:])))
 
     def messages(targets, tiles):
         return shape((targets, tiles, rows, LANES), BF16)
 
-    def near_tiles(tiles):
-        return pltpu.VMEM(messages(NEAR, tiles).shape, BF16)
+    def scratch_tiles(targets, tiles):
+        return pltpu.VMEM(messages(targets, tiles).shape, BF16)
 
     plane = shape((channels, positions), F32)
     half_plane = shape((channels, positions), BF16)
@@ -294,31 +321,40 @@
     weights = (channels, 4 * hidden)
     chunks = positions // CHUNK
     pairs = hidden // NEAR // 2
-    steps = (messages(len(STEPS), pairs),) * 2
-    wide_steps = (messages(len(STEPS), 2 * pairs),) * 2
+    panel_steps = (shape((2, len(NEAR_STEPS), pairs, rows, LANES), BF16),) * 2
+    near_steps = (messages(len(NEAR_STEPS), pairs),) * 2
+    wide_near_steps = (messages(len(NEAR_STEPS), 2 * pairs),) * 2
+    all_steps = (messages(len(ALL_STEPS), pairs),) * 2
     gate = call(gate_kernel, [plane], flops=2 * channels * channels * positions, transcendentals=channels * positions)
 
     far = (pair.reshape(positions, channels), mask, out_proj.reshape(-1, hidden), in_proj.reshape(-1, hidden))
-    outs = (messages(devices, pairs), *steps, plane, half_plane, shape((rows, LANES), F32), shape(weights, BF16))
+    outs = (*panel_steps, plane, half_plane, shape((rows, LANES), F32), shape(weights, BF16))
     scratch = [pltpu.VMEM(a.shape, a.dtype) for a in far]
     scratch += [pltpu.VMEM(weights, BF16), pltpu.VMEM((4 * channels, hidden), F32)]
-    scratch += [near_tiles(pairs), near_tiles(pairs), pltpu.SemaphoreType.DMA((chunks + 3,))]
-    b, keep, give, pair_t, normed, live, weights = call(functools.partial(first_kernel, rows, cols), outs, scratch, (4, 1))(*far)
-    b = exchange(b)
-    a = within_half(keep, give)
-    (gating,) = gate(normed, out_gate)
-    keep, give = call(functools.partial(outgoing_kernel, cols), steps, [near_tiles(pairs)] * 2)(b, *a)
-    scratch = [tiles, near_tiles(pairs), near_tiles(2 * pairs)]
-    keep, give, middle, normed = call(functools.partial(middle_kernel, rows, cols), (*wide_steps, plane, half_plane), scratch)(
-        live, weights, out_final, pair_t, gating, *within_half(keep, give)
-    )
-    came = within_half(keep, give)
+    scratch += [scratch_tiles(NEAR, pairs), pltpu.SemaphoreType.DMA((chunks + 3,))]
+    keep, give, pair_t, normed, live, weights = call(functools.partial(first_kernel, rows, cols), outs, scratch, (4, 0))(*far)
+    came = exchange_panels(keep, give)
+    gating, came = lax.optimization_barrier((gate(normed, out_gate)[0], came))
+
+    scratch = [scratch_tiles(NEAR, pairs), scratch_tiles(devices, pairs), scratch_tiles(NEAR, pairs)]
+    keep, give = call(functools.partial(outgoing_kernel, cols), near_steps, scratch)(*came)
+    came = exchange(keep, give, NEAR_STEPS)
+
+    scratch = [tiles, scratch_tiles(NEAR, pairs), scratch_tiles(NEAR, 2 * pairs)]
+    outs = (*wide_near_steps, plane, half_plane)
+    keep, give, middle, normed = call(functools.partial(middle_kernel, rows, cols), outs, scratch)(
+        live, weights, out_final, pair_t, gating, *came
+    )
+    came = exchange(keep, give, NEAR_STEPS)
     gating, came = lax.optimization_barrier((gate(normed, in_gate)[0], came))
-    (mixed,) = call(functools.partial(incoming_kernel, cols), [messages(devices, pairs)], [near_tiles(2 * pairs)])(*came)
-    scratch = [tiles, by_position, pltpu.SemaphoreType.DMA((chunks,))]
-    (out,) = call(functools.partial(last_kernel, rows, cols), [shape((positions, channels), F32)], scratch, (0, 1))(
-        exchange(mixed), middle, gating, in_final
-    )
+
+    scratch = [scratch_tiles(NEAR, 2 * pairs), scratch_tiles(devices, pairs)]
+    keep, give = call(functools.partial(incoming_kernel, cols), all_steps, scratch)(*came)
+    came = exchange(keep, give, ALL_STEPS)
+
+    scratch = [tiles, scratch_tiles(devices, pairs), by_position, pltpu.SemaphoreType.DMA((chunks,))]
+    outs = [shape((positions, channels), F32)]
+    (out,) = call(functools.partial(last_kernel, rows, cols), outs, scratch, (0, 1))(middle, gating, in_final, *came)
     return out.reshape(rows, cols, channels)
 
 

time: 67.4 us -> 63.9 us (0.948)
  blocking collectives: 18.6 us -> 0 us
  starting transfers between devices: 19.1 us -> 32.3 us
  waiting for transfers between devices: 21.6 us -> 24.2 us
    ppermute x12 -> x24, starting transfers between devices: 11.7 us -> 32.3 us  [swap(): return lax.ppermute(values, axes, [(d, d ^ step) for d in range(devices)])]
    all_to_all x1 -> x0, blocking collectives: 18.6 us -> none  [by_channel(): exchange(mixed)]
    all_to_all x1 -> x0, starting transfers between devices: 7.37 us -> none  [by_channel(): b = exchange(b)]
    ppermute x12 -> x24, waiting for transfers between devices: 21.5 us -> 24.2 us  [swap(): return lax.ppermute(values, axes, [(d, d ^ step) for d in range(devices)])]
    pallas_call x10 -> x11, Pallas kernels: 7.52 us -> 7.08 us  [run(): pl.pallas_call(kernel, out_shape=tuple(out_shape), in_specs=[hbm] * far_a...]
  transfers between devices with their start and end apart: 13 -> 24, of which waited for: 12 -> 15; matrix products, arithmetic and copies ran while one was open for 0% -> 0% of each run, Pallas kernels for 1% -> 1%
where the time goes in v6:
time: 63.9 us; the launch traced here: 63.8 us
  starting transfers between devices  32.3 us (51%)
  waiting for transfers between devices  24.2 us (38%)
  Pallas kernels  7.08 us (11%)
    ppermute x24, starting transfers between devices, swap(): return lax.ppermute(values, axes, [(d, d ^ step) for d in range(devices)])  32.3 us
    ppermute x24, waiting for transfers between devices, swap(): return lax.ppermute(values, axes, [(d, d ^ step) for d in range(devices)])  24.2 us
    pallas_call x11, Pallas kernels, run(): pl.pallas_call(kernel, out_shape=tuple(out_shape), in_specs=[hbm] * far_a...  7.08 us
  transfers between devices with their start and end apart: 24, of which 15 were waited for; matrix products, arithmetic and copies ran while one was open for 0% of the time, Pallas kernels for 1%

profile of v6, /device:TPU:0, one launch (start us, length us, event | category | flops | bytes accessed | tf_op | source)
XLA Modules:
  0.0 63.8 jit_solution(2127477557394786642)
XLA Ops:
  0.0 2.3 %shard_map.82 = (bf16[2,4,8,16,128]{4,3,2,1,0:T(8,128)(2,1)S(1)}, bf16[2,4,8,16,128]{4,3,2,1,0:T(8,128)(2,1)S(1)}, f32[128,1024]{1,0:T(8,128)S(1)}, bf16[128,102...) custom-call(f32[1024,128]{1,0:T(8,128)} %bitcast.5, s32[1,128]{1,0:T(1,128)} %bitcast.8, ...), custom_call_target="tpu_custom_call" | custom-call | bytes 2236928 | tf_op jit(solution)/shard_map/pallas_call | solution.py:273
  4.1 6.0 %collective-permute-start.1 = (bf16[2,8,16,128]{3,2,1,0:T(8,128)(2,1)S(1)}, bf16[2,8,16,128]{3,2,1,0:T(8,128)(2,1)S(1)}, u32[]{:S(2)}, u32[]{:S(2)}) collective-permute-start(bf16[2,8,16,128]{3,2,1,0:T(8,128)(2,1)S(1)} %get-tuple-element.61), channel_id=1, source_target_pairs={{0,13},{1,12},{2,15},{3,14},{4,9},{5,8},{6,11},{7,10},{8,5},{9,4},... | collective-permute-start | bytes 196616 | tf_op jit(solution)/shard_map/ppermute | solution.py:296
  10.3 1.9 %collective-permute-start.6 = (bf16[2,2,8,16,128]{4,3,2,1,0:T(8,128)(2,1)S(1)}, bf16[2,2,8,16,128]{4,3,2,1,0:T(8,128)(2,1)S(1)}, u32[]{:S(2)}, u32[]{:S(2)}) collective-permute-start(bf16[2,2,8,16,128]{4,3,2,1,0:T(8,128)(2,1)S(1)} %get-tuple-element.66), channel_id=1, source_target_pairs={{0,4},{1,5},{2,6},{3,7},{4,0},{5,1},{6,2},{7,3},{8,12},{9,13},{10,... | collective-permute-start | bytes 393224 | tf_op jit(solution)/shard_map/ppermute | solution.py:296
  12.1 1.6 %collective-permute-start.7 = (bf16[2,2,8,16,128]{4,3,2,1,0:T(8,128)(2,1)S(1)}, bf16[2,2,8,16,128]{4,3,2,1,0:T(8,128)(2,1)S(1)}, u32[]{:S(2)}, u32[]{:S(2)}) collective-permute-start(bf16[2,2,8,16,128]{4,3,2,1,0:T(8,128)(2,1)S(1)} %get-tuple-element.67), channel_id=1, source_target_pairs={{0,1},{1,0},{2,3},{3,2},{4,5},{5,4},{6,7},{7,6},{8,9},{9,8},{10,11... | collective-permute-start | bytes 393224 | tf_op jit(solution)/shard_map/ppermute | solution.py:296
  13.8 3.2 %collective-permute-start.4 = (bf16[2,8,16,128]{3,2,1,0:T(8,128)(2,1)S(1)}, bf16[2,8,16,128]{3,2,1,0:T(8,128)(2,1)S(1)}, u32[]{:S(2)}, u32[]{:S(2)}) collective-permute-start(bf16[2,8,16,128]{3,2,1,0:T(8,128)(2,1)S(1)} %get-tuple-element.64), channel_id=1, source_target_pairs={{0,9},{1,8},{2,11},{3,10},{4,13},{5,12},{6,15},{7,14},{8,1},{9,0},... | collective-permute-start | bytes 196616 | tf_op jit(solution)/shard_map/ppermute | solution.py:296
  17.6 3.3 %collective-permute-done.4.refs_5_ = bf16[2,8,16,128]{3,2,1,0:T(8,128)(2,1)S(1)} collective-permute-done((bf16[2,8,16,128]{3,2,1,0:T(8,128)(2,1)S(1)}, bf16[2,8,16,128]{3,2,1,0:T(8,128)(2,1)S(1)}, u32[]{:S(2)}, u32[]{:S(2)}) %collective-permute-start.4) | collective-permute-done | bytes 65568 | tf_op jit(solution)/shard_map/ppermute | solution.py:296
  21.0 3.4 %collective-permute-done.5.refs_6_ = bf16[2,8,16,128]{3,2,1,0:T(8,128)(2,1)S(1)} collective-permute-done((bf16[2,8,16,128]{3,2,1,0:T(8,128)(2,1)S(1)}, bf16[2,8,16,128]{3,2,1,0:T(8,128)(2,1)S(1)}, u32[]{:S(2)}, u32[]{:S(2)}) %collective-permute-start.5) | collective-permute-done | bytes 65568 | tf_op jit(solution)/shard_map/ppermute | solution.py:296
  25.0 1.3 %collective-permute-done.8.got_ref.refs_1_ = bf16[4,8,16,128]{3,2,1,0:T(8,128)(2,1)S(1)} collective-permute-done((bf16[4,8,16,128]{3,2,1,0:T(8,128)(2,1)S(1)}, bf16[4,8,16,128]{3,2,1,0:T(8,128)(2,1)S(1)}, u32[]{:S(2)}, u32[]{:S(2)}) %collective-permute-start.8) | collective-permute-done | bytes 131104 | tf_op jit(solution)/shard_map/ppermute | solution.py:296
  27.1 1.3 %collective-permute-start.10 = (bf16[2,8,16,128]{3,2,1,0:T(8,128)(2,1)S(1)}, bf16[2,8,16,128]{3,2,1,0:T(8,128)(2,1)S(1)}, u32[]{:S(2)}, u32[]{:S(2)}) collective-permute-start(bf16[2,8,16,128]{3,2,1,0:T(8,128)(2,1)S(1)} %get-tuple-element.81), channel_id=1, source_target_pairs={{0,4},{1,5},{2,6},{3,7},{4,0},{5,1},{6,2},{7,3},{8,12},{9,13},{10,... | collective-permute-start | bytes 196616 | tf_op jit(solution)/shard_map/ppermute | solution.py:296
  28.4 1.5 %collective-permute-start.11 = (bf16[2,8,16,128]{3,2,1,0:T(8,128)(2,1)S(1)}, bf16[2,8,16,128]{3,2,1,0:T(8,128)(2,1)S(1)}, u32[]{:S(2)}, u32[]{:S(2)}) collective-permute-start(bf16[2,8,16,128]{3,2,1,0:T(8,128)(2,1)S(1)} %get-tuple-element.82), channel_id=1, source_target_pairs={{0,1},{1,0},{2,3},{3,2},{4,5},{5,4},{6,7},{7,6},{8,9},{9,8},{10,11... | collective-permute-start | bytes 196616 | tf_op jit(solution)/shard_map/ppermute | solution.py:296
  29.9 2.3 %collective-permute-done.9.refs_2_ = bf16[2,8,16,128]{3,2,1,0:T(8,128)(2,1)S(1)} collective-permute-done((bf16[2,8,16,128]{3,2,1,0:T(8,128)(2,1)S(1)}, bf16[2,8,16,128]{3,2,1,0:T(8,128)(2,1)S(1)}, u32[]{:S(2)}, u32[]{:S(2)}) %collective-permute-start.9) | collective-permute-done | bytes 65568 | tf_op jit(solution)/shard_map/ppermute | solution.py:296
  32.9 1.4 %shard_map.87 = (bf16[4,16,16,128]{3,2,1,0:T(8,128)(2,1)S(1)}, bf16[4,16,16,128]{3,2,1,0:T(8,128)(2,1)S(1)}, f32[128,1024]{1,0:T(8,128)S(1)}, bf16[128,1024]{1,0:T(8,128)(2,1)S(1)}) custom-call(f32[16,128]{1,0:T(8,128)S(1)} %get-tuple-element.55.live_ref, bf16[128,512]{1,0:T(8,128)(2,1)S(1)} %get-tuple-element.56.weights, bf16[128,128]{1,0:T(8,128)(2,1)S(1)} %copy-done.2, ...), custom_call_target="tpu_custom_call" | custom-call | bytes 2990080 | tf_op jit(solution)/shard_map/pallas_call | solution.py:273
  34.4 1.5 %collective-permute-done.12.got_ref.refs_1_ = bf16[4,16,16,128]{3,2,1,0:T(8,128)(2,1)S(1)} collective-permute-done((bf16[4,16,16,128]{3,2,1,0:T(8,128)(2,1)S(1)}, bf16[4,16,16,128]{3,2,1,0:T(8,128)(2,1)S(1)}, u32[]{:S(2)}, u32[]{:S(2)}) %collective-permute-start.12) | collective-permute-done | bytes 262176 | tf_op jit(solution)/shard_map/ppermute | solution.py:296
  35.9 1.3 %collective-permute-start.13 = (bf16[2,16,16,128]{3,2,1,0:T(8,128)(2,1)S(1)}, bf16[2,16,16,128]{3,2,1,0:T(8,128)(2,1)S(1)}, u32[]{:S(2)}, u32[]{:S(2)}) collective-permute-start(bf16[2,16,16,128]{3,2,1,0:T(8,128)(2,1)S(1)} %get-tuple-element.87), channel_id=1, source_target_pairs={{0,5},{1,4},{2,7},{3,6},{4,1},{5,0},{6,3},{7,2},{8,13},{9,12},{10,... | collective-permute-start | bytes 393224 | tf_op jit(solution)/shard_map/ppermute | solution.py:296
  37.2 1.6 %collective-permute-start.14 = (bf16[2,16,16,128]{3,2,1,0:T(8,128)(2,1)S(1)}, bf16[2,16,16,128]{3,2,1,0:T(8,128)(2,1)S(1)}, u32[]{:S(2)}, u32[]{:S(2)}) collective-permute-start(bf16[2,16,16,128]{3,2,1,0:T(8,128)(2,1)S(1)} %get-tuple-element.88), channel_id=1, source_target_pairs={{0,4},{1,5},{2,6},{3,7},{4,0},{5,1},{6,2},{7,3},{8,12},{9,13},{10,... | collective-permute-start | bytes 393224 | tf_op jit(solution)/shard_map/ppermute | solution.py:296
  39.8 3.5 %collective-permute-done.13.refs_2_ = bf16[2,16,16,128]{3,2,1,0:T(8,128)(2,1)S(1)} collective-permute-done((bf16[2,16,16,128]{3,2,1,0:T(8,128)(2,1)S(1)}, bf16[2,16,16,128]{3,2,1,0:T(8,128)(2,1)S(1)}, u32[]{:S(2)}, u32[]{:S(2)}) %collective-permute-start.13) | collective-permute-done | bytes 131104 | tf_op jit(solution)/shard_map/ppermute | solution.py:296
  43.3 1.9 %collective-permute-done.14.refs_3_ = bf16[2,16,16,128]{3,2,1,0:T(8,128)(2,1)S(1)} collective-permute-done((bf16[2,16,16,128]{3,2,1,0:T(8,128)(2,1)S(1)}, bf16[2,16,16,128]{3,2,1,0:T(8,128)(2,1)S(1)}, u32[]{:S(2)}, u32[]{:S(2)}) %collective-permute-start.14) | collective-permute-done | bytes 131104 | tf_op jit(solution)/shard_map/ppermute | solution.py:296
  45.9 1.5 %collective-permute-done.16.got_ref.refs_1_ = bf16[8,8,16,128]{3,2,1,0:T(8,128)(2,1)S(1)} collective-permute-done((bf16[8,8,16,128]{3,2,1,0:T(8,128)(2,1)S(1)}, bf16[8,8,16,128]{3,2,1,0:T(8,128)(2,1)S(1)}, u32[]{:S(2)}, u32[]{:S(2)}) %collective-permute-start.16) | collective-permute-done | bytes 262176 | tf_op jit(solution)/shard_map/ppermute | solution.py:296
  47.4 2.9 %collective-permute-start.17 = (bf16[2,8,16,128]{3,2,1,0:T(8,128)(2,1)S(1)}, bf16[2,8,16,128]{3,2,1,0:T(8,128)(2,1)S(1)}, u32[]{:S(2)}, u32[]{:S(2)}) collective-permute-start(bf16[2,8,16,128]{3,2,1,0:T(8,128)(2,1)S(1)} %get-tuple-element.98), channel_id=1, source_target_pairs={{0,13},{1,12},{2,15},{3,14},{4,9},{5,8},{6,11},{7,10},{8,5},{9,4},... | collective-permute-start | bytes 196616 | tf_op jit(solution)/shard_map/ppermute | solution.py:296
  50.3 1.7 %collective-permute-start.18 = (bf16[2,8,16,128]{3,2,1,0:T(8,128)(2,1)S(1)}, bf16[2,8,16,128]{3,2,1,0:T(8,128)(2,1)S(1)}, u32[]{:S(2)}, u32[]{:S(2)}) collective-permute-start(bf16[2,8,16,128]{3,2,1,0:T(8,128)(2,1)S(1)} %get-tuple-element.99), channel_id=1, source_target_pairs={{0,12},{1,13},{2,14},{3,15},{4,8},{5,9},{6,10},{7,11},{8,4},{9,5},... | collective-permute-start | bytes 196616 | tf_op jit(solution)/shard_map/ppermute | solution.py:296
  52.1 3.6 %collective-permute-start.20 = (bf16[2,8,16,128]{3,2,1,0:T(8,128)(2,1)S(1)}, bf16[2,8,16,128]{3,2,1,0:T(8,128)(2,1)S(1)}, u32[]{:S(2)}, u32[]{:S(2)}) collective-permute-start(bf16[2,8,16,128]{3,2,1,0:T(8,128)(2,1)S(1)} %get-tuple-element.101), channel_id=1, source_target_pairs={{0,9},{1,8},{2,11},{3,10},{4,13},{5,12},{6,15},{7,14},{8,1},{9,0},... | collective-permute-start | bytes 196616 | tf_op jit(solution)/shard_map/ppermute | solution.py:296
  55.6 2.3 %collective-permute-start.22 = (bf16[2,8,16,128]{3,2,1,0:T(8,128)(2,1)S(1)}, bf16[2,8,16,128]{3,2,1,0:T(8,128)(2,1)S(1)}, u32[]{:S(2)}, u32[]{:S(2)}) collective-permute-start(bf16[2,8,16,128]{3,2,1,0:T(8,128)(2,1)S(1)} %get-tuple-element.103), channel_id=1, source_target_pairs={{0,4},{1,5},{2,6},{3,7},{4,0},{5,1},{6,2},{7,3},{8,12},{9,13},{10,... | collective-permute-start | bytes 196616 | tf_op jit(solution)/shard_map/ppermute | solution.py:296
  59.2 2.1 %collective-permute-done.20.refs_5_ = bf16[2,8,16,128]{3,2,1,0:T(8,128)(2,1)S(1)} collective-permute-done((bf16[2,8,16,128]{3,2,1,0:T(8,128)(2,1)S(1)}, bf16[2,8,16,128]{3,2,1,0:T(8,128)(2,1)S(1)}, u32[]{:S(2)}, u32[]{:S(2)}) %collective-permute-start.20) | collective-permute-done | bytes 65568 | tf_op jit(solution)/shard_map/ppermute | solution.py:296
  62.2 1.6 %shard_map.92 = f32[1024,128]{1,0:T(8,128)} custom-call(f32[128,1024]{1,0:T(8,128)S(1)} %get-tuple-element.83.middle_ref, f32[128,1024]{1,0:T(8,128)S(1)} %shard_map.88.gating_ref, bf16[128,128]{1,0:T(8,128)(2,1)S(1)} %copy-done, bf16[8,8,16,128]{3,2,1,0:T(8,128)(2,1)S(1)} %get-tuple-element.96.keep_ref.refs_0_, ...), custom_call_target="tpu_custom_call" | custom-call | bytes 2588672 | tf_op jit(solution)/shard_map/pallas_call | solution.py:273
  (43 shorter events, 8.8 us)
Async XLA Ops:
  2.3 1.7 %collective-permute-start = (bf16[2,4,8,16,128]{4,3,2,1,0:T(8,128)(2,1)S(1)}, bf16[2,4,8,16,128]{4,3,2,1,0:T(8,128)(2,1)S(1)}, u32[]{:S(2)}, u32[]{:S(2)}) collective-permute-start(bf16[2,4,8,16,128]{4,3,2,1,0:T(8,128)(2,1)S(1)} %get-tuple-element.60), channel_id=1, source_target_pairs={{0,2},{1,3},{2,0},{3,1},{4,6},{5,7},{6,4},{7,5},{8,10},{9,11},{10,... | collective-permute-start | bytes 786440 | tf_op jit(solution)/shard_map/ppermute | solution.py:296
  4.1 9.7 %collective-permute-start.1 = (bf16[2,8,16,128]{3,2,1,0:T(8,128)(2,1)S(1)}, bf16[2,8,16,128]{3,2,1,0:T(8,128)(2,1)S(1)}, u32[]{:S(2)}, u32[]{:S(2)}) collective-permute-start(bf16[2,8,16,128]{3,2,1,0:T(8,128)(2,1)S(1)} %get-tuple-element.61), channel_id=1, source_target_pairs={{0,13},{1,12},{2,15},{3,14},{4,9},{5,8},{6,11},{7,10},{8,5},{9,4},... | collective-permute-start | bytes 196616 | tf_op jit(solution)/shard_map/ppermute | solution.py:296
  10.0 6.9 %collective-permute-start.2 = (bf16[2,8,16,128]{3,2,1,0:T(8,128)(2,1)S(1)}, bf16[2,8,16,128]{3,2,1,0:T(8,128)(2,1)S(1)}, u32[]{:S(2)}, u32[]{:S(2)}) collective-permute-start(bf16[2,8,16,128]{3,2,1,0:T(8,128)(2,1)S(1)} %get-tuple-element.62), channel_id=1, source_target_pairs={{0,12},{1,13},{2,14},{3,15},{4,8},{5,9},{6,10},{7,11},{8,4},{9,5},... | collective-permute-start | bytes 196616 | tf_op jit(solution)/shard_map/ppermute | solution.py:296
  10.3 14.1 %collective-permute-start.3 = (bf16[2,2,8,16,128]{4,3,2,1,0:T(8,128)(2,1)S(1)}, bf16[2,2,8,16,128]{4,3,2,1,0:T(8,128)(2,1)S(1)}, u32[]{:S(2)}, u32[]{:S(2)}) collective-permute-start(bf16[2,2,8,16,128]{4,3,2,1,0:T(8,128)(2,1)S(1)} %get-tuple-element.63), channel_id=1, source_target_pairs={{0,5},{1,4},{2,7},{3,6},{4,1},{5,0},{6,3},{7,2},{8,13},{9,12},{10,... | collective-permute-start | bytes 393224 | tf_op jit(solution)/shard_map/ppermute | solution.py:296
  10.3 14.1 %collective-permute-start.6 = (bf16[2,2,8,16,128]{4,3,2,1,0:T(8,128)(2,1)S(1)}, bf16[2,2,8,16,128]{4,3,2,1,0:T(8,128)(2,1)S(1)}, u32[]{:S(2)}, u32[]{:S(2)}) collective-permute-start(bf16[2,2,8,16,128]{4,3,2,1,0:T(8,128)(2,1)S(1)} %get-tuple-element.66), channel_id=1, source_target_pairs={{0,4},{1,5},{2,6},{3,7},{4,0},{5,1},{6,2},{7,3},{8,12},{9,13},{10,... | collective-permute-start | bytes 393224 | tf_op jit(solution)/shard_map/ppermute | solution.py:296
  12.1 12.2 %collective-permute-start.7 = (bf16[2,2,8,16,128]{4,3,2,1,0:T(8,128)(2,1)S(1)}, bf16[2,2,8,16,128]{4,3,2,1,0:T(8,128)(2,1)S(1)}, u32[]{:S(2)}, u32[]{:S(2)}) collective-permute-start(bf16[2,2,8,16,128]{4,3,2,1,0:T(8,128)(2,1)S(1)} %get-tuple-element.67), channel_id=1, source_target_pairs={{0,1},{1,0},{2,3},{3,2},{4,5},{5,4},{6,7},{7,6},{8,9},{9,8},{10,11... | collective-permute-start | bytes 393224 | tf_op jit(solution)/shard_map/ppermute | solution.py:296
  13.8 7.2 %collective-permute-start.4 = (bf16[2,8,16,128]{3,2,1,0:T(8,128)(2,1)S(1)}, bf16[2,8,16,128]{3,2,1,0:T(8,128)(2,1)S(1)}, u32[]{:S(2)}, u32[]{:S(2)}) collective-permute-start(bf16[2,8,16,128]{3,2,1,0:T(8,128)(2,1)S(1)} %get-tuple-element.64), channel_id=1, source_target_pairs={{0,9},{1,8},{2,11},{3,10},{4,13},{5,12},{6,15},{7,14},{8,1},{9,0},... | collective-permute-start | bytes 196616 | tf_op jit(solution)/shard_map/ppermute | solution.py:296
  17.0 7.3 %collective-permute-start.5 = (bf16[2,8,16,128]{3,2,1,0:T(8,128)(2,1)S(1)}, bf16[2,8,16,128]{3,2,1,0:T(8,128)(2,1)S(1)}, u32[]{:S(2)}, u32[]{:S(2)}) collective-permute-start(bf16[2,8,16,128]{3,2,1,0:T(8,128)(2,1)S(1)} %get-tuple-element.65), channel_id=1, source_target_pairs={{0,8},{1,9},{2,10},{3,11},{4,12},{5,13},{6,14},{7,15},{8,0},{9,1},... | collective-permute-start | bytes 196616 | tf_op jit(solution)/shard_map/ppermute | solution.py:296
  24.9 1.4 %collective-permute-start.8 = (bf16[4,8,16,128]{3,2,1,0:T(8,128)(2,1)S(1)}, bf16[4,8,16,128]{3,2,1,0:T(8,128)(2,1)S(1)}, u32[]{:S(2)}, u32[]{:S(2)}) collective-permute-start(bf16[4,8,16,128]{3,2,1,0:T(8,128)(2,1)S(1)} %get-tuple-element.79), channel_id=1, source_target_pairs={{0,2},{1,3},{2,0},{3,1},{4,6},{5,7},{6,4},{7,5},{8,10},{9,11},{10,... | collective-permute-start | bytes 393224 | tf_op jit(solution)/shard_map/ppermute | solution.py:296
  26.4 5.8 %collective-permute-start.9 = (bf16[2,8,16,128]{3,2,1,0:T(8,128)(2,1)S(1)}, bf16[2,8,16,128]{3,2,1,0:T(8,128)(2,1)S(1)}, u32[]{:S(2)}, u32[]{:S(2)}) collective-permute-start(bf16[2,8,16,128]{3,2,1,0:T(8,128)(2,1)S(1)} %get-tuple-element.80), channel_id=1, source_target_pairs={{0,5},{1,4},{2,7},{3,6},{4,1},{5,0},{6,3},{7,2},{8,13},{9,12},{10,... | collective-permute-start | bytes 196616 | tf_op jit(solution)/shard_map/ppermute | solution.py:296
  27.1 5.1 %collective-permute-start.10 = (bf16[2,8,16,128]{3,2,1,0:T(8,128)(2,1)S(1)}, bf16[2,8,16,128]{3,2,1,0:T(8,128)(2,1)S(1)}, u32[]{:S(2)}, u32[]{:S(2)}) collective-permute-start(bf16[2,8,16,128]{3,2,1,0:T(8,128)(2,1)S(1)} %get-tuple-element.81), channel_id=1, source_target_pairs={{0,4},{1,5},{2,6},{3,7},{4,0},{5,1},{6,2},{7,3},{8,12},{9,13},{10,... | collective-permute-start | bytes 196616 | tf_op jit(solution)/shard_map/ppermute | solution.py:296
  28.4 4.4 %collective-permute-start.11 = (bf16[2,8,16,128]{3,2,1,0:T(8,128)(2,1)S(1)}, bf16[2,8,16,128]{3,2,1,0:T(8,128)(2,1)S(1)}, u32[]{:S(2)}, u32[]{:S(2)}) collective-permute-start(bf16[2,8,16,128]{3,2,1,0:T(8,128)(2,1)S(1)} %get-tuple-element.82), channel_id=1, source_target_pairs={{0,1},{1,0},{2,3},{3,2},{4,5},{5,4},{6,7},{7,6},{8,9},{9,8},{10,11... | collective-permute-start | bytes 196616 | tf_op jit(solution)/shard_map/ppermute | solution.py:296
  34.3 1.6 %collective-permute-start.12 = (bf16[4,16,16,128]{3,2,1,0:T(8,128)(2,1)S(1)}, bf16[4,16,16,128]{3,2,1,0:T(8,128)(2,1)S(1)}, u32[]{:S(2)}, u32[]{:S(2)}) collective-permute-start(bf16[4,16,16,128]{3,2,1,0:T(8,128)(2,1)S(1)} %get-tuple-element.86), channel_id=1, source_target_pairs={{0,2},{1,3},{2,0},{3,1},{4,6},{5,7},{6,4},{7,5},{8,10},{9,11},{10,... | collective-permute-start | bytes 786440 | tf_op jit(solution)/shard_map/ppermute | solution.py:296
  35.9 7.3 %collective-permute-start.13 = (bf16[2,16,16,128]{3,2,1,0:T(8,128)(2,1)S(1)}, bf16[2,16,16,128]{3,2,1,0:T(8,128)(2,1)S(1)}, u32[]{:S(2)}, u32[]{:S(2)}) collective-permute-start(bf16[2,16,16,128]{3,2,1,0:T(8,128)(2,1)S(1)} %get-tuple-element.87), channel_id=1, source_target_pairs={{0,5},{1,4},{2,7},{3,6},{4,1},{5,0},{6,3},{7,2},{8,13},{9,12},{10,... | collective-permute-start | bytes 393224 | tf_op jit(solution)/shard_map/ppermute | solution.py:296
  37.2 7.9 %collective-permute-start.14 = (bf16[2,16,16,128]{3,2,1,0:T(8,128)(2,1)S(1)}, bf16[2,16,16,128]{3,2,1,0:T(8,128)(2,1)S(1)}, u32[]{:S(2)}, u32[]{:S(2)}) collective-permute-start(bf16[2,16,16,128]{3,2,1,0:T(8,128)(2,1)S(1)} %get-tuple-element.88), channel_id=1, source_target_pairs={{0,4},{1,5},{2,6},{3,7},{4,0},{5,1},{6,2},{7,3},{8,12},{9,13},{10,... | collective-permute-start | bytes 393224 | tf_op jit(solution)/shard_map/ppermute | solution.py:296
  38.8 6.5 %collective-permute-start.15 = (bf16[2,16,16,128]{3,2,1,0:T(8,128)(2,1)S(1)}, bf16[2,16,16,128]{3,2,1,0:T(8,128)(2,1)S(1)}, u32[]{:S(2)}, u32[]{:S(2)}) collective-permute-start(bf16[2,16,16,128]{3,2,1,0:T(8,128)(2,1)S(1)} %get-tuple-element.89), channel_id=1, source_target_pairs={{0,1},{1,0},{2,3},{3,2},{4,5},{5,4},{6,7},{7,6},{8,9},{9,8},{10,11... | collective-permute-start | bytes 393224 | tf_op jit(solution)/shard_map/ppermute | solution.py:296
  45.8 1.6 %collective-permute-start.16 = (bf16[8,8,16,128]{3,2,1,0:T(8,128)(2,1)S(1)}, bf16[8,8,16,128]{3,2,1,0:T(8,128)(2,1)S(1)}, u32[]{:S(2)}, u32[]{:S(2)}) collective-permute-start(bf16[8,8,16,128]{3,2,1,0:T(8,128)(2,1)S(1)} %get-tuple-element.97), channel_id=1, source_target_pairs={{0,2},{1,3},{2,0},{3,1},{4,6},{5,7},{6,4},{7,5},{8,10},{9,11},{10,... | collective-permute-start | bytes 786440 | tf_op jit(solution)/shard_map/ppermute | solution.py:296
  47.4 8.2 %collective-permute-start.17 = (bf16[2,8,16,128]{3,2,1,0:T(8,128)(2,1)S(1)}, bf16[2,8,16,128]{3,2,1,0:T(8,128)(2,1)S(1)}, u32[]{:S(2)}, u32[]{:S(2)}) collective-permute-start(bf16[2,8,16,128]{3,2,1,0:T(8,128)(2,1)S(1)} %get-tuple-element.98), channel_id=1, source_target_pairs={{0,13},{1,12},{2,15},{3,14},{4,9},{5,8},{6,11},{7,10},{8,5},{9,4},... | collective-permute-start | bytes 196616 | tf_op jit(solution)/shard_map/ppermute | solution.py:296
  50.3 7.6 %collective-permute-start.18 = (bf16[2,8,16,128]{3,2,1,0:T(8,128)(2,1)S(1)}, bf16[2,8,16,128]{3,2,1,0:T(8,128)(2,1)S(1)}, u32[]{:S(2)}, u32[]{:S(2)}) collective-permute-start(bf16[2,8,16,128]{3,2,1,0:T(8,128)(2,1)S(1)} %get-tuple-element.99), channel_id=1, source_target_pairs={{0,12},{1,13},{2,14},{3,15},{4,8},{5,9},{6,10},{7,11},{8,4},{9,5},... | collective-permute-start | bytes 196616 | tf_op jit(solution)/shard_map/ppermute | solution.py:296
  52.1 7.2 %collective-permute-start.19 = (bf16[2,8,16,128]{3,2,1,0:T(8,128)(2,1)S(1)}, bf16[2,8,16,128]{3,2,1,0:T(8,128)(2,1)S(1)}, u32[]{:S(2)}, u32[]{:S(2)}) collective-permute-start(bf16[2,8,16,128]{3,2,1,0:T(8,128)(2,1)S(1)} %get-tuple-element.100), channel_id=1, source_target_pairs={{0,5},{1,4},{2,7},{3,6},{4,1},{5,0},{6,3},{7,2},{8,13},{9,12},{10,... | collective-permute-start | bytes 196616 | tf_op jit(solution)/shard_map/ppermute | solution.py:296
  52.1 9.2 %collective-permute-start.20 = (bf16[2,8,16,128]{3,2,1,0:T(8,128)(2,1)S(1)}, bf16[2,8,16,128]{3,2,1,0:T(8,128)(2,1)S(1)}, u32[]{:S(2)}, u32[]{:S(2)}) collective-permute-start(bf16[2,8,16,128]{3,2,1,0:T(8,128)(2,1)S(1)} %get-tuple-element.101), channel_id=1, source_target_pairs={{0,9},{1,8},{2,11},{3,10},{4,13},{5,12},{6,15},{7,14},{8,1},{9,0},... | collective-permute-start | bytes 196616 | tf_op jit(solution)/shard_map/ppermute | solution.py:296
  55.6 6.4 %collective-permute-start.21 = (bf16[2,8,16,128]{3,2,1,0:T(8,128)(2,1)S(1)}, bf16[2,8,16,128]{3,2,1,0:T(8,128)(2,1)S(1)}, u32[]{:S(2)}, u32[]{:S(2)}) collective-permute-start(bf16[2,8,16,128]{3,2,1,0:T(8,128)(2,1)S(1)} %get-tuple-element.102), channel_id=1, source_target_pairs={{0,8},{1,9},{2,10},{3,11},{4,12},{5,13},{6,14},{7,15},{8,0},{9,1},... | collective-permute-start | bytes 196616 | tf_op jit(solution)/shard_map/ppermute | solution.py:296
  55.6 6.4 %collective-permute-start.22 = (bf16[2,8,16,128]{3,2,1,0:T(8,128)(2,1)S(1)}, bf16[2,8,16,128]{3,2,1,0:T(8,128)(2,1)S(1)}, u32[]{:S(2)}, u32[]{:S(2)}) collective-permute-start(bf16[2,8,16,128]{3,2,1,0:T(8,128)(2,1)S(1)} %get-tuple-element.103), channel_id=1, source_target_pairs={{0,4},{1,5},{2,6},{3,7},{4,0},{5,1},{6,2},{7,3},{8,12},{9,13},{10,... | collective-permute-start | bytes 196616 | tf_op jit(solution)/shard_map/ppermute | solution.py:296
  57.9 4.3 %collective-permute-start.23 = (bf16[2,8,16,128]{3,2,1,0:T(8,128)(2,1)S(1)}, bf16[2,8,16,128]{3,2,1,0:T(8,128)(2,1)S(1)}, u32[]{:S(2)}, u32[]{:S(2)}) collective-permute-start(bf16[2,8,16,128]{3,2,1,0:T(8,128)(2,1)S(1)} %get-tuple-element.104), channel_id=1, source_target_pairs={{0,1},{1,0},{2,3},{3,2},{4,5},{5,4},{6,7},{7,6},{8,9},{9,8},{10,11... | collective-permute-start | bytes 196616 | tf_op jit(solution)/shard_map/ppermute | solution.py:296
  (4 other events, 38.3 us)

commit v7 on v6

--- a/solution.py
+++ b/solution.py
@@ -15,6 +15,7 @@
 SIBLING = 2
 NEAR_STEPS = (0, 5, 4, 1)
 ALL_STEPS = (0, 13, 12, 5, 9, 8, 4, 1)
+CHIPS = len(NEAR_STEPS)
 EPS = 1e-05
 
 
@@ -129,36 +130,25 @@
         tiles[(me ^ step ^ SIBLING) % count] = moved_ref[1]
 
 
-def forward_panels_kernel(keep_ref, got_ref, *out_refs):
-    for step, out_ref in zip(ALL_STEPS[1:], out_refs):
-        n = NEAR_STEPS.index(step % NEAR)
-        for core, ref in enumerate((keep_ref, got_ref)):
-            if step < NEAR:
-                out_ref[core, 0] = ref[0, n]
-                out_ref[core, 1] = ref[1, n]
-            else:
-                out_ref[core] = ref[1, n]
-
-
-def take_in_panels(refs, a_tiles, b_tiles):
-    keep_ref, got_ref, *moved_refs = refs
-    me = own_index()
-    for step, ref in ((0, keep_ref), (SIBLING, got_ref)):
-        a_tiles[(me ^ step) % NEAR] = ref[0, 0]
-        b_tiles[me ^ step] = ref[1, 0]
-    for step, moved_ref in zip(ALL_STEPS[1:], moved_refs):
-        for core, source in enumerate((me ^ step, me ^ step ^ SIBLING)):
-            if step < NEAR:
-                a_tiles[source % NEAR] = moved_ref[core, 0]
-                b_tiles[source] = moved_ref[core, 1]
-            else:
-                b_tiles[source] = moved_ref[core]
-
-
-def first_kernel(
-    rows, cols, pair_hbm, mask_hbm, proj_hbm, proj2_hbm, keep_ref, give_ref, pair_t_ref, normed_ref, live_ref, weights2,
-    pair_ref, mask_ref, proj_ref, proj2_ref, weights, wide, by_near, done,
-):
+def chip_blocks(tiles, index):
+    base = (index % tiles.shape[0]) & ~SIBLING
+    return base, base | SIBLING
+
+
+def chip_of(index):
+    return (index // 4 % 2) * 2 + index % 2
+
+
+def all_b_kernel(*refs):
+    *came_refs, out_ref = refs
+    for n, ref in enumerate(came_refs):
+        out_ref[n] = ref[1] if n < CHIPS else ref[...]
+
+
+def first_kernel(rows, cols, pair_hbm, mask_hbm, proj_hbm, proj2_hbm, *refs):
+    both_refs, b_refs = refs[:CHIPS], refs[CHIPS : 2 * CHIPS]
+    pair_t_ref, normed_ref, live_ref, weights2 = refs[2 * CHIPS : 2 * CHIPS + 4]
+    pair_ref, mask_ref, proj_ref, proj2_ref, weights, wide, by_near, done = refs[2 * CHIPS + 4 :]
     chunks = [slice(at, at + CHUNK) for at in range(0, rows * cols, CHUNK)]
     whole = [(mask_hbm, mask_ref), (proj_hbm, proj_ref), (proj2_hbm, proj2_ref)]
     coming = copies([(pair_hbm.at[at], pair_ref.at[at]) for at in chunks] + whole, done)
@@ -174,15 +164,21 @@
     pair_t_ref[...] = pair
     normed = over_channels(pair).astype(BF16)
     normed_ref[...] = normed
-    for n, values in enumerate(panels(normed, weights)):
+    for p, values in enumerate(panels(normed, weights)):
         half = values.shape[0] // 2
         by_near[...] = paired(values[:half], values[half:], live, cols).reshape(by_near.shape)
-        hand_out(by_near, NEAR_STEPS, keep_ref.at[n], give_ref.at[n])
+        for step, both_ref, b_ref in zip(NEAR_STEPS, both_refs, b_refs):
+            for n, block in enumerate(chip_blocks(by_near, own_index() ^ step)):
+                both_ref[p, n] = by_near[block]
+                if p == 1:
+                    b_ref[n] = by_near[block]
 
 
 def middle_kernel(rows, cols, live_ref, weights, final_ref, pair_t_ref, gating_ref, *refs):
     *came_refs, keep_ref, give_ref, middle_ref, normed_ref, tiles, came, by_near = refs
-    take_in(came_refs, NEAR_STEPS, came)
+    for step, ref in zip(NEAR_STEPS, came_refs):
+        for n, block in enumerate(chip_blocks(came, own_index() ^ step)):
+            came[block] = ref[n]
     middle = pair_t_ref[...] + gating_ref[...] * projected(came, final_ref, tiles, rows, cols)
     middle_ref[...] = middle
     normed = over_channels(middle).astype(BF16)
@@ -229,8 +225,16 @@
 
 
 def outgoing_kernel(cols, *refs):
-    *came_refs, keep_ref, give_ref, a_ref, b_ref, msg_ref = refs
-    take_in_panels(came_refs, a_ref, b_ref)
+    both_refs, far_refs, sibling_ref = refs[:CHIPS], refs[CHIPS : 2 * CHIPS], refs[2 * CHIPS]
+    *out_refs, a_ref, b_ref, msg_ref = refs[2 * CHIPS + 1 :]
+    me = own_index()
+    one = a_ref.shape[1:]
+    for n, step in enumerate(NEAR_STEPS):
+        a_ref[chip_of(me ^ step)] = both_refs[n][0].reshape(one)
+        b_ref[me ^ step] = both_refs[n][1].reshape(one)
+        b_ref[me ^ step ^ SIBLING] = sibling_ref[n].reshape(one)
+        b_ref[me ^ step ^ NEAR] = far_refs[n][...].reshape(one)
+        b_ref[me ^ step ^ NEAR ^ SIBLING] = sibling_ref[CHIPS + n].reshape(one)
     for q in range(msg_ref.shape[1]):
         even, odd = both(a_ref, q)
         low = low_of(even, cols)
@@ -242,7 +246,8 @@
         y = lax.dot_general(a2, b2, (((1,), (1,)), ((), ())), preferred_element_type=F32)
         low = low_of(x, cols)
         put(jnp.where(low, x, pltpu.roll(y, cols, 1)), jnp.where(low, pltpu.roll(x, cols, 1), y), msg_ref, q)
-    hand_out(msg_ref, NEAR_STEPS, keep_ref, give_ref)
+    for step, out_ref in zip(NEAR_STEPS, out_refs):
+        out_ref[...] = msg_ref[chip_of(me ^ step)].reshape(out_ref.shape)
 
 
 def incoming_kernel(cols, *refs):
@@ -300,12 +305,15 @@
         moving = call(forward_kernel, [shape((2,) + keep.shape[1:], BF16)] * (len(steps) - 1))(keep, got)
         return (keep, got, *(swap(block, step) for block, step in zip(moving, steps[1:])))
 
-    def exchange_panels(keep, give):
-        got = swap(give, SIBLING)
-        one = keep.shape[2:]
-        outs = [shape((2, 2) + one if step < NEAR else (2,) + one, BF16) for step in ALL_STEPS[1:]]
-        moving = call(forward_panels_kernel, outs)(keep, got)
-        return (keep, got, *(swap(block, step) for block, step in zip(moving, ALL_STEPS[1:])))
+    def exchange_panels(both, b):
+        moved = {0: both[0]}
+        for step in ALL_STEPS[1:]:
+            n = NEAR_STEPS.index(step % NEAR)
+            moved[step] = swap(both[n] if step < NEAR else b[n], step)
+        near = [moved[step] for step in NEAR_STEPS]
+        far = [moved[step ^ NEAR] for step in NEAR_STEPS]
+        (all_b,) = call(all_b_kernel, [shape((2 * CHIPS,) + both[0].shape[1:], BF16)])(*near, *far)
+        return (*near, *far, swap(all_b, SIBLING))
 
     def messages(targets, tiles):
         return shape((targets, tiles, rows, LANES), BF16)
@@ -321,24 +329,25 @@
     weights = (channels, 4 * hidden)
     chunks = positions // CHUNK
     pairs = hidden // NEAR // 2
-    panel_steps = (shape((2, len(NEAR_STEPS), pairs, rows, LANES), BF16),) * 2
-    near_steps = (messages(len(NEAR_STEPS), pairs),) * 2
+    per_chip = (messages(2, pairs),) * CHIPS
+    both_per_chip = (shape((2, 2, pairs, rows, LANES), BF16),) * CHIPS
     wide_near_steps = (messages(len(NEAR_STEPS), 2 * pairs),) * 2
     all_steps = (messages(len(ALL_STEPS), pairs),) * 2
     gate = call(gate_kernel, [plane], flops=2 * channels * channels * positions, transcendentals=channels * positions)
 
     far = (pair.reshape(positions, channels), mask, out_proj.reshape(-1, hidden), in_proj.reshape(-1, hidden))
-    outs = (*panel_steps, plane, half_plane, shape((rows, LANES), F32), shape(weights, BF16))
+    outs = (*both_per_chip, *per_chip, plane, half_plane, shape((rows, LANES), F32), shape(weights, BF16))
     scratch = [pltpu.VMEM(a.shape, a.dtype) for a in far]
     scratch += [pltpu.VMEM(weights, BF16), pltpu.VMEM((4 * channels, hidden), F32)]
     scratch += [scratch_tiles(NEAR, pairs), pltpu.SemaphoreType.DMA((chunks + 3,))]
-    keep, give, pair_t, normed, live, weights = call(functools.partial(first_kernel, rows, cols), outs, scratch, (4, 0))(*far)
-    came = exchange_panels(keep, give)
+    outs = call(functools.partial(first_kernel, rows, cols), outs, scratch, (4, 0))(*far)
+    pair_t, normed, live, weights = outs[2 * CHIPS :]
+    came = exchange_panels(outs[:CHIPS], outs[CHIPS : 2 * CHIPS])
     gating, came = lax.optimization_barrier((gate(normed, out_gate)[0], came))
 
-    scratch = [scratch_tiles(NEAR, pairs), scratch_tiles(devices, pairs), scratch_tiles(NEAR, pairs)]
-    keep, give = call(functools.partial(outgoing_kernel, cols), near_steps, scratch)(*came)
-    came = exchange(keep, give, NEAR_STEPS)
+    scratch = [scratch_tiles(CHIPS, 2 * pairs), scratch_tiles(devices, 2 * pairs), scratch_tiles(CHIPS, 2 * pairs)]
+    own, *others = call(functools.partial(outgoing_kernel, cols), per_chip, scratch)(*came)
+    came = (own, *(swap(block, step) for block, step in zip(others, NEAR_STEPS[1:])))
 
     scratch = [tiles, scratch_tiles(NEAR, pairs), scratch_tiles(NEAR, 2 * pairs)]
     outs = (*wide_near_steps, plane, half_plane)

time: 63.9 us -> 63.5 us (level)
  waiting for transfers between devices: 24.2 us -> 22.1 us
  starting transfers between devices: 32.3 us -> 33.1 us
    ppermute x24 -> x23, waiting for transfers between devices: 24.2 us -> 22.1 us  [swap(): return lax.ppermute(values, axes, [(d, d ^ step) for d in range(devices)])]
    ppermute x24 -> x23, starting transfers between devices: 32.3 us -> 33.1 us  [swap(): return lax.ppermute(values, axes, [(d, d ^ step) for d in range(devices)])]
    pallas_call x11 -> x10, Pallas kernels: 7.08 us -> 7.32 us  [run(): pl.pallas_call(kernel, out_shape=tuple(out_shape), in_specs=[hbm] * far_a...]
  transfers between devices with their start and end apart: 24 -> 23, of which waited for: 15 -> 13; matrix products, arithmetic and copies ran while one was open for 0% -> 0% of each run, Pallas kernels for 1% -> 1%
where the time goes in v7:
time: 63.5 us; the launch traced here: 63.3 us
  starting transfers between devices  33.1 us (52%)
  waiting for transfers between devices  22.1 us (35%)
  Pallas kernels  7.32 us (12%)
  local copies, waits for them, and re-layouts  0.64 us (1%)
    ppermute x23, starting transfers between devices, swap(): return lax.ppermute(values, axes, [(d, d ^ step) for d in range(devices)])  33.1 us
    ppermute x23, waiting for transfers between devices, swap(): return lax.ppermute(values, axes, [(d, d ^ step) for d in range(devices)])  22.1 us
    pallas_call x10, Pallas kernels, run(): pl.pallas_call(kernel, out_shape=tuple(out_shape), in_specs=[hbm] * far_a...  7.32 us
  transfers between devices with their start and end apart: 23, of which 13 were waited for; matrix products, arithmetic and copies ran while one was open for 0% of the time, Pallas kernels for 1%

profile of v7, /device:TPU:0, one launch (start us, length us, event | category | flops | bytes accessed | tf_op | source)
XLA Modules:
  0.0 63.3 jit_solution(6258605671886820270)
XLA Ops:
  0.0 2.4 %shard_map.82 = (bf16[2,2,8,16,128]{4,3,2,1,0:T(8,128)(2,1)S(1)}, bf16[2,2,8,16,128]{4,3,2,1,0:T(8,128)(2,1)S(1)}, bf16[2,2,8,16,128]{4,3,2,1,0:T(8,128)(2,1)S(1...) custom-call(f32[1024,128]{1,0:T(8,128)} %bitcast.5, ...), custom_call_target="tpu_custom_call" | custom-call | bytes 2499072 | tf_op jit(solution)/shard_map/pallas_call | solution.py:278
  2.4 4.1 %collective-permute-start.3 = (bf16[2,8,16,128]{3,2,1,0:T(8,128)(2,1)S(1)}, bf16[2,8,16,128]{3,2,1,0:T(8,128)(2,1)S(1)}, u32[]{:S(2)}, u32[]{:S(2)}) collective-permute-start(bf16[2,8,16,128]{3,2,1,0:T(8,128)(2,1)S(1)} %get-tuple-element.61), channel_id=1, source_target_pairs={{0,8},{1,9},{2,10},{3,11},{4,12},{5,13},{6,14},{7,15},{8,0},{9,1},... | collective-permute-start | bytes 196616 | tf_op jit(solution)/shard_map/ppermute | solution.py:301
  6.5 2.3 %collective-permute-start.4 = (bf16[2,8,16,128]{3,2,1,0:T(8,128)(2,1)S(1)}, bf16[2,8,16,128]{3,2,1,0:T(8,128)(2,1)S(1)}, u32[]{:S(2)}, u32[]{:S(2)}) collective-permute-start(bf16[2,8,16,128]{3,2,1,0:T(8,128)(2,1)S(1)} %get-tuple-element.62), channel_id=1, source_target_pairs={{0,13},{1,12},{2,15},{3,14},{4,9},{5,8},{6,11},{7,10},{8,5},{9,4},... | collective-permute-start | bytes 196616 | tf_op jit(solution)/shard_map/ppermute | solution.py:301
  9.0 1.8 %collective-permute-start.1 = (bf16[2,2,8,16,128]{4,3,2,1,0:T(8,128)(2,1)S(1)}, bf16[2,2,8,16,128]{4,3,2,1,0:T(8,128)(2,1)S(1)}, u32[]{:S(2)}, u32[]{:S(2)}) collective-permute-start(bf16[2,2,8,16,128]{4,3,2,1,0:T(8,128)(2,1)S(1)} %get-tuple-element.59), channel_id=1, source_target_pairs={{0,4},{1,5},{2,6},{3,7},{4,0},{5,1},{6,2},{7,3},{8,12},{9,13},{10,... | collective-permute-start | bytes 393224 | tf_op jit(solution)/shard_map/ppermute | solution.py:301
  10.7 1.5 %collective-permute-start.2 = (bf16[2,2,8,16,128]{4,3,2,1,0:T(8,128)(2,1)S(1)}, bf16[2,2,8,16,128]{4,3,2,1,0:T(8,128)(2,1)S(1)}, u32[]{:S(2)}, u32[]{:S(2)}) collective-permute-start(bf16[2,2,8,16,128]{4,3,2,1,0:T(8,128)(2,1)S(1)} %get-tuple-element.60), channel_id=1, source_target_pairs={{0,1},{1,0},{2,3},{3,2},{4,5},{5,4},{6,7},{7,6},{8,9},{9,8},{10,11... | collective-permute-start | bytes 393224 | tf_op jit(solution)/shard_map/ppermute | solution.py:301
  12.2 2.9 %collective-permute-start.5 = (bf16[2,8,16,128]{3,2,1,0:T(8,128)(2,1)S(1)}, bf16[2,8,16,128]{3,2,1,0:T(8,128)(2,1)S(1)}, u32[]{:S(2)}, u32[]{:S(2)}) collective-permute-start(bf16[2,8,16,128]{3,2,1,0:T(8,128)(2,1)S(1)} %get-tuple-element.63), channel_id=1, source_target_pairs={{0,12},{1,13},{2,14},{3,15},{4,8},{5,9},{6,10},{7,11},{8,4},{9,5},... | collective-permute-start | bytes 196616 | tf_op jit(solution)/shard_map/ppermute | solution.py:301
  15.2 1.8 %collective-permute-start.6 = (bf16[2,8,16,128]{3,2,1,0:T(8,128)(2,1)S(1)}, bf16[2,8,16,128]{3,2,1,0:T(8,128)(2,1)S(1)}, u32[]{:S(2)}, u32[]{:S(2)}) collective-permute-start(bf16[2,8,16,128]{3,2,1,0:T(8,128)(2,1)S(1)} %get-tuple-element.64), channel_id=1, source_target_pairs={{0,9},{1,8},{2,11},{3,10},{4,13},{5,12},{6,15},{7,14},{8,1},{9,0},... | collective-permute-start | bytes 196616 | tf_op jit(solution)/shard_map/ppermute | solution.py:301
  16.9 3.6 %collective-permute-done.5.refs_6_ = bf16[2,8,16,128]{3,2,1,0:T(8,128)(2,1)S(1)} collective-permute-done((bf16[2,8,16,128]{3,2,1,0:T(8,128)(2,1)S(1)}, bf16[2,8,16,128]{3,2,1,0:T(8,128)(2,1)S(1)}, u32[]{:S(2)}, u32[]{:S(2)}) %collective-permute-start.5) | collective-permute-done | bytes 65568 | tf_op jit(solution)/shard_map/ppermute | solution.py:301
  20.6 1.9 %collective-permute-done.6.refs_7_ = bf16[2,8,16,128]{3,2,1,0:T(8,128)(2,1)S(1)} collective-permute-done((bf16[2,8,16,128]{3,2,1,0:T(8,128)(2,1)S(1)}, bf16[2,8,16,128]{3,2,1,0:T(8,128)(2,1)S(1)}, u32[]{:S(2)}, u32[]{:S(2)}) %collective-permute-start.6) | collective-permute-done | bytes 65568 | tf_op jit(solution)/shard_map/ppermute | solution.py:301
  25.4 1.1 %collective-permute-start.10 = (bf16[2,8,16,128]{3,2,1,0:T(8,128)(2,1)S(1)}, bf16[2,8,16,128]{3,2,1,0:T(8,128)(2,1)S(1)}, u32[]{:S(2)}, u32[]{:S(2)}) collective-permute-start(bf16[2,8,16,128]{3,2,1,0:T(8,128)(2,1)S(1)} %get-tuple-element.78), channel_id=1, source_target_pairs={{0,1},{1,0},{2,3},{3,2},{4,5},{5,4},{6,7},{7,6},{8,9},{9,8},{10,11... | collective-permute-start | bytes 196616 | tf_op jit(solution)/shard_map/ppermute | solution.py:301
  26.8 2.2 %collective-permute-start.9 = (bf16[2,8,16,128]{3,2,1,0:T(8,128)(2,1)S(1)}, bf16[2,8,16,128]{3,2,1,0:T(8,128)(2,1)S(1)}, u32[]{:S(2)}, u32[]{:S(2)}) collective-permute-start(bf16[2,8,16,128]{3,2,1,0:T(8,128)(2,1)S(1)} %get-tuple-element.77), channel_id=1, source_target_pairs={{0,4},{1,5},{2,6},{3,7},{4,0},{5,1},{6,2},{7,3},{8,12},{9,13},{10,... | collective-permute-start | bytes 196616 | tf_op jit(solution)/shard_map/ppermute | solution.py:301
  29.7 2.2 %collective-permute-done.8.refs_1_ = bf16[2,8,16,128]{3,2,1,0:T(8,128)(2,1)S(1)} collective-permute-done((bf16[2,8,16,128]{3,2,1,0:T(8,128)(2,1)S(1)}, bf16[2,8,16,128]{3,2,1,0:T(8,128)(2,1)S(1)}, u32[]{:S(2)}, u32[]{:S(2)}) %collective-permute-start.8) | collective-permute-done | bytes 65568 | tf_op jit(solution)/shard_map/ppermute | solution.py:301
  32.2 1.4 %shard_map.86 = (bf16[4,16,16,128]{3,2,1,0:T(8,128)(2,1)S(1)}, bf16[4,16,16,128]{3,2,1,0:T(8,128)(2,1)S(1)}, f32[128,1024]{1,0:T(8,128)S(1)}, bf16[128,1024]{1,0:T(8,128)(2,1)S(1)}) custom-call(f32[16,128]{1,0:T(8,128)S(1)} %get-tuple-element.53.live_ref, bf16[128,512]{1,0:T(8,128)(2,1)S(1)} %get-tuple-element.54.weights, bf16[128,128]{1,0:T(8,128)(2,1)S(1)} %copy-done.2, ...), custom_call_target="tpu_custom_call" | custom-call | bytes 2793472 | tf_op jit(solution)/shard_map/pallas_call | solution.py:278
  33.7 1.5 %collective-permute-done.11.got_ref.refs_1_ = bf16[4,16,16,128]{3,2,1,0:T(8,128)(2,1)S(1)} collective-permute-done((bf16[4,16,16,128]{3,2,1,0:T(8,128)(2,1)S(1)}, bf16[4,16,16,128]{3,2,1,0:T(8,128)(2,1)S(1)}, u32[]{:S(2)}, u32[]{:S(2)}) %collective-permute-start.11) | collective-permute-done | bytes 262176 | tf_op jit(solution)/shard_map/ppermute | solution.py:301
  35.2 1.5 %collective-permute-start.12 = (bf16[2,16,16,128]{3,2,1,0:T(8,128)(2,1)S(1)}, bf16[2,16,16,128]{3,2,1,0:T(8,128)(2,1)S(1)}, u32[]{:S(2)}, u32[]{:S(2)}) collective-permute-start(bf16[2,16,16,128]{3,2,1,0:T(8,128)(2,1)S(1)} %get-tuple-element.83), channel_id=1, source_target_pairs={{0,5},{1,4},{2,7},{3,6},{4,1},{5,0},{6,3},{7,2},{8,13},{9,12},{10,... | collective-permute-start | bytes 393224 | tf_op jit(solution)/shard_map/ppermute | solution.py:301
  39.0 3.5 %collective-permute-done.12.refs_2_ = bf16[2,16,16,128]{3,2,1,0:T(8,128)(2,1)S(1)} collective-permute-done((bf16[2,16,16,128]{3,2,1,0:T(8,128)(2,1)S(1)}, bf16[2,16,16,128]{3,2,1,0:T(8,128)(2,1)S(1)}, u32[]{:S(2)}, u32[]{:S(2)}) %collective-permute-start.12) | collective-permute-done | bytes 131104 | tf_op jit(solution)/shard_map/ppermute | solution.py:301
  42.5 1.6 %collective-permute-done.13.refs_3_ = bf16[2,16,16,128]{3,2,1,0:T(8,128)(2,1)S(1)} collective-permute-done((bf16[2,16,16,128]{3,2,1,0:T(8,128)(2,1)S(1)}, bf16[2,16,16,128]{3,2,1,0:T(8,128)(2,1)S(1)}, u32[]{:S(2)}, u32[]{:S(2)}) %collective-permute-start.13) | collective-permute-done | bytes 131104 | tf_op jit(solution)/shard_map/ppermute | solution.py:301
  45.1 1.5 %collective-permute-done.15.got_ref.refs_1_ = bf16[8,8,16,128]{3,2,1,0:T(8,128)(2,1)S(1)} collective-permute-done((bf16[8,8,16,128]{3,2,1,0:T(8,128)(2,1)S(1)}, bf16[8,8,16,128]{3,2,1,0:T(8,128)(2,1)S(1)}, u32[]{:S(2)}, u32[]{:S(2)}) %collective-permute-start.15) | collective-permute-done | bytes 262176 | tf_op jit(solution)/shard_map/ppermute | solution.py:301
  46.7 1.8 %collective-permute-start.16 = (bf16[2,8,16,128]{3,2,1,0:T(8,128)(2,1)S(1)}, bf16[2,8,16,128]{3,2,1,0:T(8,128)(2,1)S(1)}, u32[]{:S(2)}, u32[]{:S(2)}) collective-permute-start(bf16[2,8,16,128]{3,2,1,0:T(8,128)(2,1)S(1)} %get-tuple-element.94), channel_id=1, source_target_pairs={{0,13},{1,12},{2,15},{3,14},{4,9},{5,8},{6,11},{7,10},{8,5},{9,4},... | collective-permute-start | bytes 196616 | tf_op jit(solution)/shard_map/ppermute | solution.py:301
  48.5 2.5 %collective-permute-start.17 = (bf16[2,8,16,128]{3,2,1,0:T(8,128)(2,1)S(1)}, bf16[2,8,16,128]{3,2,1,0:T(8,128)(2,1)S(1)}, u32[]{:S(2)}, u32[]{:S(2)}) collective-permute-start(bf16[2,8,16,128]{3,2,1,0:T(8,128)(2,1)S(1)} %get-tuple-element.95), channel_id=1, source_target_pairs={{0,12},{1,13},{2,14},{3,15},{4,8},{5,9},{6,10},{7,11},{8,4},{9,5},... | collective-permute-start | bytes 196616 | tf_op jit(solution)/shard_map/ppermute | solution.py:301
  51.0 2.8 %collective-permute-start.19 = (bf16[2,8,16,128]{3,2,1,0:T(8,128)(2,1)S(1)}, bf16[2,8,16,128]{3,2,1,0:T(8,128)(2,1)S(1)}, u32[]{:S(2)}, u32[]{:S(2)}) collective-permute-start(bf16[2,8,16,128]{3,2,1,0:T(8,128)(2,1)S(1)} %get-tuple-element.97), channel_id=1, source_target_pairs={{0,9},{1,8},{2,11},{3,10},{4,13},{5,12},{6,15},{7,14},{8,1},{9,0},... | collective-permute-start | bytes 196616 | tf_op jit(solution)/shard_map/ppermute | solution.py:301
  54.4 2.5 %collective-permute-start.21 = (bf16[2,8,16,128]{3,2,1,0:T(8,128)(2,1)S(1)}, bf16[2,8,16,128]{3,2,1,0:T(8,128)(2,1)S(1)}, u32[]{:S(2)}, u32[]{:S(2)}) collective-permute-start(bf16[2,8,16,128]{3,2,1,0:T(8,128)(2,1)S(1)} %get-tuple-element.99), channel_id=1, source_target_pairs={{0,4},{1,5},{2,6},{3,7},{4,0},{5,1},{6,2},{7,3},{8,12},{9,13},{10,... | collective-permute-start | bytes 196616 | tf_op jit(solution)/shard_map/ppermute | solution.py:301
  57.9 3.6 %collective-permute-done.19.refs_5_ = bf16[2,8,16,128]{3,2,1,0:T(8,128)(2,1)S(1)} collective-permute-done((bf16[2,8,16,128]{3,2,1,0:T(8,128)(2,1)S(1)}, bf16[2,8,16,128]{3,2,1,0:T(8,128)(2,1)S(1)}, u32[]{:S(2)}, u32[]{:S(2)}) %collective-permute-start.19) | collective-permute-done | bytes 65568 | tf_op jit(solution)/shard_map/ppermute | solution.py:301
  61.7 1.6 %shard_map.91 = f32[1024,128]{1,0:T(8,128)} custom-call(f32[128,1024]{1,0:T(8,128)S(1)} %get-tuple-element.79.middle_ref, f32[128,1024]{1,0:T(8,128)S(1)} %shard_map.87.gating_ref, bf16[128,128]{1,0:T(8,128)(2,1)S(1)} %copy-done, bf16[8,8,16,128]{3,2,1,0:T(8,128)(2,1)S(1)} %get-tuple-element.92.keep_ref.refs_0_, ...), custom_call_target="tpu_custom_call" | custom-call | bytes 2588672 | tf_op jit(solution)/shard_map/pallas_call | solution.py:278
  (40 shorter events, 9.7 us)
Async XLA Ops:
  2.4 9.9 %collective-permute-start.3 = (bf16[2,8,16,128]{3,2,1,0:T(8,128)(2,1)S(1)}, bf16[2,8,16,128]{3,2,1,0:T(8,128)(2,1)S(1)}, u32[]{:S(2)}, u32[]{:S(2)}) collective-permute-start(bf16[2,8,16,128]{3,2,1,0:T(8,128)(2,1)S(1)} %get-tuple-element.61), channel_id=1, source_target_pairs={{0,8},{1,9},{2,10},{3,11},{4,12},{5,13},{6,14},{7,15},{8,0},{9,1},... | collective-permute-start | bytes 196616 | tf_op jit(solution)/shard_map/ppermute | solution.py:301
  6.5 8.7 %collective-permute-start.4 = (bf16[2,8,16,128]{3,2,1,0:T(8,128)(2,1)S(1)}, bf16[2,8,16,128]{3,2,1,0:T(8,128)(2,1)S(1)}, u32[]{:S(2)}, u32[]{:S(2)}) collective-permute-start(bf16[2,8,16,128]{3,2,1,0:T(8,128)(2,1)S(1)} %get-tuple-element.62), channel_id=1, source_target_pairs={{0,13},{1,12},{2,15},{3,14},{4,9},{5,8},{6,11},{7,10},{8,5},{9,4},... | collective-permute-start | bytes 196616 | tf_op jit(solution)/shard_map/ppermute | solution.py:301
  8.7 13.8 %collective-permute-start = (bf16[2,2,8,16,128]{4,3,2,1,0:T(8,128)(2,1)S(1)}, bf16[2,2,8,16,128]{4,3,2,1,0:T(8,128)(2,1)S(1)}, u32[]{:S(2)}, u32[]{:S(2)}) collective-permute-start(bf16[2,2,8,16,128]{4,3,2,1,0:T(8,128)(2,1)S(1)} %get-tuple-element.58), channel_id=1, source_target_pairs={{0,5},{1,4},{2,7},{3,6},{4,1},{5,0},{6,3},{7,2},{8,13},{9,12},{10,... | collective-permute-start | bytes 393224 | tf_op jit(solution)/shard_map/ppermute | solution.py:301
  9.0 13.5 %collective-permute-start.1 = (bf16[2,2,8,16,128]{4,3,2,1,0:T(8,128)(2,1)S(1)}, bf16[2,2,8,16,128]{4,3,2,1,0:T(8,128)(2,1)S(1)}, u32[]{:S(2)}, u32[]{:S(2)}) collective-permute-start(bf16[2,2,8,16,128]{4,3,2,1,0:T(8,128)(2,1)S(1)} %get-tuple-element.59), channel_id=1, source_target_pairs={{0,4},{1,5},{2,6},{3,7},{4,0},{5,1},{6,2},{7,3},{8,12},{9,13},{10,... | collective-permute-start | bytes 393224 | tf_op jit(solution)/shard_map/ppermute | solution.py:301
  10.7 11.8 %collective-permute-start.2 = (bf16[2,2,8,16,128]{4,3,2,1,0:T(8,128)(2,1)S(1)}, bf16[2,2,8,16,128]{4,3,2,1,0:T(8,128)(2,1)S(1)}, u32[]{:S(2)}, u32[]{:S(2)}) collective-permute-start(bf16[2,2,8,16,128]{4,3,2,1,0:T(8,128)(2,1)S(1)} %get-tuple-element.60), channel_id=1, source_target_pairs={{0,1},{1,0},{2,3},{3,2},{4,5},{5,4},{6,7},{7,6},{8,9},{9,8},{10,11... | collective-permute-start | bytes 393224 | tf_op jit(solution)/shard_map/ppermute | solution.py:301
  12.2 8.3 %collective-permute-start.5 = (bf16[2,8,16,128]{3,2,1,0:T(8,128)(2,1)S(1)}, bf16[2,8,16,128]{3,2,1,0:T(8,128)(2,1)S(1)}, u32[]{:S(2)}, u32[]{:S(2)}) collective-permute-start(bf16[2,8,16,128]{3,2,1,0:T(8,128)(2,1)S(1)} %get-tuple-element.63), channel_id=1, source_target_pairs={{0,12},{1,13},{2,14},{3,15},{4,8},{5,9},{6,10},{7,11},{8,4},{9,5},... | collective-permute-start | bytes 196616 | tf_op jit(solution)/shard_map/ppermute | solution.py:301
  15.2 7.3 %collective-permute-start.6 = (bf16[2,8,16,128]{3,2,1,0:T(8,128)(2,1)S(1)}, bf16[2,8,16,128]{3,2,1,0:T(8,128)(2,1)S(1)}, u32[]{:S(2)}, u32[]{:S(2)}) collective-permute-start(bf16[2,8,16,128]{3,2,1,0:T(8,128)(2,1)S(1)} %get-tuple-element.64), channel_id=1, source_target_pairs={{0,9},{1,8},{2,11},{3,10},{4,13},{5,12},{6,15},{7,14},{8,1},{9,0},... | collective-permute-start | bytes 196616 | tf_op jit(solution)/shard_map/ppermute | solution.py:301
  22.6 2.0 %collective-permute-start.7 = (bf16[8,2,8,16,128]{4,3,2,1,0:T(8,128)(2,1)S(1)}, bf16[8,2,8,16,128]{4,3,2,1,0:T(8,128)(2,1)S(1)}, u32[]{:S(2)}, u32[]{:S(2)}) collective-permute-start(bf16[8,2,8,16,128]{4,3,2,1,0:T(8,128)(2,1)S(1)} %shard_map.84), channel_id=1, source_target_pairs={{0,2},{1,3},{2,0},{3,1},{4,6},{5,7},{6,4},{7,5},{8,10},{9,11},{10,... | collective-permute-start | bytes 1572872 | tf_op jit(solution)/shard_map/ppermute | solution.py:301
  25.4 4.3 %collective-permute-start.10 = (bf16[2,8,16,128]{3,2,1,0:T(8,128)(2,1)S(1)}, bf16[2,8,16,128]{3,2,1,0:T(8,128)(2,1)S(1)}, u32[]{:S(2)}, u32[]{:S(2)}) collective-permute-start(bf16[2,8,16,128]{3,2,1,0:T(8,128)(2,1)S(1)} %get-tuple-element.78), channel_id=1, source_target_pairs={{0,1},{1,0},{2,3},{3,2},{4,5},{5,4},{6,7},{7,6},{8,9},{9,8},{10,11... | collective-permute-start | bytes 196616 | tf_op jit(solution)/shard_map/ppermute | solution.py:301
  26.5 5.5 %collective-permute-start.8 = (bf16[2,8,16,128]{3,2,1,0:T(8,128)(2,1)S(1)}, bf16[2,8,16,128]{3,2,1,0:T(8,128)(2,1)S(1)}, u32[]{:S(2)}, u32[]{:S(2)}) collective-permute-start(bf16[2,8,16,128]{3,2,1,0:T(8,128)(2,1)S(1)} %get-tuple-element.76), channel_id=1, source_target_pairs={{0,5},{1,4},{2,7},{3,6},{4,1},{5,0},{6,3},{7,2},{8,13},{9,12},{10,... | collective-permute-start | bytes 196616 | tf_op jit(solution)/shard_map/ppermute | solution.py:301
  26.8 5.4 %collective-permute-start.9 = (bf16[2,8,16,128]{3,2,1,0:T(8,128)(2,1)S(1)}, bf16[2,8,16,128]{3,2,1,0:T(8,128)(2,1)S(1)}, u32[]{:S(2)}, u32[]{:S(2)}) collective-permute-start(bf16[2,8,16,128]{3,2,1,0:T(8,128)(2,1)S(1)} %get-tuple-element.77), channel_id=1, source_target_pairs={{0,4},{1,5},{2,6},{3,7},{4,0},{5,1},{6,2},{7,3},{8,12},{9,13},{10,... | collective-permute-start | bytes 196616 | tf_op jit(solution)/shard_map/ppermute | solution.py:301
  33.6 1.6 %collective-permute-start.11 = (bf16[4,16,16,128]{3,2,1,0:T(8,128)(2,1)S(1)}, bf16[4,16,16,128]{3,2,1,0:T(8,128)(2,1)S(1)}, u32[]{:S(2)}, u32[]{:S(2)}) collective-permute-start(bf16[4,16,16,128]{3,2,1,0:T(8,128)(2,1)S(1)} %get-tuple-element.82), channel_id=1, source_target_pairs={{0,2},{1,3},{2,0},{3,1},{4,6},{5,7},{6,4},{7,5},{8,10},{9,11},{10,... | collective-permute-start | bytes 786440 | tf_op jit(solution)/shard_map/ppermute | solution.py:301
  35.2 7.3 %collective-permute-start.12 = (bf16[2,16,16,128]{3,2,1,0:T(8,128)(2,1)S(1)}, bf16[2,16,16,128]{3,2,1,0:T(8,128)(2,1)S(1)}, u32[]{:S(2)}, u32[]{:S(2)}) collective-permute-start(bf16[2,16,16,128]{3,2,1,0:T(8,128)(2,1)S(1)} %get-tuple-element.83), channel_id=1, source_target_pairs={{0,5},{1,4},{2,7},{3,6},{4,1},{5,0},{6,3},{7,2},{8,13},{9,12},{10,... | collective-permute-start | bytes 393224 | tf_op jit(solution)/shard_map/ppermute | solution.py:301
  36.8 7.3 %collective-permute-start.13 = (bf16[2,16,16,128]{3,2,1,0:T(8,128)(2,1)S(1)}, bf16[2,16,16,128]{3,2,1,0:T(8,128)(2,1)S(1)}, u32[]{:S(2)}, u32[]{:S(2)}) collective-permute-start(bf16[2,16,16,128]{3,2,1,0:T(8,128)(2,1)S(1)} %get-tuple-element.84), channel_id=1, source_target_pairs={{0,4},{1,5},{2,6},{3,7},{4,0},{5,1},{6,2},{7,3},{8,12},{9,13},{10,... | collective-permute-start | bytes 393224 | tf_op jit(solution)/shard_map/ppermute | solution.py:301
  37.8 6.8 %collective-permute-start.14 = (bf16[2,16,16,128]{3,2,1,0:T(8,128)(2,1)S(1)}, bf16[2,16,16,128]{3,2,1,0:T(8,128)(2,1)S(1)}, u32[]{:S(2)}, u32[]{:S(2)}) collective-permute-start(bf16[2,16,16,128]{3,2,1,0:T(8,128)(2,1)S(1)} %get-tuple-element.85), channel_id=1, source_target_pairs={{0,1},{1,0},{2,3},{3,2},{4,5},{5,4},{6,7},{7,6},{8,9},{9,8},{10,11... | collective-permute-start | bytes 393224 | tf_op jit(solution)/shard_map/ppermute | solution.py:301
  45.1 1.6 %collective-permute-start.15 = (bf16[8,8,16,128]{3,2,1,0:T(8,128)(2,1)S(1)}, bf16[8,8,16,128]{3,2,1,0:T(8,128)(2,1)S(1)}, u32[]{:S(2)}, u32[]{:S(2)}) collective-permute-start(bf16[8,8,16,128]{3,2,1,0:T(8,128)(2,1)S(1)} %get-tuple-element.93), channel_id=1, source_target_pairs={{0,2},{1,3},{2,0},{3,1},{4,6},{5,7},{6,4},{7,5},{8,10},{9,11},{10,... | collective-permute-start | bytes 786440 | tf_op jit(solution)/shard_map/ppermute | solution.py:301
  46.7 15.0 %copy-start = (bf16[128,128]{1,0:T(8,128)(2,1)S(1)}, bf16[128,128]{1,0:T(8,128)(2,1)}, u32[]{:S(2)}) copy-start(bf16[128,128]{1,0:T(8,128)(2,1)} %final_ref.3) | copy-start | bytes 98308
  46.7 7.7 %collective-permute-start.16 = (bf16[2,8,16,128]{3,2,1,0:T(8,128)(2,1)S(1)}, bf16[2,8,16,128]{3,2,1,0:T(8,128)(2,1)S(1)}, u32[]{:S(2)}, u32[]{:S(2)}) collective-permute-start(bf16[2,8,16,128]{3,2,1,0:T(8,128)(2,1)S(1)} %get-tuple-element.94), channel_id=1, source_target_pairs={{0,13},{1,12},{2,15},{3,14},{4,9},{5,8},{6,11},{7,10},{8,5},{9,4},... | collective-permute-start | bytes 196616 | tf_op jit(solution)/shard_map/ppermute | solution.py:301
  48.5 8.4 %collective-permute-start.17 = (bf16[2,8,16,128]{3,2,1,0:T(8,128)(2,1)S(1)}, bf16[2,8,16,128]{3,2,1,0:T(8,128)(2,1)S(1)}, u32[]{:S(2)}, u32[]{:S(2)}) collective-permute-start(bf16[2,8,16,128]{3,2,1,0:T(8,128)(2,1)S(1)} %get-tuple-element.95), channel_id=1, source_target_pairs={{0,12},{1,13},{2,14},{3,15},{4,8},{5,9},{6,10},{7,11},{8,4},{9,5},... | collective-permute-start | bytes 196616 | tf_op jit(solution)/shard_map/ppermute | solution.py:301
  51.0 6.9 %collective-permute-start.18 = (bf16[2,8,16,128]{3,2,1,0:T(8,128)(2,1)S(1)}, bf16[2,8,16,128]{3,2,1,0:T(8,128)(2,1)S(1)}, u32[]{:S(2)}, u32[]{:S(2)}) collective-permute-start(bf16[2,8,16,128]{3,2,1,0:T(8,128)(2,1)S(1)} %get-tuple-element.96), channel_id=1, source_target_pairs={{0,5},{1,4},{2,7},{3,6},{4,1},{5,0},{6,3},{7,2},{8,13},{9,12},{10,... | collective-permute-start | bytes 196616 | tf_op jit(solution)/shard_map/ppermute | solution.py:301
  51.0 10.5 %collective-permute-start.19 = (bf16[2,8,16,128]{3,2,1,0:T(8,128)(2,1)S(1)}, bf16[2,8,16,128]{3,2,1,0:T(8,128)(2,1)S(1)}, u32[]{:S(2)}, u32[]{:S(2)}) collective-permute-start(bf16[2,8,16,128]{3,2,1,0:T(8,128)(2,1)S(1)} %get-tuple-element.97), channel_id=1, source_target_pairs={{0,9},{1,8},{2,11},{3,10},{4,13},{5,12},{6,15},{7,14},{8,1},{9,0},... | collective-permute-start | bytes 196616 | tf_op jit(solution)/shard_map/ppermute | solution.py:301
  53.8 7.8 %collective-permute-start.20 = (bf16[2,8,16,128]{3,2,1,0:T(8,128)(2,1)S(1)}, bf16[2,8,16,128]{3,2,1,0:T(8,128)(2,1)S(1)}, u32[]{:S(2)}, u32[]{:S(2)}) collective-permute-start(bf16[2,8,16,128]{3,2,1,0:T(8,128)(2,1)S(1)} %get-tuple-element.98), channel_id=1, source_target_pairs={{0,8},{1,9},{2,10},{3,11},{4,12},{5,13},{6,14},{7,15},{8,0},{9,1},... | collective-permute-start | bytes 196616 | tf_op jit(solution)/shard_map/ppermute | solution.py:301
  54.4 7.2 %collective-permute-start.21 = (bf16[2,8,16,128]{3,2,1,0:T(8,128)(2,1)S(1)}, bf16[2,8,16,128]{3,2,1,0:T(8,128)(2,1)S(1)}, u32[]{:S(2)}, u32[]{:S(2)}) collective-permute-start(bf16[2,8,16,128]{3,2,1,0:T(8,128)(2,1)S(1)} %get-tuple-element.99), channel_id=1, source_target_pairs={{0,4},{1,5},{2,6},{3,7},{4,0},{5,1},{6,2},{7,3},{8,12},{9,13},{10,... | collective-permute-start | bytes 196616 | tf_op jit(solution)/shard_map/ppermute | solution.py:301
  56.9 4.8 %collective-permute-start.22 = (bf16[2,8,16,128]{3,2,1,0:T(8,128)(2,1)S(1)}, bf16[2,8,16,128]{3,2,1,0:T(8,128)(2,1)S(1)}, u32[]{:S(2)}, u32[]{:S(2)}) collective-permute-start(bf16[2,8,16,128]{3,2,1,0:T(8,128)(2,1)S(1)} %get-tuple-element.100), channel_id=1, source_target_pairs={{0,1},{1,0},{2,3},{3,2},{4,5},{5,4},{6,7},{7,6},{8,9},{9,8},{10,11... | collective-permute-start | bytes 196616 | tf_op jit(solution)/shard_map/ppermute | solution.py:301
  (3 other events, 12.0 us)

commit v8 on v7

--- a/solution.py
+++ b/solution.py
@@ -10,7 +10,7 @@
 F32 = jnp.float32
 BF16 = jnp.bfloat16
 LANES = 128
-CHUNK = 256
+CHUNK = 512
 NEAR = 8
 SIBLING = 2
 NEAR_STEPS = (0, 5, 4, 1)
@@ -75,19 +75,23 @@
     return jnp.swapaxes(jnp.stack(by_row, axis=0), 0, 1)
 
 
-def projected(recv_ref, final_ref, tiles, rows, cols):
+def summed(values):
+    chains = values.reshape((values.shape[0] // 8, 8) + values.shape[1:])
+    return jnp.sum(jnp.sum(chains, axis=0), axis=0)
+
+
+def projected(recv_ref, final_ref, rows, cols):
     half = final_ref.shape[0] // 2
     values = jnp.sum(recv_ref[...].reshape(-1, half, rows, LANES).astype(F32), axis=0)
-    total = jnp.sum(values, axis=0)
+    total = summed(values)
     centred = values - ((total + pltpu.roll(total, cols, 1)) / (2 * half))[None]
-    square = jnp.sum(centred * centred, axis=0)
+    square = summed(centred * centred)
     variance = (square + pltpu.roll(square, cols, 1)) / (2 * half)
-    tiles[: half * rows, :] = (centred * lax.rsqrt(variance + EPS)[None]).reshape(half * rows, LANES)
+    scaled = jnp.swapaxes((centred * lax.rsqrt(variance + EPS)[None]).astype(BF16), 0, 1).astype(F32)
     low = lax.broadcasted_iota(jnp.int32, (half, LANES), 1) < cols
     parts = []
     for t in range(rows // 2):
-        a = tiles[pl.ds(2 * t, half, stride=rows), :]
-        b = tiles[pl.ds(2 * t + 1, half, stride=rows), :]
+        a, b = scaled[2 * t], scaled[2 * t + 1]
         upper = jnp.where(low, a, pltpu.roll(b, cols, 1))
         lower = jnp.where(low, pltpu.roll(a, cols, 1), b)
         parts.append(jnp.concatenate([upper, lower], axis=0).astype(BF16))
@@ -145,17 +149,20 @@
         out_ref[n] = ref[1] if n < CHIPS else ref[...]
 
 
-def first_kernel(rows, cols, pair_hbm, mask_hbm, proj_hbm, proj2_hbm, *refs):
+def second_weights_kernel(proj_ref, weights, wide):
+    side_by_side(proj_ref, wide, weights, "panels")
+
+
+def first_kernel(rows, cols, pair_hbm, mask_hbm, proj_hbm, *refs):
     both_refs, b_refs = refs[:CHIPS], refs[CHIPS : 2 * CHIPS]
-    pair_t_ref, normed_ref, live_ref, weights2 = refs[2 * CHIPS : 2 * CHIPS + 4]
-    pair_ref, mask_ref, proj_ref, proj2_ref, weights, wide, by_near, done = refs[2 * CHIPS + 4 :]
+    pair_t_ref, normed_ref, live_ref = refs[2 * CHIPS : 2 * CHIPS + 3]
+    pair_ref, mask_ref, proj_ref, weights, wide, by_near, done = refs[2 * CHIPS + 3 :]
     chunks = [slice(at, at + CHUNK) for at in range(0, rows * cols, CHUNK)]
-    whole = [(mask_hbm, mask_ref), (proj_hbm, proj_ref), (proj2_hbm, proj2_ref)]
+    whole = [(mask_hbm, mask_ref), (proj_hbm, proj_ref)]
     coming = copies([(pair_hbm.at[at], pair_ref.at[at]) for at in chunks] + whole, done)
     for copy in coming[len(chunks) :]:
         copy.wait()
     side_by_side(proj_ref, wide, weights, "halves")
-    side_by_side(proj2_ref, wide, weights2, "panels")
     live = live_tile(mask_ref, rows, cols)
     live_ref[...] = live
     for copy in coming[: len(chunks)]:
@@ -175,11 +182,11 @@
 
 
 def middle_kernel(rows, cols, live_ref, weights, final_ref, pair_t_ref, gating_ref, *refs):
-    *came_refs, keep_ref, give_ref, middle_ref, normed_ref, tiles, came, by_near = refs
+    *came_refs, keep_ref, give_ref, middle_ref, normed_ref, came, by_near = refs
     for step, ref in zip(NEAR_STEPS, came_refs):
         for n, block in enumerate(chip_blocks(came, own_index() ^ step)):
             came[block] = ref[n]
-    middle = pair_t_ref[...] + gating_ref[...] * projected(came, final_ref, tiles, rows, cols)
+    middle = pair_t_ref[...] + gating_ref[...] * projected(came, final_ref, rows, cols)
     middle_ref[...] = middle
     normed = over_channels(middle).astype(BF16)
     normed_ref[...] = normed
@@ -195,9 +202,9 @@
 
 
 def last_kernel(rows, cols, middle_ref, gating_ref, final_ref, *refs):
-    *came_refs, out_hbm, tiles, came, out_ref, done = refs
+    *came_refs, out_hbm, came, out_ref, done = refs
     take_in(came_refs, ALL_STEPS, came)
-    change = projected(came, final_ref, tiles, rows, cols)
+    change = projected(came, final_ref, rows, cols)
     leaving = []
     for n in range(rows * cols // CHUNK):
         at = slice(n * CHUNK, (n + 1) * CHUNK)
@@ -325,7 +332,6 @@
     half_plane = shape((channels, positions), BF16)
     mask = residue_mask.reshape(1, -1)
     by_position = pltpu.VMEM((positions, channels), F32)
-    tiles = pltpu.VMEM((positions, LANES), F32)
     weights = (channels, 4 * hidden)
     chunks = positions // CHUNK
     pairs = hidden // NEAR // 2
@@ -335,21 +341,23 @@
     all_steps = (messages(len(ALL_STEPS), pairs),) * 2
     gate = call(gate_kernel, [plane], flops=2 * channels * channels * positions, transcendentals=channels * positions)
 
-    far = (pair.reshape(positions, channels), mask, out_proj.reshape(-1, hidden), in_proj.reshape(-1, hidden))
-    outs = (*both_per_chip, *per_chip, plane, half_plane, shape((rows, LANES), F32), shape(weights, BF16))
+    far = (pair.reshape(positions, channels), mask, out_proj.reshape(-1, hidden))
+    outs = (*both_per_chip, *per_chip, plane, half_plane, shape((rows, LANES), F32))
     scratch = [pltpu.VMEM(a.shape, a.dtype) for a in far]
-    scratch += [pltpu.VMEM(weights, BF16), pltpu.VMEM((4 * channels, hidden), F32)]
-    scratch += [scratch_tiles(NEAR, pairs), pltpu.SemaphoreType.DMA((chunks + 3,))]
-    outs = call(functools.partial(first_kernel, rows, cols), outs, scratch, (4, 0))(*far)
-    pair_t, normed, live, weights = outs[2 * CHIPS :]
+    wide = pltpu.VMEM((4 * channels, hidden), F32)
+    scratch += [pltpu.VMEM(weights, BF16), wide]
+    scratch += [scratch_tiles(NEAR, pairs), pltpu.SemaphoreType.DMA((chunks + 2,))]
+    outs = call(functools.partial(first_kernel, rows, cols), outs, scratch, (3, 0))(*far)
+    pair_t, normed, live = outs[2 * CHIPS :]
     came = exchange_panels(outs[:CHIPS], outs[CHIPS : 2 * CHIPS])
-    gating, came = lax.optimization_barrier((gate(normed, out_gate)[0], came))
+    (weights,) = call(second_weights_kernel, [shape(weights, BF16)], [wide])(in_proj.reshape(-1, hidden))
+    gating, weights, came = lax.optimization_barrier((gate(normed, out_gate)[0], weights, came))
 
     scratch = [scratch_tiles(CHIPS, 2 * pairs), scratch_tiles(devices, 2 * pairs), scratch_tiles(CHIPS, 2 * pairs)]
     own, *others = call(functools.partial(outgoing_kernel, cols), per_chip, scratch)(*came)
     came = (own, *(swap(block, step) for block, step in zip(others, NEAR_STEPS[1:])))
 
-    scratch = [tiles, scratch_tiles(NEAR, pairs), scratch_tiles(NEAR, 2 * pairs)]
+    scratch = [scratch_tiles(NEAR, pairs), scratch_tiles(NEAR, 2 * pairs)]
     outs = (*wide_near_steps, plane, half_plane)
     keep, give, middle, normed = call(functools.partial(middle_kernel, rows, cols), outs, scratch)(
         live, weights, out_final, pair_t, gating, *came
@@ -361,7 +369,7 @@
     keep, give = call(functools.partial(incoming_kernel, cols), all_steps, scratch)(*came)
     came = exchange(keep, give, ALL_STEPS)
 
-    scratch = [tiles, scratch_tiles(devices, pairs), by_position, pltpu.SemaphoreType.DMA((chunks,))]
+    scratch = [scratch_tiles(devices, pairs), by_position, pltpu.SemaphoreType.DMA((chunks,))]
     outs = [shape((positions, channels), F32)]
     (out,) = call(functools.partial(last_kernel, rows, cols), outs, scratch, (0, 1))(middle, gating, in_final, *came)
     return out.reshape(rows, cols, channels)

time: 63.5 us -> 63.2 us (level)
  waiting for transfers between devices: 22.1 us -> 21.2 us
  local copies, waits for them, and re-layouts: 0.64 us -> 1.49 us
    ppermute x23, waiting for transfers between devices: 22.1 us -> 21.2 us  [swap(): return lax.ppermute(values, axes, [(d, d ^ step) for d in range(devices)])]
    unnamed x8 -> x10, local copies, waits for them, and re-layouts: 0.64 us -> 1.49 us
    pallas_call x10 -> x11, Pallas kernels: 7.32 us -> 7.11 us  [run(): pl.pallas_call(kernel, out_shape=tuple(out_shape), in_specs=[hbm] * far_a...]
where the time goes in v8:
time: 63.2 us; the launch traced here: 63 us
  starting transfers between devices  33.1 us (52%)
  waiting for transfers between devices  21.2 us (34%)
  Pallas kernels  7.11 us (11%)
  local copies, waits for them, and re-layouts  1.49 us (2%)
    ppermute x23, starting transfers between devices, swap(): return lax.ppermute(values, axes, [(d, d ^ step) for d in range(devices)])  33.1 us
    ppermute x23, waiting for transfers between devices, swap(): return lax.ppermute(values, axes, [(d, d ^ step) for d in range(devices)])  21.2 us
    pallas_call x11, Pallas kernels, run(): pl.pallas_call(kernel, out_shape=tuple(out_shape), in_specs=[hbm] * far_a...  7.11 us
    unnamed x10, local copies, waits for them, and re-layouts  1.49 us
  transfers between devices with their start and end apart: 23, of which 13 were waited for; matrix products, arithmetic and copies ran while one was open for 0% of the time, Pallas kernels for 1%

profile of v8, /device:TPU:0, one launch (start us, length us, event | category | flops | bytes accessed | tf_op | source)
XLA Modules:
  0.0 63.0 jit_solution(17910609485853174044)
XLA Ops:
  0.0 2.2 %shard_map.82 = (bf16[2,2,8,16,128]{4,3,2,1,0:T(8,128)(2,1)S(1)}, bf16[2,2,8,16,128]{4,3,2,1,0:T(8,128)(2,1)S(1)}, bf16[2,2,8,16,128]{4,3,2,1,0:T(8,128)(2,1)S(1...) custom-call(f32[1024,128]{1,0:T(8,128)} %bitcast.6, ...), custom_call_target="tpu_custom_call" | custom-call | bytes 2236928 | tf_op jit(solution)/shard_map/pallas_call | solution.py:285
  2.2 4.1 %collective-permute-start.3 = (bf16[2,8,16,128]{3,2,1,0:T(8,128)(2,1)S(1)}, bf16[2,8,16,128]{3,2,1,0:T(8,128)(2,1)S(1)}, u32[]{:S(2)}, u32[]{:S(2)}) collective-permute-start(bf16[2,8,16,128]{3,2,1,0:T(8,128)(2,1)S(1)} %get-tuple-element.59), channel_id=1, source_target_pairs={{0,8},{1,9},{2,10},{3,11},{4,12},{5,13},{6,14},{7,15},{8,0},{9,1},... | collective-permute-start | bytes 196616 | tf_op jit(solution)/shard_map/ppermute | solution.py:308
  6.3 2.3 %collective-permute-start.4 = (bf16[2,8,16,128]{3,2,1,0:T(8,128)(2,1)S(1)}, bf16[2,8,16,128]{3,2,1,0:T(8,128)(2,1)S(1)}, u32[]{:S(2)}, u32[]{:S(2)}) collective-permute-start(bf16[2,8,16,128]{3,2,1,0:T(8,128)(2,1)S(1)} %get-tuple-element.60), channel_id=1, source_target_pairs={{0,13},{1,12},{2,15},{3,14},{4,9},{5,8},{6,11},{7,10},{8,5},{9,4},... | collective-permute-start | bytes 196616 | tf_op jit(solution)/shard_map/ppermute | solution.py:308
  8.8 1.8 %collective-permute-start.1 = (bf16[2,2,8,16,128]{4,3,2,1,0:T(8,128)(2,1)S(1)}, bf16[2,2,8,16,128]{4,3,2,1,0:T(8,128)(2,1)S(1)}, u32[]{:S(2)}, u32[]{:S(2)}) collective-permute-start(bf16[2,2,8,16,128]{4,3,2,1,0:T(8,128)(2,1)S(1)} %get-tuple-element.57), channel_id=1, source_target_pairs={{0,4},{1,5},{2,6},{3,7},{4,0},{5,1},{6,2},{7,3},{8,12},{9,13},{10,... | collective-permute-start | bytes 393224 | tf_op jit(solution)/shard_map/ppermute | solution.py:308
  10.6 1.5 %collective-permute-start.2 = (bf16[2,2,8,16,128]{4,3,2,1,0:T(8,128)(2,1)S(1)}, bf16[2,2,8,16,128]{4,3,2,1,0:T(8,128)(2,1)S(1)}, u32[]{:S(2)}, u32[]{:S(2)}) collective-permute-start(bf16[2,2,8,16,128]{4,3,2,1,0:T(8,128)(2,1)S(1)} %get-tuple-element.58), channel_id=1, source_target_pairs={{0,1},{1,0},{2,3},{3,2},{4,5},{5,4},{6,7},{7,6},{8,9},{9,8},{10,11... | collective-permute-start | bytes 393224 | tf_op jit(solution)/shard_map/ppermute | solution.py:308
  12.1 2.9 %collective-permute-start.5 = (bf16[2,8,16,128]{3,2,1,0:T(8,128)(2,1)S(1)}, bf16[2,8,16,128]{3,2,1,0:T(8,128)(2,1)S(1)}, u32[]{:S(2)}, u32[]{:S(2)}) collective-permute-start(bf16[2,8,16,128]{3,2,1,0:T(8,128)(2,1)S(1)} %get-tuple-element.61), channel_id=1, source_target_pairs={{0,12},{1,13},{2,14},{3,15},{4,8},{5,9},{6,10},{7,11},{8,4},{9,5},... | collective-permute-start | bytes 196616 | tf_op jit(solution)/shard_map/ppermute | solution.py:308
  15.0 1.8 %collective-permute-start.6 = (bf16[2,8,16,128]{3,2,1,0:T(8,128)(2,1)S(1)}, bf16[2,8,16,128]{3,2,1,0:T(8,128)(2,1)S(1)}, u32[]{:S(2)}, u32[]{:S(2)}) collective-permute-start(bf16[2,8,16,128]{3,2,1,0:T(8,128)(2,1)S(1)} %get-tuple-element.62), channel_id=1, source_target_pairs={{0,9},{1,8},{2,11},{3,10},{4,13},{5,12},{6,15},{7,14},{8,1},{9,0},... | collective-permute-start | bytes 196616 | tf_op jit(solution)/shard_map/ppermute | solution.py:308
  16.7 3.6 %collective-permute-done.5.refs_6_ = bf16[2,8,16,128]{3,2,1,0:T(8,128)(2,1)S(1)} collective-permute-done((bf16[2,8,16,128]{3,2,1,0:T(8,128)(2,1)S(1)}, bf16[2,8,16,128]{3,2,1,0:T(8,128)(2,1)S(1)}, u32[]{:S(2)}, u32[]{:S(2)}) %collective-permute-start.5) | collective-permute-done | bytes 65568 | tf_op jit(solution)/shard_map/ppermute | solution.py:308
  20.4 1.9 %collective-permute-done.6.refs_7_ = bf16[2,8,16,128]{3,2,1,0:T(8,128)(2,1)S(1)} collective-permute-done((bf16[2,8,16,128]{3,2,1,0:T(8,128)(2,1)S(1)}, bf16[2,8,16,128]{3,2,1,0:T(8,128)(2,1)S(1)}, u32[]{:S(2)}, u32[]{:S(2)}) %collective-permute-start.6) | collective-permute-done | bytes 65568 | tf_op jit(solution)/shard_map/ppermute | solution.py:308
  25.2 1.1 %collective-permute-start.10 = (bf16[2,8,16,128]{3,2,1,0:T(8,128)(2,1)S(1)}, bf16[2,8,16,128]{3,2,1,0:T(8,128)(2,1)S(1)}, u32[]{:S(2)}, u32[]{:S(2)}) collective-permute-start(bf16[2,8,16,128]{3,2,1,0:T(8,128)(2,1)S(1)} %get-tuple-element.78), channel_id=1, source_target_pairs={{0,1},{1,0},{2,3},{3,2},{4,5},{5,4},{6,7},{7,6},{8,9},{9,8},{10,11... | collective-permute-start | bytes 196616 | tf_op jit(solution)/shard_map/ppermute | solution.py:308
  26.6 2.2 %collective-permute-start.9 = (bf16[2,8,16,128]{3,2,1,0:T(8,128)(2,1)S(1)}, bf16[2,8,16,128]{3,2,1,0:T(8,128)(2,1)S(1)}, u32[]{:S(2)}, u32[]{:S(2)}) collective-permute-start(bf16[2,8,16,128]{3,2,1,0:T(8,128)(2,1)S(1)} %get-tuple-element.77), channel_id=1, source_target_pairs={{0,4},{1,5},{2,6},{3,7},{4,0},{5,1},{6,2},{7,3},{8,12},{9,13},{10,... | collective-permute-start | bytes 196616 | tf_op jit(solution)/shard_map/ppermute | solution.py:308
  29.5 2.2 %collective-permute-done.8.refs_1_ = bf16[2,8,16,128]{3,2,1,0:T(8,128)(2,1)S(1)} collective-permute-done((bf16[2,8,16,128]{3,2,1,0:T(8,128)(2,1)S(1)}, bf16[2,8,16,128]{3,2,1,0:T(8,128)(2,1)S(1)}, u32[]{:S(2)}, u32[]{:S(2)}) %collective-permute-start.8) | collective-permute-done | bytes 65568 | tf_op jit(solution)/shard_map/ppermute | solution.py:308
  32.0 1.4 %shard_map.87 = (bf16[4,16,16,128]{3,2,1,0:T(8,128)(2,1)S(1)}, bf16[4,16,16,128]{3,2,1,0:T(8,128)(2,1)S(1)}, f32[128,1024]{1,0:T(8,128)S(1)}, bf16[128,1024]{1,0:T(8,128)(2,1)S(1)}) custom-call(f32[16,128]{1,0:T(8,128)S(1)} %get-tuple-element.53.live_ref, bf16[128,512]{1,0:T(8,128)(2,1)S(1)} %shard_map.84.weights, bf16[128,128]{1,0:T(8,128)(2,1)S(1)} %copy-done.3, ...), custom_call_target="tpu_custom_call" | custom-call | bytes 2793472 | tf_op jit(solution)/shard_map/pallas_call | solution.py:285
  33.5 1.5 %collective-permute-done.11.got_ref.refs_1_ = bf16[4,16,16,128]{3,2,1,0:T(8,128)(2,1)S(1)} collective-permute-done((bf16[4,16,16,128]{3,2,1,0:T(8,128)(2,1)S(1)}, bf16[4,16,16,128]{3,2,1,0:T(8,128)(2,1)S(1)}, u32[]{:S(2)}, u32[]{:S(2)}) %collective-permute-start.11) | collective-permute-done | bytes 262176 | tf_op jit(solution)/shard_map/ppermute | solution.py:308
  35.0 1.6 %collective-permute-start.12 = (bf16[2,16,16,128]{3,2,1,0:T(8,128)(2,1)S(1)}, bf16[2,16,16,128]{3,2,1,0:T(8,128)(2,1)S(1)}, u32[]{:S(2)}, u32[]{:S(2)}) collective-permute-start(bf16[2,16,16,128]{3,2,1,0:T(8,128)(2,1)S(1)} %get-tuple-element.83), channel_id=1, source_target_pairs={{0,5},{1,4},{2,7},{3,6},{4,1},{5,0},{6,3},{7,2},{8,13},{9,12},{10,... | collective-permute-start | bytes 393224 | tf_op jit(solution)/shard_map/ppermute | solution.py:308
  38.8 3.5 %collective-permute-done.12.refs_2_ = bf16[2,16,16,128]{3,2,1,0:T(8,128)(2,1)S(1)} collective-permute-done((bf16[2,16,16,128]{3,2,1,0:T(8,128)(2,1)S(1)}, bf16[2,16,16,128]{3,2,1,0:T(8,128)(2,1)S(1)}, u32[]{:S(2)}, u32[]{:S(2)}) %collective-permute-start.12) | collective-permute-done | bytes 131104 | tf_op jit(solution)/shard_map/ppermute | solution.py:308
  42.3 1.6 %collective-permute-done.13.refs_3_ = bf16[2,16,16,128]{3,2,1,0:T(8,128)(2,1)S(1)} collective-permute-done((bf16[2,16,16,128]{3,2,1,0:T(8,128)(2,1)S(1)}, bf16[2,16,16,128]{3,2,1,0:T(8,128)(2,1)S(1)}, u32[]{:S(2)}, u32[]{:S(2)}) %collective-permute-start.13) | collective-permute-done | bytes 131104 | tf_op jit(solution)/shard_map/ppermute | solution.py:308
  44.9 1.5 %collective-permute-done.15.got_ref.refs_1_ = bf16[8,8,16,128]{3,2,1,0:T(8,128)(2,1)S(1)} collective-permute-done((bf16[8,8,16,128]{3,2,1,0:T(8,128)(2,1)S(1)}, bf16[8,8,16,128]{3,2,1,0:T(8,128)(2,1)S(1)}, u32[]{:S(2)}, u32[]{:S(2)}) %collective-permute-start.15) | collective-permute-done | bytes 262176 | tf_op jit(solution)/shard_map/ppermute | solution.py:308
  46.5 1.8 %collective-permute-start.16 = (bf16[2,8,16,128]{3,2,1,0:T(8,128)(2,1)S(1)}, bf16[2,8,16,128]{3,2,1,0:T(8,128)(2,1)S(1)}, u32[]{:S(2)}, u32[]{:S(2)}) collective-permute-start(bf16[2,8,16,128]{3,2,1,0:T(8,128)(2,1)S(1)} %get-tuple-element.94), channel_id=1, source_target_pairs={{0,13},{1,12},{2,15},{3,14},{4,9},{5,8},{6,11},{7,10},{8,5},{9,4},... | collective-permute-start | bytes 196616 | tf_op jit(solution)/shard_map/ppermute | solution.py:308
  48.3 2.5 %collective-permute-start.17 = (bf16[2,8,16,128]{3,2,1,0:T(8,128)(2,1)S(1)}, bf16[2,8,16,128]{3,2,1,0:T(8,128)(2,1)S(1)}, u32[]{:S(2)}, u32[]{:S(2)}) collective-permute-start(bf16[2,8,16,128]{3,2,1,0:T(8,128)(2,1)S(1)} %get-tuple-element.95), channel_id=1, source_target_pairs={{0,12},{1,13},{2,14},{3,15},{4,8},{5,9},{6,10},{7,11},{8,4},{9,5},... | collective-permute-start | bytes 196616 | tf_op jit(solution)/shard_map/ppermute | solution.py:308
  50.8 2.8 %collective-permute-start.19 = (bf16[2,8,16,128]{3,2,1,0:T(8,128)(2,1)S(1)}, bf16[2,8,16,128]{3,2,1,0:T(8,128)(2,1)S(1)}, u32[]{:S(2)}, u32[]{:S(2)}) collective-permute-start(bf16[2,8,16,128]{3,2,1,0:T(8,128)(2,1)S(1)} %get-tuple-element.97), channel_id=1, source_target_pairs={{0,9},{1,8},{2,11},{3,10},{4,13},{5,12},{6,15},{7,14},{8,1},{9,0},... | collective-permute-start | bytes 196616 | tf_op jit(solution)/shard_map/ppermute | solution.py:308
  54.2 2.5 %collective-permute-start.21 = (bf16[2,8,16,128]{3,2,1,0:T(8,128)(2,1)S(1)}, bf16[2,8,16,128]{3,2,1,0:T(8,128)(2,1)S(1)}, u32[]{:S(2)}, u32[]{:S(2)}) collective-permute-start(bf16[2,8,16,128]{3,2,1,0:T(8,128)(2,1)S(1)} %get-tuple-element.99), channel_id=1, source_target_pairs={{0,4},{1,5},{2,6},{3,7},{4,0},{5,1},{6,2},{7,3},{8,12},{9,13},{10,... | collective-permute-start | bytes 196616 | tf_op jit(solution)/shard_map/ppermute | solution.py:308
  57.7 3.6 %collective-permute-done.19.refs_5_ = bf16[2,8,16,128]{3,2,1,0:T(8,128)(2,1)S(1)} collective-permute-done((bf16[2,8,16,128]{3,2,1,0:T(8,128)(2,1)S(1)}, bf16[2,8,16,128]{3,2,1,0:T(8,128)(2,1)S(1)}, u32[]{:S(2)}, u32[]{:S(2)}) %collective-permute-start.19) | collective-permute-done | bytes 65568 | tf_op jit(solution)/shard_map/ppermute | solution.py:308
  61.5 1.5 %shard_map.92 = f32[1024,128]{1,0:T(8,128)} custom-call(f32[128,1024]{1,0:T(8,128)S(1)} %get-tuple-element.79.middle_ref, f32[128,1024]{1,0:T(8,128)S(1)} %shard_map.88.gating_ref, bf16[128,128]{1,0:T(8,128)(2,1)S(1)} %copy-done.1, bf16[8,8,16,128]{3,2,1,0:T(8,128)(2,1)S(1)} %get-tuple-element.92.keep_ref.refs_0_, ...), custom_call_target="tpu_custom_call" | custom-call | bytes 2588672 | tf_op jit(solution)/shard_map/pallas_call | solution.py:285
  (43 shorter events, 9.6 us)
Async XLA Ops:
  2.2 9.9 %collective-permute-start.3 = (bf16[2,8,16,128]{3,2,1,0:T(8,128)(2,1)S(1)}, bf16[2,8,16,128]{3,2,1,0:T(8,128)(2,1)S(1)}, u32[]{:S(2)}, u32[]{:S(2)}) collective-permute-start(bf16[2,8,16,128]{3,2,1,0:T(8,128)(2,1)S(1)} %get-tuple-element.59), channel_id=1, source_target_pairs={{0,8},{1,9},{2,10},{3,11},{4,12},{5,13},{6,14},{7,15},{8,0},{9,1},... | collective-permute-start | bytes 196616 | tf_op jit(solution)/shard_map/ppermute | solution.py:308
  6.3 8.7 %collective-permute-start.4 = (bf16[2,8,16,128]{3,2,1,0:T(8,128)(2,1)S(1)}, bf16[2,8,16,128]{3,2,1,0:T(8,128)(2,1)S(1)}, u32[]{:S(2)}, u32[]{:S(2)}) collective-permute-start(bf16[2,8,16,128]{3,2,1,0:T(8,128)(2,1)S(1)} %get-tuple-element.60), channel_id=1, source_target_pairs={{0,13},{1,12},{2,15},{3,14},{4,9},{5,8},{6,11},{7,10},{8,5},{9,4},... | collective-permute-start | bytes 196616 | tf_op jit(solution)/shard_map/ppermute | solution.py:308
  8.6 13.8 %collective-permute-start = (bf16[2,2,8,16,128]{4,3,2,1,0:T(8,128)(2,1)S(1)}, bf16[2,2,8,16,128]{4,3,2,1,0:T(8,128)(2,1)S(1)}, u32[]{:S(2)}, u32[]{:S(2)}) collective-permute-start(bf16[2,2,8,16,128]{4,3,2,1,0:T(8,128)(2,1)S(1)} %get-tuple-element.56), channel_id=1, source_target_pairs={{0,5},{1,4},{2,7},{3,6},{4,1},{5,0},{6,3},{7,2},{8,13},{9,12},{10,... | collective-permute-start | bytes 393224 | tf_op jit(solution)/shard_map/ppermute | solution.py:308
  8.8 13.5 %collective-permute-start.1 = (bf16[2,2,8,16,128]{4,3,2,1,0:T(8,128)(2,1)S(1)}, bf16[2,2,8,16,128]{4,3,2,1,0:T(8,128)(2,1)S(1)}, u32[]{:S(2)}, u32[]{:S(2)}) collective-permute-start(bf16[2,2,8,16,128]{4,3,2,1,0:T(8,128)(2,1)S(1)} %get-tuple-element.57), channel_id=1, source_target_pairs={{0,4},{1,5},{2,6},{3,7},{4,0},{5,1},{6,2},{7,3},{8,12},{9,13},{10,... | collective-permute-start | bytes 393224 | tf_op jit(solution)/shard_map/ppermute | solution.py:308
  10.6 11.8 %collective-permute-start.2 = (bf16[2,2,8,16,128]{4,3,2,1,0:T(8,128)(2,1)S(1)}, bf16[2,2,8,16,128]{4,3,2,1,0:T(8,128)(2,1)S(1)}, u32[]{:S(2)}, u32[]{:S(2)}) collective-permute-start(bf16[2,2,8,16,128]{4,3,2,1,0:T(8,128)(2,1)S(1)} %get-tuple-element.58), channel_id=1, source_target_pairs={{0,1},{1,0},{2,3},{3,2},{4,5},{5,4},{6,7},{7,6},{8,9},{9,8},{10,11... | collective-permute-start | bytes 393224 | tf_op jit(solution)/shard_map/ppermute | solution.py:308
  12.1 8.3 %collective-permute-start.5 = (bf16[2,8,16,128]{3,2,1,0:T(8,128)(2,1)S(1)}, bf16[2,8,16,128]{3,2,1,0:T(8,128)(2,1)S(1)}, u32[]{:S(2)}, u32[]{:S(2)}) collective-permute-start(bf16[2,8,16,128]{3,2,1,0:T(8,128)(2,1)S(1)} %get-tuple-element.61), channel_id=1, source_target_pairs={{0,12},{1,13},{2,14},{3,15},{4,8},{5,9},{6,10},{7,11},{8,4},{9,5},... | collective-permute-start | bytes 196616 | tf_op jit(solution)/shard_map/ppermute | solution.py:308
  15.0 7.3 %collective-permute-start.6 = (bf16[2,8,16,128]{3,2,1,0:T(8,128)(2,1)S(1)}, bf16[2,8,16,128]{3,2,1,0:T(8,128)(2,1)S(1)}, u32[]{:S(2)}, u32[]{:S(2)}) collective-permute-start(bf16[2,8,16,128]{3,2,1,0:T(8,128)(2,1)S(1)} %get-tuple-element.62), channel_id=1, source_target_pairs={{0,9},{1,8},{2,11},{3,10},{4,13},{5,12},{6,15},{7,14},{8,1},{9,0},... | collective-permute-start | bytes 196616 | tf_op jit(solution)/shard_map/ppermute | solution.py:308
  22.4 2.0 %collective-permute-start.7 = (bf16[8,2,8,16,128]{4,3,2,1,0:T(8,128)(2,1)S(1)}, bf16[8,2,8,16,128]{4,3,2,1,0:T(8,128)(2,1)S(1)}, u32[]{:S(2)}, u32[]{:S(2)}) collective-permute-start(bf16[8,2,8,16,128]{4,3,2,1,0:T(8,128)(2,1)S(1)} %shard_map.85), channel_id=1, source_target_pairs={{0,2},{1,3},{2,0},{3,1},{4,6},{5,7},{6,4},{7,5},{8,10},{9,11},{10,... | collective-permute-start | bytes 1572872 | tf_op jit(solution)/shard_map/ppermute | solution.py:308
  25.2 4.3 %collective-permute-start.10 = (bf16[2,8,16,128]{3,2,1,0:T(8,128)(2,1)S(1)}, bf16[2,8,16,128]{3,2,1,0:T(8,128)(2,1)S(1)}, u32[]{:S(2)}, u32[]{:S(2)}) collective-permute-start(bf16[2,8,16,128]{3,2,1,0:T(8,128)(2,1)S(1)} %get-tuple-element.78), channel_id=1, source_target_pairs={{0,1},{1,0},{2,3},{3,2},{4,5},{5,4},{6,7},{7,6},{8,9},{9,8},{10,11... | collective-permute-start | bytes 196616 | tf_op jit(solution)/shard_map/ppermute | solution.py:308
  26.3 5.5 %collective-permute-start.8 = (bf16[2,8,16,128]{3,2,1,0:T(8,128)(2,1)S(1)}, bf16[2,8,16,128]{3,2,1,0:T(8,128)(2,1)S(1)}, u32[]{:S(2)}, u32[]{:S(2)}) collective-permute-start(bf16[2,8,16,128]{3,2,1,0:T(8,128)(2,1)S(1)} %get-tuple-element.76), channel_id=1, source_target_pairs={{0,5},{1,4},{2,7},{3,6},{4,1},{5,0},{6,3},{7,2},{8,13},{9,12},{10,... | collective-permute-start | bytes 196616 | tf_op jit(solution)/shard_map/ppermute | solution.py:308
  26.6 5.4 %collective-permute-start.9 = (bf16[2,8,16,128]{3,2,1,0:T(8,128)(2,1)S(1)}, bf16[2,8,16,128]{3,2,1,0:T(8,128)(2,1)S(1)}, u32[]{:S(2)}, u32[]{:S(2)}) collective-permute-start(bf16[2,8,16,128]{3,2,1,0:T(8,128)(2,1)S(1)} %get-tuple-element.77), channel_id=1, source_target_pairs={{0,4},{1,5},{2,6},{3,7},{4,0},{5,1},{6,2},{7,3},{8,12},{9,13},{10,... | collective-permute-start | bytes 196616 | tf_op jit(solution)/shard_map/ppermute | solution.py:308
  33.4 1.6 %collective-permute-start.11 = (bf16[4,16,16,128]{3,2,1,0:T(8,128)(2,1)S(1)}, bf16[4,16,16,128]{3,2,1,0:T(8,128)(2,1)S(1)}, u32[]{:S(2)}, u32[]{:S(2)}) collective-permute-start(bf16[4,16,16,128]{3,2,1,0:T(8,128)(2,1)S(1)} %get-tuple-element.82), channel_id=1, source_target_pairs={{0,2},{1,3},{2,0},{3,1},{4,6},{5,7},{6,4},{7,5},{8,10},{9,11},{10,... | collective-permute-start | bytes 786440 | tf_op jit(solution)/shard_map/ppermute | solution.py:308
  35.0 7.3 %collective-permute-start.12 = (bf16[2,16,16,128]{3,2,1,0:T(8,128)(2,1)S(1)}, bf16[2,16,16,128]{3,2,1,0:T(8,128)(2,1)S(1)}, u32[]{:S(2)}, u32[]{:S(2)}) collective-permute-start(bf16[2,16,16,128]{3,2,1,0:T(8,128)(2,1)S(1)} %get-tuple-element.83), channel_id=1, source_target_pairs={{0,5},{1,4},{2,7},{3,6},{4,1},{5,0},{6,3},{7,2},{8,13},{9,12},{10,... | collective-permute-start | bytes 393224 | tf_op jit(solution)/shard_map/ppermute | solution.py:308
  36.6 7.3 %collective-permute-start.13 = (bf16[2,16,16,128]{3,2,1,0:T(8,128)(2,1)S(1)}, bf16[2,16,16,128]{3,2,1,0:T(8,128)(2,1)S(1)}, u32[]{:S(2)}, u32[]{:S(2)}) collective-permute-start(bf16[2,16,16,128]{3,2,1,0:T(8,128)(2,1)S(1)} %get-tuple-element.84), channel_id=1, source_target_pairs={{0,4},{1,5},{2,6},{3,7},{4,0},{5,1},{6,2},{7,3},{8,12},{9,13},{10,... | collective-permute-start | bytes 393224 | tf_op jit(solution)/shard_map/ppermute | solution.py:308
  37.6 6.8 %collective-permute-start.14 = (bf16[2,16,16,128]{3,2,1,0:T(8,128)(2,1)S(1)}, bf16[2,16,16,128]{3,2,1,0:T(8,128)(2,1)S(1)}, u32[]{:S(2)}, u32[]{:S(2)}) collective-permute-start(bf16[2,16,16,128]{3,2,1,0:T(8,128)(2,1)S(1)} %get-tuple-element.85), channel_id=1, source_target_pairs={{0,1},{1,0},{2,3},{3,2},{4,5},{5,4},{6,7},{7,6},{8,9},{9,8},{10,11... | collective-permute-start | bytes 393224 | tf_op jit(solution)/shard_map/ppermute | solution.py:308
  44.9 1.6 %collective-permute-start.15 = (bf16[8,8,16,128]{3,2,1,0:T(8,128)(2,1)S(1)}, bf16[8,8,16,128]{3,2,1,0:T(8,128)(2,1)S(1)}, u32[]{:S(2)}, u32[]{:S(2)}) collective-permute-start(bf16[8,8,16,128]{3,2,1,0:T(8,128)(2,1)S(1)} %get-tuple-element.93), channel_id=1, source_target_pairs={{0,2},{1,3},{2,0},{3,1},{4,6},{5,7},{6,4},{7,5},{8,10},{9,11},{10,... | collective-permute-start | bytes 786440 | tf_op jit(solution)/shard_map/ppermute | solution.py:308
  46.5 15.0 %copy-start.1 = (bf16[128,128]{1,0:T(8,128)(2,1)S(1)}, bf16[128,128]{1,0:T(8,128)(2,1)}, u32[]{:S(2)}) copy-start(bf16[128,128]{1,0:T(8,128)(2,1)} %final_ref.3) | copy-start | bytes 98308
  46.5 7.7 %collective-permute-start.16 = (bf16[2,8,16,128]{3,2,1,0:T(8,128)(2,1)S(1)}, bf16[2,8,16,128]{3,2,1,0:T(8,128)(2,1)S(1)}, u32[]{:S(2)}, u32[]{:S(2)}) collective-permute-start(bf16[2,8,16,128]{3,2,1,0:T(8,128)(2,1)S(1)} %get-tuple-element.94), channel_id=1, source_target_pairs={{0,13},{1,12},{2,15},{3,14},{4,9},{5,8},{6,11},{7,10},{8,5},{9,4},... | collective-permute-start | bytes 196616 | tf_op jit(solution)/shard_map/ppermute | solution.py:308
  48.3 8.4 %collective-permute-start.17 = (bf16[2,8,16,128]{3,2,1,0:T(8,128)(2,1)S(1)}, bf16[2,8,16,128]{3,2,1,0:T(8,128)(2,1)S(1)}, u32[]{:S(2)}, u32[]{:S(2)}) collective-permute-start(bf16[2,8,16,128]{3,2,1,0:T(8,128)(2,1)S(1)} %get-tuple-element.95), channel_id=1, source_target_pairs={{0,12},{1,13},{2,14},{3,15},{4,8},{5,9},{6,10},{7,11},{8,4},{9,5},... | collective-permute-start | bytes 196616 | tf_op jit(solution)/shard_map/ppermute | solution.py:308
  50.8 6.9 %collective-permute-start.18 = (bf16[2,8,16,128]{3,2,1,0:T(8,128)(2,1)S(1)}, bf16[2,8,16,128]{3,2,1,0:T(8,128)(2,1)S(1)}, u32[]{:S(2)}, u32[]{:S(2)}) collective-permute-start(bf16[2,8,16,128]{3,2,1,0:T(8,128)(2,1)S(1)} %get-tuple-element.96), channel_id=1, source_target_pairs={{0,5},{1,4},{2,7},{3,6},{4,1},{5,0},{6,3},{7,2},{8,13},{9,12},{10,... | collective-permute-start | bytes 196616 | tf_op jit(solution)/shard_map/ppermute | solution.py:308
  50.8 10.5 %collective-permute-start.19 = (bf16[2,8,16,128]{3,2,1,0:T(8,128)(2,1)S(1)}, bf16[2,8,16,128]{3,2,1,0:T(8,128)(2,1)S(1)}, u32[]{:S(2)}, u32[]{:S(2)}) collective-permute-start(bf16[2,8,16,128]{3,2,1,0:T(8,128)(2,1)S(1)} %get-tuple-element.97), channel_id=1, source_target_pairs={{0,9},{1,8},{2,11},{3,10},{4,13},{5,12},{6,15},{7,14},{8,1},{9,0},... | collective-permute-start | bytes 196616 | tf_op jit(solution)/shard_map/ppermute | solution.py:308
  53.6 7.9 %collective-permute-start.20 = (bf16[2,8,16,128]{3,2,1,0:T(8,128)(2,1)S(1)}, bf16[2,8,16,128]{3,2,1,0:T(8,128)(2,1)S(1)}, u32[]{:S(2)}, u32[]{:S(2)}) collective-permute-start(bf16[2,8,16,128]{3,2,1,0:T(8,128)(2,1)S(1)} %get-tuple-element.98), channel_id=1, source_target_pairs={{0,8},{1,9},{2,10},{3,11},{4,12},{5,13},{6,14},{7,15},{8,0},{9,1},... | collective-permute-start | bytes 196616 | tf_op jit(solution)/shard_map/ppermute | solution.py:308
  54.2 7.2 %collective-permute-start.21 = (bf16[2,8,16,128]{3,2,1,0:T(8,128)(2,1)S(1)}, bf16[2,8,16,128]{3,2,1,0:T(8,128)(2,1)S(1)}, u32[]{:S(2)}, u32[]{:S(2)}) collective-permute-start(bf16[2,8,16,128]{3,2,1,0:T(8,128)(2,1)S(1)} %get-tuple-element.99), channel_id=1, source_target_pairs={{0,4},{1,5},{2,6},{3,7},{4,0},{5,1},{6,2},{7,3},{8,12},{9,13},{10,... | collective-permute-start | bytes 196616 | tf_op jit(solution)/shard_map/ppermute | solution.py:308
  56.7 4.8 %collective-permute-start.22 = (bf16[2,8,16,128]{3,2,1,0:T(8,128)(2,1)S(1)}, bf16[2,8,16,128]{3,2,1,0:T(8,128)(2,1)S(1)}, u32[]{:S(2)}, u32[]{:S(2)}) collective-permute-start(bf16[2,8,16,128]{3,2,1,0:T(8,128)(2,1)S(1)} %get-tuple-element.100), channel_id=1, source_target_pairs={{0,1},{1,0},{2,3},{3,2},{4,5},{5,4},{6,7},{7,6},{8,9},{9,8},{10,11... | collective-permute-start | bytes 196616 | tf_op jit(solution)/shard_map/ppermute | solution.py:308
  (4 other events, 12.9 us)

commit v9 on v8

--- a/solution.py
+++ b/solution.py
@@ -29,17 +29,37 @@
     return lax.dot_general(weight, values, (((0,), (0,)), ((), ())), preferred_element_type=F32)
 
 
-def side_by_side(proj_ref, wide, weights, order):
+def panels_of(proj_ref, wide, channels):
+    wide[...] = proj_ref[...].astype(F32)
+    return [wide[pl.ds(n, channels, stride=4), :] for n in range(4)]
+
+
+def first_weights(proj_ref, wide, weights):
     channels, hidden = weights.shape[0], weights.shape[1] // 4
-    wide[...] = proj_ref[...].astype(F32)
-    col = lax.axis_index("col")
-    for n in range(4):
-        if order == "panels":
-            panel = wide[pl.ds(n + 2 * col if n < 2 else n - 2 * col, channels, stride=4), :]
-        else:
-            panel = wide[pl.ds(n, channels, stride=4), :]
-            panel = jnp.where(col == 1, pltpu.roll(panel, hidden // 2, 1), panel)
+    odd = lax.axis_index("col") == 1
+    for n, panel in enumerate(panels_of(proj_ref, wide, channels)):
+        panel = jnp.where(odd, pltpu.roll(panel, hidden // 2, 1), panel)
         weights[:, n * hidden : (n + 1) * hidden] = panel.astype(BF16)
+
+
+def second_weights_kernel(proj_ref, weights, wide):
+    channels, hidden = weights.shape[0], weights.shape[1] // 4
+    quarter = hidden // 4
+    odd = lax.axis_index("col") == 1
+    upper = lax.axis_index("row") % 2 == 1
+    a, a_gate, b, b_gate = panels_of(proj_ref, wide, channels)
+    panels = [jnp.where(odd, b, a), jnp.where(odd, b_gate, a_gate), jnp.where(odd, a, b), jnp.where(odd, a_gate, b_gate)]
+    lane = lax.broadcasted_iota(jnp.int32, (channels, hidden), 1)
+    kept, given = [], []
+    for panel in panels:
+        shifted = pltpu.roll(panel, hidden - quarter, 1)
+        lower_part = jnp.where(lane < quarter, panel, shifted)
+        upper_part = jnp.where(lane < quarter, shifted, pltpu.roll(panel, hidden // 2, 1))
+        kept.append(jnp.where(upper, upper_part, lower_part))
+        given.append(jnp.where(upper, lower_part, upper_part))
+    for n, (x, y) in enumerate(((kept[0], kept[1]), (kept[2], kept[3]), (given[0], given[1]), (given[2], given[3]))):
+        both = jnp.where(lane < hidden // 2, x, pltpu.roll(y, hidden // 2, 1))
+        weights[:, n * hidden : (n + 1) * hidden] = both.astype(BF16)
 
 
 def live_tile(mask_ref, rows, cols):
@@ -109,12 +129,23 @@
     return lax.axis_index("row") * 2 + lax.axis_index("col")
 
 
+def within_half(index):
+    return index & (NEAR - 1)
+
+
+def chip_of(index):
+    return (index >> 1) & 2 | index & 1
+
+
+def by_owner(index):
+    return index & NEAR | (index & SIBLING) << 1 | chip_of(index)
+
+
 def hand_out(tiles, steps, keep_ref, give_ref):
     me = own_index()
-    count = tiles.shape[0]
     for n, step in enumerate(steps):
-        keep_ref[n] = tiles[(me ^ step) % count]
-        give_ref[n] = tiles[(me ^ step ^ SIBLING) % count]
+        keep_ref[n] = tiles[me ^ step]
+        give_ref[n] = tiles[me ^ (step ^ SIBLING)]
 
 
 def forward_kernel(keep_ref, got_ref, *out_refs):
@@ -123,34 +154,25 @@
         out_ref[1] = got_ref[n + 1]
 
 
-def take_in(refs, steps, tiles):
+def take_in(refs, steps, tiles, place):
     keep_ref, got_ref, *moved_refs = refs
-    me = own_index()
-    count = tiles.shape[0]
-    tiles[me % count] = keep_ref[0]
-    tiles[(me ^ SIBLING) % count] = got_ref[0]
+    me = place(own_index())
+    tiles[me] = keep_ref[0]
+    tiles[me ^ place(SIBLING)] = got_ref[0]
     for step, moved_ref in zip(steps[1:], moved_refs):
-        tiles[(me ^ step) % count] = moved_ref[0]
-        tiles[(me ^ step ^ SIBLING) % count] = moved_ref[1]
-
-
-def chip_blocks(tiles, index):
-    base = (index % tiles.shape[0]) & ~SIBLING
+        tiles[me ^ place(step)] = moved_ref[0]
+        tiles[me ^ place(step ^ SIBLING)] = moved_ref[1]
+
+
+def chip_blocks(me, step):
+    base = (within_half(me) & ~SIBLING) ^ (within_half(step) & ~SIBLING)
     return base, base | SIBLING
-
-
-def chip_of(index):
-    return (index // 4 % 2) * 2 + index % 2
 
 
 def all_b_kernel(*refs):
     *came_refs, out_ref = refs
     for n, ref in enumerate(came_refs):
         out_ref[n] = ref[1] if n < CHIPS else ref[...]
-
-
-def second_weights_kernel(proj_ref, weights, wide):
-    side_by_side(proj_ref, wide, weights, "panels")
 
 
 def first_kernel(rows, cols, pair_hbm, mask_hbm, proj_hbm, *refs):
@@ -162,7 +184,7 @@
     coming = copies([(pair_hbm.at[at], pair_ref.at[at]) for at in chunks] + whole, done)
     for copy in coming[len(chunks) :]:
         copy.wait()
-    side_by_side(proj_ref, wide, weights, "halves")
+    first_weights(proj_ref, wide, weights)
     live = live_tile(mask_ref, rows, cols)
     live_ref[...] = live
     for copy in coming[: len(chunks)]:
@@ -171,39 +193,48 @@
     pair_t_ref[...] = pair
     normed = over_channels(pair).astype(BF16)
     normed_ref[...] = normed
+    me = own_index()
     for p, values in enumerate(panels(normed, weights)):
         half = values.shape[0] // 2
         by_near[...] = paired(values[:half], values[half:], live, cols).reshape(by_near.shape)
         for step, both_ref, b_ref in zip(NEAR_STEPS, both_refs, b_refs):
-            for n, block in enumerate(chip_blocks(by_near, own_index() ^ step)):
+            for n, block in enumerate(chip_blocks(me, step)):
                 both_ref[p, n] = by_near[block]
                 if p == 1:
                     b_ref[n] = by_near[block]
 
 
+def to_chips(normed, weights, live, cols, by_chip, out_ref):
+    tiles = paired(*panels(normed, weights), live, cols)
+    per_chip = tiles.shape[0] // 2 // CHIPS
+    for d in range(CHIPS):
+        by_chip[d, :per_chip] = tiles[d * per_chip : (d + 1) * per_chip]
+        by_chip[d, per_chip:] = tiles[(CHIPS + d) * per_chip : (CHIPS + d + 1) * per_chip]
+    me = chip_of(own_index())
+    for n, step in enumerate(NEAR_STEPS):
+        out_ref[n] = by_chip[me ^ chip_of(step)]
+
+
 def middle_kernel(rows, cols, live_ref, weights, final_ref, pair_t_ref, gating_ref, *refs):
-    *came_refs, keep_ref, give_ref, middle_ref, normed_ref, came, by_near = refs
+    *came_refs, give_ref, middle_ref, normed_ref, came, by_chip = refs
+    me = own_index()
     for step, ref in zip(NEAR_STEPS, came_refs):
-        for n, block in enumerate(chip_blocks(came, own_index() ^ step)):
+        for n, block in enumerate(chip_blocks(me, step)):
             came[block] = ref[n]
     middle = pair_t_ref[...] + gating_ref[...] * projected(came, final_ref, rows, cols)
     middle_ref[...] = middle
     normed = over_channels(middle).astype(BF16)
     normed_ref[...] = normed
-    a, b = panels(normed, weights)
-    hidden = a.shape[0]
-    by_hidden = paired(a, b, live_ref[...], cols)
-    devices, per_device = by_near.shape[:2]
-    half = per_device // 2
-    for d in range(devices):
-        by_near[d, :half] = by_hidden[d * half : (d + 1) * half]
-        by_near[d, half:] = by_hidden[hidden // 2 + d * half : hidden // 2 + (d + 1) * half]
-    hand_out(by_near, NEAR_STEPS, keep_ref, give_ref)
+    to_chips(normed, weights[:, weights.shape[1] // 2 :], live_ref[...], cols, by_chip, give_ref)
+
+
+def keep_kernel(cols, live_ref, weights, normed_ref, keep_ref, by_chip):
+    to_chips(normed_ref[...], weights[:, : weights.shape[1] // 2], live_ref[...], cols, by_chip, keep_ref)
 
 
 def last_kernel(rows, cols, middle_ref, gating_ref, final_ref, *refs):
     *came_refs, out_hbm, came, out_ref, done = refs
-    take_in(came_refs, ALL_STEPS, came)
+    take_in(came_refs, ALL_STEPS, came, by_owner)
     change = projected(came, final_ref, rows, cols)
     leaving = []
     for n in range(rows * cols // CHUNK):
@@ -237,11 +268,11 @@
     me = own_index()
     one = a_ref.shape[1:]
     for n, step in enumerate(NEAR_STEPS):
-        a_ref[chip_of(me ^ step)] = both_refs[n][0].reshape(one)
+        a_ref[chip_of(me) ^ chip_of(step)] = both_refs[n][0].reshape(one)
         b_ref[me ^ step] = both_refs[n][1].reshape(one)
-        b_ref[me ^ step ^ SIBLING] = sibling_ref[n].reshape(one)
-        b_ref[me ^ step ^ NEAR] = far_refs[n][...].reshape(one)
-        b_ref[me ^ step ^ NEAR ^ SIBLING] = sibling_ref[CHIPS + n].reshape(one)
+        b_ref[me ^ (step ^ SIBLING)] = sibling_ref[n].reshape(one)
+        b_ref[me ^ (step ^ NEAR)] = far_refs[n][...].reshape(one)
+        b_ref[me ^ (step ^ NEAR ^ SIBLING)] = sibling_ref[CHIPS + n].reshape(one)
     for q in range(msg_ref.shape[1]):
         even, odd = both(a_ref, q)
         low = low_of(even, cols)
@@ -254,12 +285,12 @@
         low = low_of(x, cols)
         put(jnp.where(low, x, pltpu.roll(y, cols, 1)), jnp.where(low, pltpu.roll(x, cols, 1), y), msg_ref, q)
     for step, out_ref in zip(NEAR_STEPS, out_refs):
-        out_ref[...] = msg_ref[chip_of(me ^ step)].reshape(out_ref.shape)
+        out_ref[...] = msg_ref[chip_of(me) ^ chip_of(step)].reshape(out_ref.shape)
 
 
 def incoming_kernel(cols, *refs):
     *came_refs, keep_ref, give_ref, recv_ref, msg_ref = refs
-    take_in(came_refs, NEAR_STEPS, recv_ref)
+    take_in(came_refs, NEAR_STEPS, recv_ref, within_half)
     half = msg_ref.shape[1]
 
     def mixed(e):
@@ -337,7 +368,6 @@
     pairs = hidden // NEAR // 2
     per_chip = (messages(2, pairs),) * CHIPS
     both_per_chip = (shape((2, 2, pairs, rows, LANES), BF16),) * CHIPS
-    wide_near_steps = (messages(len(NEAR_STEPS), 2 * pairs),) * 2
     all_steps = (messages(len(ALL_STEPS), pairs),) * 2
     gate = call(gate_kernel, [plane], flops=2 * channels * channels * positions, transcendentals=channels * positions)
 
@@ -357,11 +387,14 @@
     own, *others = call(functools.partial(outgoing_kernel, cols), per_chip, scratch)(*came)
     came = (own, *(swap(block, step) for block, step in zip(others, NEAR_STEPS[1:])))
 
-    scratch = [scratch_tiles(NEAR, pairs), scratch_tiles(NEAR, 2 * pairs)]
-    outs = (*wide_near_steps, plane, half_plane)
-    keep, give, middle, normed = call(functools.partial(middle_kernel, rows, cols), outs, scratch)(
+    chip_tiles = scratch_tiles(CHIPS, 2 * pairs)
+    half_step = messages(len(NEAR_STEPS), 2 * pairs)
+    outs = (half_step, plane, half_plane)
+    give, middle, normed = call(functools.partial(middle_kernel, rows, cols), outs, [scratch_tiles(NEAR, pairs), chip_tiles])(
         live, weights, out_final, pair_t, gating, *came
     )
+    work = 4 * channels * hidden * positions
+    (keep,) = call(functools.partial(keep_kernel, cols), [half_step], [chip_tiles], flops=work)(live, weights, normed)
     came = exchange(keep, give, NEAR_STEPS)
     gating, came = lax.optimization_barrier((gate(normed, in_gate)[0], came))
 

time: 63.2 us -> 63 us (level)
    pallas_call x11 -> x12, Pallas kernels: 7.11 us -> 7.52 us  [run(): pl.pallas_call(kernel, out_shape=tuple(out_shape), in_specs=[hbm] * far_a...]
  transfers between devices with their start and end apart: 23 -> 23, of which waited for: 13 -> 13; matrix products, arithmetic and copies ran while one was open for 0% -> 0% of each run, Pallas kernels for 1% -> 2%
where the time goes in v9:
time: 63 us; the launch traced here: 62.8 us
  starting transfers between devices  33.1 us (53%)
  waiting for transfers between devices  20.7 us (33%)
  Pallas kernels  7.52 us (12%)
  local copies, waits for them, and re-layouts  1.29 us (2%)
    ppermute x23, starting transfers between devices, swap(): return lax.ppermute(values, axes, [(d, d ^ step) for d in range(devices)])  33.1 us
    ppermute x23, waiting for transfers between devices, swap(): return lax.ppermute(values, axes, [(d, d ^ step) for d in range(devices)])  20.7 us
    pallas_call x12, Pallas kernels, run(): pl.pallas_call(kernel, out_shape=tuple(out_shape), in_specs=[hbm] * far_a...  7.52 us
    unnamed x10, local copies, waits for them, and re-layouts  1.29 us
  transfers between devices with their start and end apart: 23, of which 13 were waited for; matrix products, arithmetic and copies ran while one was open for 0% of the time, Pallas kernels for 2%

profile of v9, /device:TPU:0, one launch (start us, length us, event | category | flops | bytes accessed | tf_op | source)
XLA Modules:
  0.0 62.8 jit_solution(11681741384181067837)
XLA Ops:
  0.0 2.2 %shard_map.82 = (bf16[2,2,8,16,128]{4,3,2,1,0:T(8,128)(2,1)S(1)}, bf16[2,2,8,16,128]{4,3,2,1,0:T(8,128)(2,1)S(1)}, bf16[2,2,8,16,128]{4,3,2,1,0:T(8,128)(2,1)S(1...) custom-call(f32[1024,128]{1,0:T(8,128)} %bitcast.6, ...), custom_call_target="tpu_custom_call" | custom-call | bytes 2236928 | tf_op jit(solution)/shard_map/pallas_call | solution.py:316
  2.2 4.1 %collective-permute-start.3 = (bf16[2,8,16,128]{3,2,1,0:T(8,128)(2,1)S(1)}, bf16[2,8,16,128]{3,2,1,0:T(8,128)(2,1)S(1)}, u32[]{:S(2)}, u32[]{:S(2)}) collective-permute-start(bf16[2,8,16,128]{3,2,1,0:T(8,128)(2,1)S(1)} %get-tuple-element.58), channel_id=1, source_target_pairs={{0,8},{1,9},{2,10},{3,11},{4,12},{5,13},{6,14},{7,15},{8,0},{9,1},... | collective-permute-start | bytes 196616 | tf_op jit(solution)/shard_map/ppermute | solution.py:339
  6.3 2.3 %collective-permute-start.4 = (bf16[2,8,16,128]{3,2,1,0:T(8,128)(2,1)S(1)}, bf16[2,8,16,128]{3,2,1,0:T(8,128)(2,1)S(1)}, u32[]{:S(2)}, u32[]{:S(2)}) collective-permute-start(bf16[2,8,16,128]{3,2,1,0:T(8,128)(2,1)S(1)} %get-tuple-element.59), channel_id=1, source_target_pairs={{0,13},{1,12},{2,15},{3,14},{4,9},{5,8},{6,11},{7,10},{8,5},{9,4},... | collective-permute-start | bytes 196616 | tf_op jit(solution)/shard_map/ppermute | solution.py:339
  8.8 1.8 %collective-permute-start.1 = (bf16[2,2,8,16,128]{4,3,2,1,0:T(8,128)(2,1)S(1)}, bf16[2,2,8,16,128]{4,3,2,1,0:T(8,128)(2,1)S(1)}, u32[]{:S(2)}, u32[]{:S(2)}) collective-permute-start(bf16[2,2,8,16,128]{4,3,2,1,0:T(8,128)(2,1)S(1)} %get-tuple-element.56), channel_id=1, source_target_pairs={{0,4},{1,5},{2,6},{3,7},{4,0},{5,1},{6,2},{7,3},{8,12},{9,13},{10,... | collective-permute-start | bytes 393224 | tf_op jit(solution)/shard_map/ppermute | solution.py:339
  10.6 1.5 %collective-permute-start.2 = (bf16[2,2,8,16,128]{4,3,2,1,0:T(8,128)(2,1)S(1)}, bf16[2,2,8,16,128]{4,3,2,1,0:T(8,128)(2,1)S(1)}, u32[]{:S(2)}, u32[]{:S(2)}) collective-permute-start(bf16[2,2,8,16,128]{4,3,2,1,0:T(8,128)(2,1)S(1)} %get-tuple-element.57), channel_id=1, source_target_pairs={{0,1},{1,0},{2,3},{3,2},{4,5},{5,4},{6,7},{7,6},{8,9},{9,8},{10,11... | collective-permute-start | bytes 393224 | tf_op jit(solution)/shard_map/ppermute | solution.py:339
  12.0 2.9 %collective-permute-start.5 = (bf16[2,8,16,128]{3,2,1,0:T(8,128)(2,1)S(1)}, bf16[2,8,16,128]{3,2,1,0:T(8,128)(2,1)S(1)}, u32[]{:S(2)}, u32[]{:S(2)}) collective-permute-start(bf16[2,8,16,128]{3,2,1,0:T(8,128)(2,1)S(1)} %get-tuple-element.60), channel_id=1, source_target_pairs={{0,12},{1,13},{2,14},{3,15},{4,8},{5,9},{6,10},{7,11},{8,4},{9,5},... | collective-permute-start | bytes 196616 | tf_op jit(solution)/shard_map/ppermute | solution.py:339
  15.0 1.8 %collective-permute-start.6 = (bf16[2,8,16,128]{3,2,1,0:T(8,128)(2,1)S(1)}, bf16[2,8,16,128]{3,2,1,0:T(8,128)(2,1)S(1)}, u32[]{:S(2)}, u32[]{:S(2)}) collective-permute-start(bf16[2,8,16,128]{3,2,1,0:T(8,128)(2,1)S(1)} %get-tuple-element.61), channel_id=1, source_target_pairs={{0,9},{1,8},{2,11},{3,10},{4,13},{5,12},{6,15},{7,14},{8,1},{9,0},... | collective-permute-start | bytes 196616 | tf_op jit(solution)/shard_map/ppermute | solution.py:339
  16.7 3.7 %collective-permute-done.5.refs_6_ = bf16[2,8,16,128]{3,2,1,0:T(8,128)(2,1)S(1)} collective-permute-done((bf16[2,8,16,128]{3,2,1,0:T(8,128)(2,1)S(1)}, bf16[2,8,16,128]{3,2,1,0:T(8,128)(2,1)S(1)}, u32[]{:S(2)}, u32[]{:S(2)}) %collective-permute-start.5) | collective-permute-done | bytes 65568 | tf_op jit(solution)/shard_map/ppermute | solution.py:339
  20.4 1.9 %collective-permute-done.6.refs_7_ = bf16[2,8,16,128]{3,2,1,0:T(8,128)(2,1)S(1)} collective-permute-done((bf16[2,8,16,128]{3,2,1,0:T(8,128)(2,1)S(1)}, bf16[2,8,16,128]{3,2,1,0:T(8,128)(2,1)S(1)}, u32[]{:S(2)}, u32[]{:S(2)}) %collective-permute-start.6) | collective-permute-done | bytes 65568 | tf_op jit(solution)/shard_map/ppermute | solution.py:339
  25.2 1.1 %collective-permute-start.10 = (bf16[2,8,16,128]{3,2,1,0:T(8,128)(2,1)S(1)}, bf16[2,8,16,128]{3,2,1,0:T(8,128)(2,1)S(1)}, u32[]{:S(2)}, u32[]{:S(2)}) collective-permute-start(bf16[2,8,16,128]{3,2,1,0:T(8,128)(2,1)S(1)} %get-tuple-element.77), channel_id=1, source_target_pairs={{0,1},{1,0},{2,3},{3,2},{4,5},{5,4},{6,7},{7,6},{8,9},{9,8},{10,11... | collective-permute-start | bytes 196616 | tf_op jit(solution)/shard_map/ppermute | solution.py:339
  26.6 2.2 %collective-permute-start.9 = (bf16[2,8,16,128]{3,2,1,0:T(8,128)(2,1)S(1)}, bf16[2,8,16,128]{3,2,1,0:T(8,128)(2,1)S(1)}, u32[]{:S(2)}, u32[]{:S(2)}) collective-permute-start(bf16[2,8,16,128]{3,2,1,0:T(8,128)(2,1)S(1)} %get-tuple-element.76), channel_id=1, source_target_pairs={{0,4},{1,5},{2,6},{3,7},{4,0},{5,1},{6,2},{7,3},{8,12},{9,13},{10,... | collective-permute-start | bytes 196616 | tf_op jit(solution)/shard_map/ppermute | solution.py:339
  29.5 2.2 %collective-permute-done.8.refs_1_ = bf16[2,8,16,128]{3,2,1,0:T(8,128)(2,1)S(1)} collective-permute-done((bf16[2,8,16,128]{3,2,1,0:T(8,128)(2,1)S(1)}, bf16[2,8,16,128]{3,2,1,0:T(8,128)(2,1)S(1)}, u32[]{:S(2)}, u32[]{:S(2)}) %collective-permute-start.8) | collective-permute-done | bytes 65568 | tf_op jit(solution)/shard_map/ppermute | solution.py:339
  32.0 1.2 %shard_map.87 = (bf16[4,16,16,128]{3,2,1,0:T(8,128)(2,1)S(1)}, f32[128,1024]{1,0:T(8,128)S(1)}, bf16[128,1024]{1,0:T(8,128)(2,1)S(1)}) custom-call(f32[16,128]{1,0:T(8,128)S(1)} %get-tuple-element.52.live_ref, bf16[128,512]{1,0:T(8,128)(2,1)S(1)} %shard_map.84.weights, bf16[128,128]{1,0:T(8,128)(2,1)S(1)} %copy-done.3, ...), custom_call_target="tpu_custom_call" | custom-call | bytes 2531328 | tf_op jit(solution)/shard_map/pallas_call | solution.py:316
  33.7 1.0 %collective-permute-done.11.got_ref.refs_1_ = bf16[4,16,16,128]{3,2,1,0:T(8,128)(2,1)S(1)} collective-permute-done((bf16[4,16,16,128]{3,2,1,0:T(8,128)(2,1)S(1)}, bf16[4,16,16,128]{3,2,1,0:T(8,128)(2,1)S(1)}, u32[]{:S(2)}, u32[]{:S(2)}) %collective-permute-start.11) | collective-permute-done | bytes 262176 | tf_op jit(solution)/shard_map/ppermute | solution.py:339
  34.8 1.6 %collective-permute-start.12 = (bf16[2,16,16,128]{3,2,1,0:T(8,128)(2,1)S(1)}, bf16[2,16,16,128]{3,2,1,0:T(8,128)(2,1)S(1)}, u32[]{:S(2)}, u32[]{:S(2)}) collective-permute-start(bf16[2,16,16,128]{3,2,1,0:T(8,128)(2,1)S(1)} %get-tuple-element.81), channel_id=1, source_target_pairs={{0,5},{1,4},{2,7},{3,6},{4,1},{5,0},{6,3},{7,2},{8,13},{9,12},{10,... | collective-permute-start | bytes 393224 | tf_op jit(solution)/shard_map/ppermute | solution.py:339
  38.6 3.5 %collective-permute-done.12.refs_2_ = bf16[2,16,16,128]{3,2,1,0:T(8,128)(2,1)S(1)} collective-permute-done((bf16[2,16,16,128]{3,2,1,0:T(8,128)(2,1)S(1)}, bf16[2,16,16,128]{3,2,1,0:T(8,128)(2,1)S(1)}, u32[]{:S(2)}, u32[]{:S(2)}) %collective-permute-start.12) | collective-permute-done | bytes 131104 | tf_op jit(solution)/shard_map/ppermute | solution.py:339
  42.1 1.6 %collective-permute-done.13.refs_3_ = bf16[2,16,16,128]{3,2,1,0:T(8,128)(2,1)S(1)} collective-permute-done((bf16[2,16,16,128]{3,2,1,0:T(8,128)(2,1)S(1)}, bf16[2,16,16,128]{3,2,1,0:T(8,128)(2,1)S(1)}, u32[]{:S(2)}, u32[]{:S(2)}) %collective-permute-start.13) | collective-permute-done | bytes 131104 | tf_op jit(solution)/shard_map/ppermute | solution.py:339
  44.7 1.5 %collective-permute-done.15.got_ref.refs_1_ = bf16[8,8,16,128]{3,2,1,0:T(8,128)(2,1)S(1)} collective-permute-done((bf16[8,8,16,128]{3,2,1,0:T(8,128)(2,1)S(1)}, bf16[8,8,16,128]{3,2,1,0:T(8,128)(2,1)S(1)}, u32[]{:S(2)}, u32[]{:S(2)}) %collective-permute-start.15) | collective-permute-done | bytes 262176 | tf_op jit(solution)/shard_map/ppermute | solution.py:339
  46.2 1.8 %collective-permute-start.16 = (bf16[2,8,16,128]{3,2,1,0:T(8,128)(2,1)S(1)}, bf16[2,8,16,128]{3,2,1,0:T(8,128)(2,1)S(1)}, u32[]{:S(2)}, u32[]{:S(2)}) collective-permute-start(bf16[2,8,16,128]{3,2,1,0:T(8,128)(2,1)S(1)} %get-tuple-element.92), channel_id=1, source_target_pairs={{0,13},{1,12},{2,15},{3,14},{4,9},{5,8},{6,11},{7,10},{8,5},{9,4},... | collective-permute-start | bytes 196616 | tf_op jit(solution)/shard_map/ppermute | solution.py:339
  48.1 2.5 %collective-permute-start.17 = (bf16[2,8,16,128]{3,2,1,0:T(8,128)(2,1)S(1)}, bf16[2,8,16,128]{3,2,1,0:T(8,128)(2,1)S(1)}, u32[]{:S(2)}, u32[]{:S(2)}) collective-permute-start(bf16[2,8,16,128]{3,2,1,0:T(8,128)(2,1)S(1)} %get-tuple-element.93), channel_id=1, source_target_pairs={{0,12},{1,13},{2,14},{3,15},{4,8},{5,9},{6,10},{7,11},{8,4},{9,5},... | collective-permute-start | bytes 196616 | tf_op jit(solution)/shard_map/ppermute | solution.py:339
  50.6 2.8 %collective-permute-start.19 = (bf16[2,8,16,128]{3,2,1,0:T(8,128)(2,1)S(1)}, bf16[2,8,16,128]{3,2,1,0:T(8,128)(2,1)S(1)}, u32[]{:S(2)}, u32[]{:S(2)}) collective-permute-start(bf16[2,8,16,128]{3,2,1,0:T(8,128)(2,1)S(1)} %get-tuple-element.95), channel_id=1, source_target_pairs={{0,9},{1,8},{2,11},{3,10},{4,13},{5,12},{6,15},{7,14},{8,1},{9,0},... | collective-permute-start | bytes 196616 | tf_op jit(solution)/shard_map/ppermute | solution.py:339
  54.0 2.5 %collective-permute-start.21 = (bf16[2,8,16,128]{3,2,1,0:T(8,128)(2,1)S(1)}, bf16[2,8,16,128]{3,2,1,0:T(8,128)(2,1)S(1)}, u32[]{:S(2)}, u32[]{:S(2)}) collective-permute-start(bf16[2,8,16,128]{3,2,1,0:T(8,128)(2,1)S(1)} %get-tuple-element.97), channel_id=1, source_target_pairs={{0,4},{1,5},{2,6},{3,7},{4,0},{5,1},{6,2},{7,3},{8,12},{9,13},{10,... | collective-permute-start | bytes 196616 | tf_op jit(solution)/shard_map/ppermute | solution.py:339
  57.5 3.6 %collective-permute-done.19.refs_5_ = bf16[2,8,16,128]{3,2,1,0:T(8,128)(2,1)S(1)} collective-permute-done((bf16[2,8,16,128]{3,2,1,0:T(8,128)(2,1)S(1)}, bf16[2,8,16,128]{3,2,1,0:T(8,128)(2,1)S(1)}, u32[]{:S(2)}, u32[]{:S(2)}) %collective-permute-start.19) | collective-permute-done | bytes 65568 | tf_op jit(solution)/shard_map/ppermute | solution.py:339
  61.2 1.5 %shard_map.93 = f32[1024,128]{1,0:T(8,128)} custom-call(f32[128,1024]{1,0:T(8,128)S(1)} %get-tuple-element.78.middle_ref, f32[128,1024]{1,0:T(8,128)S(1)} %shard_map.88.gating_ref, bf16[128,128]{1,0:T(8,128)(2,1)S(1)} %copy-done.1, bf16[8,8,16,128]{3,2,1,0:T(8,128)(2,1)S(1)} %get-tuple-element.90.keep_ref.refs_0_, ...), custom_call_target="tpu_custom_call" | custom-call | bytes 2588672 | tf_op jit(solution)/shard_map/pallas_call | solution.py:316
  (44 shorter events, 10.1 us)
Async XLA Ops:
  2.2 9.9 %collective-permute-start.3 = (bf16[2,8,16,128]{3,2,1,0:T(8,128)(2,1)S(1)}, bf16[2,8,16,128]{3,2,1,0:T(8,128)(2,1)S(1)}, u32[]{:S(2)}, u32[]{:S(2)}) collective-permute-start(bf16[2,8,16,128]{3,2,1,0:T(8,128)(2,1)S(1)} %get-tuple-element.58), channel_id=1, source_target_pairs={{0,8},{1,9},{2,10},{3,11},{4,12},{5,13},{6,14},{7,15},{8,0},{9,1},... | collective-permute-start | bytes 196616 | tf_op jit(solution)/shard_map/ppermute | solution.py:339
  6.3 8.7 %collective-permute-start.4 = (bf16[2,8,16,128]{3,2,1,0:T(8,128)(2,1)S(1)}, bf16[2,8,16,128]{3,2,1,0:T(8,128)(2,1)S(1)}, u32[]{:S(2)}, u32[]{:S(2)}) collective-permute-start(bf16[2,8,16,128]{3,2,1,0:T(8,128)(2,1)S(1)} %get-tuple-element.59), channel_id=1, source_target_pairs={{0,13},{1,12},{2,15},{3,14},{4,9},{5,8},{6,11},{7,10},{8,5},{9,4},... | collective-permute-start | bytes 196616 | tf_op jit(solution)/shard_map/ppermute | solution.py:339
  8.6 13.7 %collective-permute-start = (bf16[2,2,8,16,128]{4,3,2,1,0:T(8,128)(2,1)S(1)}, bf16[2,2,8,16,128]{4,3,2,1,0:T(8,128)(2,1)S(1)}, u32[]{:S(2)}, u32[]{:S(2)}) collective-permute-start(bf16[2,2,8,16,128]{4,3,2,1,0:T(8,128)(2,1)S(1)} %get-tuple-element.55), channel_id=1, source_target_pairs={{0,5},{1,4},{2,7},{3,6},{4,1},{5,0},{6,3},{7,2},{8,13},{9,12},{10,... | collective-permute-start | bytes 393224 | tf_op jit(solution)/shard_map/ppermute | solution.py:339
  8.8 13.5 %collective-permute-start.1 = (bf16[2,2,8,16,128]{4,3,2,1,0:T(8,128)(2,1)S(1)}, bf16[2,2,8,16,128]{4,3,2,1,0:T(8,128)(2,1)S(1)}, u32[]{:S(2)}, u32[]{:S(2)}) collective-permute-start(bf16[2,2,8,16,128]{4,3,2,1,0:T(8,128)(2,1)S(1)} %get-tuple-element.56), channel_id=1, source_target_pairs={{0,4},{1,5},{2,6},{3,7},{4,0},{5,1},{6,2},{7,3},{8,12},{9,13},{10,... | collective-permute-start | bytes 393224 | tf_op jit(solution)/shard_map/ppermute | solution.py:339
  10.6 11.7 %collective-permute-start.2 = (bf16[2,2,8,16,128]{4,3,2,1,0:T(8,128)(2,1)S(1)}, bf16[2,2,8,16,128]{4,3,2,1,0:T(8,128)(2,1)S(1)}, u32[]{:S(2)}, u32[]{:S(2)}) collective-permute-start(bf16[2,2,8,16,128]{4,3,2,1,0:T(8,128)(2,1)S(1)} %get-tuple-element.57), channel_id=1, source_target_pairs={{0,1},{1,0},{2,3},{3,2},{4,5},{5,4},{6,7},{7,6},{8,9},{9,8},{10,11... | collective-permute-start | bytes 393224 | tf_op jit(solution)/shard_map/ppermute | solution.py:339
  12.0 8.3 %collective-permute-start.5 = (bf16[2,8,16,128]{3,2,1,0:T(8,128)(2,1)S(1)}, bf16[2,8,16,128]{3,2,1,0:T(8,128)(2,1)S(1)}, u32[]{:S(2)}, u32[]{:S(2)}) collective-permute-start(bf16[2,8,16,128]{3,2,1,0:T(8,128)(2,1)S(1)} %get-tuple-element.60), channel_id=1, source_target_pairs={{0,12},{1,13},{2,14},{3,15},{4,8},{5,9},{6,10},{7,11},{8,4},{9,5},... | collective-permute-start | bytes 196616 | tf_op jit(solution)/shard_map/ppermute | solution.py:339
  15.0 7.3 %collective-permute-start.6 = (bf16[2,8,16,128]{3,2,1,0:T(8,128)(2,1)S(1)}, bf16[2,8,16,128]{3,2,1,0:T(8,128)(2,1)S(1)}, u32[]{:S(2)}, u32[]{:S(2)}) collective-permute-start(bf16[2,8,16,128]{3,2,1,0:T(8,128)(2,1)S(1)} %get-tuple-element.61), channel_id=1, source_target_pairs={{0,9},{1,8},{2,11},{3,10},{4,13},{5,12},{6,15},{7,14},{8,1},{9,0},... | collective-permute-start | bytes 196616 | tf_op jit(solution)/shard_map/ppermute | solution.py:339
  22.4 2.0 %collective-permute-start.7 = (bf16[8,2,8,16,128]{4,3,2,1,0:T(8,128)(2,1)S(1)}, bf16[8,2,8,16,128]{4,3,2,1,0:T(8,128)(2,1)S(1)}, u32[]{:S(2)}, u32[]{:S(2)}) collective-permute-start(bf16[8,2,8,16,128]{4,3,2,1,0:T(8,128)(2,1)S(1)} %shard_map.85), channel_id=1, source_target_pairs={{0,2},{1,3},{2,0},{3,1},{4,6},{5,7},{6,4},{7,5},{8,10},{9,11},{10,... | collective-permute-start | bytes 1572872 | tf_op jit(solution)/shard_map/ppermute | solution.py:339
  25.2 4.3 %collective-permute-start.10 = (bf16[2,8,16,128]{3,2,1,0:T(8,128)(2,1)S(1)}, bf16[2,8,16,128]{3,2,1,0:T(8,128)(2,1)S(1)}, u32[]{:S(2)}, u32[]{:S(2)}) collective-permute-start(bf16[2,8,16,128]{3,2,1,0:T(8,128)(2,1)S(1)} %get-tuple-element.77), channel_id=1, source_target_pairs={{0,1},{1,0},{2,3},{3,2},{4,5},{5,4},{6,7},{7,6},{8,9},{9,8},{10,11... | collective-permute-start | bytes 196616 | tf_op jit(solution)/shard_map/ppermute | solution.py:339
  26.3 5.5 %collective-permute-start.8 = (bf16[2,8,16,128]{3,2,1,0:T(8,128)(2,1)S(1)}, bf16[2,8,16,128]{3,2,1,0:T(8,128)(2,1)S(1)}, u32[]{:S(2)}, u32[]{:S(2)}) collective-permute-start(bf16[2,8,16,128]{3,2,1,0:T(8,128)(2,1)S(1)} %get-tuple-element.75), channel_id=1, source_target_pairs={{0,5},{1,4},{2,7},{3,6},{4,1},{5,0},{6,3},{7,2},{8,13},{9,12},{10,... | collective-permute-start | bytes 196616 | tf_op jit(solution)/shard_map/ppermute | solution.py:339
  26.6 5.4 %collective-permute-start.9 = (bf16[2,8,16,128]{3,2,1,0:T(8,128)(2,1)S(1)}, bf16[2,8,16,128]{3,2,1,0:T(8,128)(2,1)S(1)}, u32[]{:S(2)}, u32[]{:S(2)}) collective-permute-start(bf16[2,8,16,128]{3,2,1,0:T(8,128)(2,1)S(1)} %get-tuple-element.76), channel_id=1, source_target_pairs={{0,4},{1,5},{2,6},{3,7},{4,0},{5,1},{6,2},{7,3},{8,12},{9,13},{10,... | collective-permute-start | bytes 196616 | tf_op jit(solution)/shard_map/ppermute | solution.py:339
  33.2 1.6 %collective-permute-start.11 = (bf16[4,16,16,128]{3,2,1,0:T(8,128)(2,1)S(1)}, bf16[4,16,16,128]{3,2,1,0:T(8,128)(2,1)S(1)}, u32[]{:S(2)}, u32[]{:S(2)}) collective-permute-start(bf16[4,16,16,128]{3,2,1,0:T(8,128)(2,1)S(1)} %get-tuple-element.80), channel_id=1, source_target_pairs={{0,2},{1,3},{2,0},{3,1},{4,6},{5,7},{6,4},{7,5},{8,10},{9,11},{10,... | collective-permute-start | bytes 786440 | tf_op jit(solution)/shard_map/ppermute | solution.py:339
  34.8 7.3 %collective-permute-start.12 = (bf16[2,16,16,128]{3,2,1,0:T(8,128)(2,1)S(1)}, bf16[2,16,16,128]{3,2,1,0:T(8,128)(2,1)S(1)}, u32[]{:S(2)}, u32[]{:S(2)}) collective-permute-start(bf16[2,16,16,128]{3,2,1,0:T(8,128)(2,1)S(1)} %get-tuple-element.81), channel_id=1, source_target_pairs={{0,5},{1,4},{2,7},{3,6},{4,1},{5,0},{6,3},{7,2},{8,13},{9,12},{10,... | collective-permute-start | bytes 393224 | tf_op jit(solution)/shard_map/ppermute | solution.py:339
  36.4 7.3 %collective-permute-start.13 = (bf16[2,16,16,128]{3,2,1,0:T(8,128)(2,1)S(1)}, bf16[2,16,16,128]{3,2,1,0:T(8,128)(2,1)S(1)}, u32[]{:S(2)}, u32[]{:S(2)}) collective-permute-start(bf16[2,16,16,128]{3,2,1,0:T(8,128)(2,1)S(1)} %get-tuple-element.82), channel_id=1, source_target_pairs={{0,4},{1,5},{2,6},{3,7},{4,0},{5,1},{6,2},{7,3},{8,12},{9,13},{10,... | collective-permute-start | bytes 393224 | tf_op jit(solution)/shard_map/ppermute | solution.py:339
  37.3 6.8 %collective-permute-start.14 = (bf16[2,16,16,128]{3,2,1,0:T(8,128)(2,1)S(1)}, bf16[2,16,16,128]{3,2,1,0:T(8,128)(2,1)S(1)}, u32[]{:S(2)}, u32[]{:S(2)}) collective-permute-start(bf16[2,16,16,128]{3,2,1,0:T(8,128)(2,1)S(1)} %get-tuple-element.83), channel_id=1, source_target_pairs={{0,1},{1,0},{2,3},{3,2},{4,5},{5,4},{6,7},{7,6},{8,9},{9,8},{10,11... | collective-permute-start | bytes 393224 | tf_op jit(solution)/shard_map/ppermute | solution.py:339
  44.6 1.6 %collective-permute-start.15 = (bf16[8,8,16,128]{3,2,1,0:T(8,128)(2,1)S(1)}, bf16[8,8,16,128]{3,2,1,0:T(8,128)(2,1)S(1)}, u32[]{:S(2)}, u32[]{:S(2)}) collective-permute-start(bf16[8,8,16,128]{3,2,1,0:T(8,128)(2,1)S(1)} %get-tuple-element.91), channel_id=1, source_target_pairs={{0,2},{1,3},{2,0},{3,1},{4,6},{5,7},{6,4},{7,5},{8,10},{9,11},{10,... | collective-permute-start | bytes 786440 | tf_op jit(solution)/shard_map/ppermute | solution.py:339
  46.2 15.0 %copy-start.1 = (bf16[128,128]{1,0:T(8,128)(2,1)S(1)}, bf16[128,128]{1,0:T(8,128)(2,1)}, u32[]{:S(2)}) copy-start(bf16[128,128]{1,0:T(8,128)(2,1)} %final_ref.3) | copy-start | bytes 98308
  46.2 7.7 %collective-permute-start.16 = (bf16[2,8,16,128]{3,2,1,0:T(8,128)(2,1)S(1)}, bf16[2,8,16,128]{3,2,1,0:T(8,128)(2,1)S(1)}, u32[]{:S(2)}, u32[]{:S(2)}) collective-permute-start(bf16[2,8,16,128]{3,2,1,0:T(8,128)(2,1)S(1)} %get-tuple-element.92), channel_id=1, source_target_pairs={{0,13},{1,12},{2,15},{3,14},{4,9},{5,8},{6,11},{7,10},{8,5},{9,4},... | collective-permute-start | bytes 196616 | tf_op jit(solution)/shard_map/ppermute | solution.py:339
  48.1 8.4 %collective-permute-start.17 = (bf16[2,8,16,128]{3,2,1,0:T(8,128)(2,1)S(1)}, bf16[2,8,16,128]{3,2,1,0:T(8,128)(2,1)S(1)}, u32[]{:S(2)}, u32[]{:S(2)}) collective-permute-start(bf16[2,8,16,128]{3,2,1,0:T(8,128)(2,1)S(1)} %get-tuple-element.93), channel_id=1, source_target_pairs={{0,12},{1,13},{2,14},{3,15},{4,8},{5,9},{6,10},{7,11},{8,4},{9,5},... | collective-permute-start | bytes 196616 | tf_op jit(solution)/shard_map/ppermute | solution.py:339
  50.6 6.9 %collective-permute-start.18 = (bf16[2,8,16,128]{3,2,1,0:T(8,128)(2,1)S(1)}, bf16[2,8,16,128]{3,2,1,0:T(8,128)(2,1)S(1)}, u32[]{:S(2)}, u32[]{:S(2)}) collective-permute-start(bf16[2,8,16,128]{3,2,1,0:T(8,128)(2,1)S(1)} %get-tuple-element.94), channel_id=1, source_target_pairs={{0,5},{1,4},{2,7},{3,6},{4,1},{5,0},{6,3},{7,2},{8,13},{9,12},{10,... | collective-permute-start | bytes 196616 | tf_op jit(solution)/shard_map/ppermute | solution.py:339
  50.6 10.4 %collective-permute-start.19 = (bf16[2,8,16,128]{3,2,1,0:T(8,128)(2,1)S(1)}, bf16[2,8,16,128]{3,2,1,0:T(8,128)(2,1)S(1)}, u32[]{:S(2)}, u32[]{:S(2)}) collective-permute-start(bf16[2,8,16,128]{3,2,1,0:T(8,128)(2,1)S(1)} %get-tuple-element.95), channel_id=1, source_target_pairs={{0,9},{1,8},{2,11},{3,10},{4,13},{5,12},{6,15},{7,14},{8,1},{9,0},... | collective-permute-start | bytes 196616 | tf_op jit(solution)/shard_map/ppermute | solution.py:339
  53.4 7.8 %collective-permute-start.20 = (bf16[2,8,16,128]{3,2,1,0:T(8,128)(2,1)S(1)}, bf16[2,8,16,128]{3,2,1,0:T(8,128)(2,1)S(1)}, u32[]{:S(2)}, u32[]{:S(2)}) collective-permute-start(bf16[2,8,16,128]{3,2,1,0:T(8,128)(2,1)S(1)} %get-tuple-element.96), channel_id=1, source_target_pairs={{0,8},{1,9},{2,10},{3,11},{4,12},{5,13},{6,14},{7,15},{8,0},{9,1},... | collective-permute-start | bytes 196616 | tf_op jit(solution)/shard_map/ppermute | solution.py:339
  54.0 7.2 %collective-permute-start.21 = (bf16[2,8,16,128]{3,2,1,0:T(8,128)(2,1)S(1)}, bf16[2,8,16,128]{3,2,1,0:T(8,128)(2,1)S(1)}, u32[]{:S(2)}, u32[]{:S(2)}) collective-permute-start(bf16[2,8,16,128]{3,2,1,0:T(8,128)(2,1)S(1)} %get-tuple-element.97), channel_id=1, source_target_pairs={{0,4},{1,5},{2,6},{3,7},{4,0},{5,1},{6,2},{7,3},{8,12},{9,13},{10,... | collective-permute-start | bytes 196616 | tf_op jit(solution)/shard_map/ppermute | solution.py:339
  56.5 4.8 %collective-permute-start.22 = (bf16[2,8,16,128]{3,2,1,0:T(8,128)(2,1)S(1)}, bf16[2,8,16,128]{3,2,1,0:T(8,128)(2,1)S(1)}, u32[]{:S(2)}, u32[]{:S(2)}) collective-permute-start(bf16[2,8,16,128]{3,2,1,0:T(8,128)(2,1)S(1)} %get-tuple-element.98), channel_id=1, source_target_pairs={{0,1},{1,0},{2,3},{3,2},{4,5},{5,4},{6,7},{7,6},{8,9},{9,8},{10,11... | collective-permute-start | bytes 196616 | tf_op jit(solution)/shard_map/ppermute | solution.py:339
  (4 other events, 13.9 us)

commit v10 on v9

--- a/solution.py
+++ b/solution.py
@@ -179,15 +179,15 @@
     both_refs, b_refs = refs[:CHIPS], refs[CHIPS : 2 * CHIPS]
     pair_t_ref, normed_ref, live_ref = refs[2 * CHIPS : 2 * CHIPS + 3]
     pair_ref, mask_ref, proj_ref, weights, wide, by_near, done = refs[2 * CHIPS + 3 :]
-    chunks = [slice(at, at + CHUNK) for at in range(0, rows * cols, CHUNK)]
+    chunks = [slice(0, rows * cols)]
     whole = [(mask_hbm, mask_ref), (proj_hbm, proj_ref)]
-    coming = copies([(pair_hbm.at[at], pair_ref.at[at]) for at in chunks] + whole, done)
-    for copy in coming[len(chunks) :]:
+    coming = copies(whole + [(pair_hbm.at[at], pair_ref.at[at]) for at in chunks], done)
+    for copy in coming[: len(whole)]:
         copy.wait()
     first_weights(proj_ref, wide, weights)
     live = live_tile(mask_ref, rows, cols)
     live_ref[...] = live
-    for copy in coming[: len(chunks)]:
+    for copy in coming[len(whole) :]:
         copy.wait()
     pair = pair_ref[...].T
     pair_t_ref[...] = pair

time: 63 us -> 62.9 us (level)
  no operation moved by 1% of the time
where the time goes in v10:
time: 62.9 us; the launch traced here: 62.7 us
  starting transfers between devices  33.1 us (53%)
  waiting for transfers between devices  20.7 us (33%)
  Pallas kernels  7.42 us (12%)
  local copies, waits for them, and re-layouts  1.29 us (2%)
    ppermute x23, starting transfers between devices, swap(): return lax.ppermute(values, axes, [(d, d ^ step) for d in range(devices)])  33.1 us
    ppermute x23, waiting for transfers between devices, swap(): return lax.ppermute(values, axes, [(d, d ^ step) for d in range(devices)])  20.7 us
    pallas_call x12, Pallas kernels, run(): pl.pallas_call(kernel, out_shape=tuple(out_shape), in_specs=[hbm] * far_a...  7.42 us
    unnamed x10, local copies, waits for them, and re-layouts  1.29 us
  transfers between devices with their start and end apart: 23, of which 13 were waited for; matrix products, arithmetic and copies ran while one was open for 0% of the time, Pallas kernels for 2%

profile of v10, /device:TPU:0, one launch (start us, length us, event | category | flops | bytes accessed | tf_op | source)
XLA Modules:
  0.0 62.7 jit_solution(1027697509436952111)
XLA Ops:
  0.0 2.1 %shard_map.82 = (bf16[2,2,8,16,128]{4,3,2,1,0:T(8,128)(2,1)S(1)}, bf16[2,2,8,16,128]{4,3,2,1,0:T(8,128)(2,1)S(1)}, bf16[2,2,8,16,128]{4,3,2,1,0:T(8,128)(2,1)S(1...) custom-call(f32[1024,128]{1,0:T(8,128)} %bitcast.6, ...), custom_call_target="tpu_custom_call" | custom-call | bytes 2236928 | tf_op jit(solution)/shard_map/pallas_call | solution.py:316
  2.1 4.1 %collective-permute-start.3 = (bf16[2,8,16,128]{3,2,1,0:T(8,128)(2,1)S(1)}, bf16[2,8,16,128]{3,2,1,0:T(8,128)(2,1)S(1)}, u32[]{:S(2)}, u32[]{:S(2)}) collective-permute-start(bf16[2,8,16,128]{3,2,1,0:T(8,128)(2,1)S(1)} %get-tuple-element.58), channel_id=1, source_target_pairs={{0,8},{1,9},{2,10},{3,11},{4,12},{5,13},{6,14},{7,15},{8,0},{9,1},... | collective-permute-start | bytes 196616 | tf_op jit(solution)/shard_map/ppermute | solution.py:339
  6.2 2.3 %collective-permute-start.4 = (bf16[2,8,16,128]{3,2,1,0:T(8,128)(2,1)S(1)}, bf16[2,8,16,128]{3,2,1,0:T(8,128)(2,1)S(1)}, u32[]{:S(2)}, u32[]{:S(2)}) collective-permute-start(bf16[2,8,16,128]{3,2,1,0:T(8,128)(2,1)S(1)} %get-tuple-element.59), channel_id=1, source_target_pairs={{0,13},{1,12},{2,15},{3,14},{4,9},{5,8},{6,11},{7,10},{8,5},{9,4},... | collective-permute-start | bytes 196616 | tf_op jit(solution)/shard_map/ppermute | solution.py:339
  8.7 1.8 %collective-permute-start.1 = (bf16[2,2,8,16,128]{4,3,2,1,0:T(8,128)(2,1)S(1)}, bf16[2,2,8,16,128]{4,3,2,1,0:T(8,128)(2,1)S(1)}, u32[]{:S(2)}, u32[]{:S(2)}) collective-permute-start(bf16[2,2,8,16,128]{4,3,2,1,0:T(8,128)(2,1)S(1)} %get-tuple-element.56), channel_id=1, source_target_pairs={{0,4},{1,5},{2,6},{3,7},{4,0},{5,1},{6,2},{7,3},{8,12},{9,13},{10,... | collective-permute-start | bytes 393224 | tf_op jit(solution)/shard_map/ppermute | solution.py:339
  10.4 1.5 %collective-permute-start.2 = (bf16[2,2,8,16,128]{4,3,2,1,0:T(8,128)(2,1)S(1)}, bf16[2,2,8,16,128]{4,3,2,1,0:T(8,128)(2,1)S(1)}, u32[]{:S(2)}, u32[]{:S(2)}) collective-permute-start(bf16[2,2,8,16,128]{4,3,2,1,0:T(8,128)(2,1)S(1)} %get-tuple-element.57), channel_id=1, source_target_pairs={{0,1},{1,0},{2,3},{3,2},{4,5},{5,4},{6,7},{7,6},{8,9},{9,8},{10,11... | collective-permute-start | bytes 393224 | tf_op jit(solution)/shard_map/ppermute | solution.py:339
  11.9 2.9 %collective-permute-start.5 = (bf16[2,8,16,128]{3,2,1,0:T(8,128)(2,1)S(1)}, bf16[2,8,16,128]{3,2,1,0:T(8,128)(2,1)S(1)}, u32[]{:S(2)}, u32[]{:S(2)}) collective-permute-start(bf16[2,8,16,128]{3,2,1,0:T(8,128)(2,1)S(1)} %get-tuple-element.60), channel_id=1, source_target_pairs={{0,12},{1,13},{2,14},{3,15},{4,8},{5,9},{6,10},{7,11},{8,4},{9,5},... | collective-permute-start | bytes 196616 | tf_op jit(solution)/shard_map/ppermute | solution.py:339
  14.8 1.8 %collective-permute-start.6 = (bf16[2,8,16,128]{3,2,1,0:T(8,128)(2,1)S(1)}, bf16[2,8,16,128]{3,2,1,0:T(8,128)(2,1)S(1)}, u32[]{:S(2)}, u32[]{:S(2)}) collective-permute-start(bf16[2,8,16,128]{3,2,1,0:T(8,128)(2,1)S(1)} %get-tuple-element.61), channel_id=1, source_target_pairs={{0,9},{1,8},{2,11},{3,10},{4,13},{5,12},{6,15},{7,14},{8,1},{9,0},... | collective-permute-start | bytes 196616 | tf_op jit(solution)/shard_map/ppermute | solution.py:339
  16.7 3.6 %collective-permute-done.5.refs_6_ = bf16[2,8,16,128]{3,2,1,0:T(8,128)(2,1)S(1)} collective-permute-done((bf16[2,8,16,128]{3,2,1,0:T(8,128)(2,1)S(1)}, bf16[2,8,16,128]{3,2,1,0:T(8,128)(2,1)S(1)}, u32[]{:S(2)}, u32[]{:S(2)}) %collective-permute-start.5) | collective-permute-done | bytes 65568 | tf_op jit(solution)/shard_map/ppermute | solution.py:339
  20.3 1.9 %collective-permute-done.6.refs_7_ = bf16[2,8,16,128]{3,2,1,0:T(8,128)(2,1)S(1)} collective-permute-done((bf16[2,8,16,128]{3,2,1,0:T(8,128)(2,1)S(1)}, bf16[2,8,16,128]{3,2,1,0:T(8,128)(2,1)S(1)}, u32[]{:S(2)}, u32[]{:S(2)}) %collective-permute-start.6) | collective-permute-done | bytes 65568 | tf_op jit(solution)/shard_map/ppermute | solution.py:339
  25.1 1.1 %collective-permute-start.10 = (bf16[2,8,16,128]{3,2,1,0:T(8,128)(2,1)S(1)}, bf16[2,8,16,128]{3,2,1,0:T(8,128)(2,1)S(1)}, u32[]{:S(2)}, u32[]{:S(2)}) collective-permute-start(bf16[2,8,16,128]{3,2,1,0:T(8,128)(2,1)S(1)} %get-tuple-element.77), channel_id=1, source_target_pairs={{0,1},{1,0},{2,3},{3,2},{4,5},{5,4},{6,7},{7,6},{8,9},{9,8},{10,11... | collective-permute-start | bytes 196616 | tf_op jit(solution)/shard_map/ppermute | solution.py:339
  26.5 2.2 %collective-permute-start.9 = (bf16[2,8,16,128]{3,2,1,0:T(8,128)(2,1)S(1)}, bf16[2,8,16,128]{3,2,1,0:T(8,128)(2,1)S(1)}, u32[]{:S(2)}, u32[]{:S(2)}) collective-permute-start(bf16[2,8,16,128]{3,2,1,0:T(8,128)(2,1)S(1)} %get-tuple-element.76), channel_id=1, source_target_pairs={{0,4},{1,5},{2,6},{3,7},{4,0},{5,1},{6,2},{7,3},{8,12},{9,13},{10,... | collective-permute-start | bytes 196616 | tf_op jit(solution)/shard_map/ppermute | solution.py:339
  29.4 2.2 %collective-permute-done.8.refs_1_ = bf16[2,8,16,128]{3,2,1,0:T(8,128)(2,1)S(1)} collective-permute-done((bf16[2,8,16,128]{3,2,1,0:T(8,128)(2,1)S(1)}, bf16[2,8,16,128]{3,2,1,0:T(8,128)(2,1)S(1)}, u32[]{:S(2)}, u32[]{:S(2)}) %collective-permute-start.8) | collective-permute-done | bytes 65568 | tf_op jit(solution)/shard_map/ppermute | solution.py:339
  31.9 1.2 %shard_map.87 = (bf16[4,16,16,128]{3,2,1,0:T(8,128)(2,1)S(1)}, f32[128,1024]{1,0:T(8,128)S(1)}, bf16[128,1024]{1,0:T(8,128)(2,1)S(1)}) custom-call(f32[16,128]{1,0:T(8,128)S(1)} %get-tuple-element.52.live_ref, bf16[128,512]{1,0:T(8,128)(2,1)S(1)} %shard_map.84.weights, bf16[128,128]{1,0:T(8,128)(2,1)S(1)} %copy-done.3, ...), custom_call_target="tpu_custom_call" | custom-call | bytes 2531328 | tf_op jit(solution)/shard_map/pallas_call | solution.py:316
  33.6 1.0 %collective-permute-done.11.got_ref.refs_1_ = bf16[4,16,16,128]{3,2,1,0:T(8,128)(2,1)S(1)} collective-permute-done((bf16[4,16,16,128]{3,2,1,0:T(8,128)(2,1)S(1)}, bf16[4,16,16,128]{3,2,1,0:T(8,128)(2,1)S(1)}, u32[]{:S(2)}, u32[]{:S(2)}) %collective-permute-start.11) | collective-permute-done | bytes 262176 | tf_op jit(solution)/shard_map/ppermute | solution.py:339
  34.7 1.6 %collective-permute-start.12 = (bf16[2,16,16,128]{3,2,1,0:T(8,128)(2,1)S(1)}, bf16[2,16,16,128]{3,2,1,0:T(8,128)(2,1)S(1)}, u32[]{:S(2)}, u32[]{:S(2)}) collective-permute-start(bf16[2,16,16,128]{3,2,1,0:T(8,128)(2,1)S(1)} %get-tuple-element.81), channel_id=1, source_target_pairs={{0,5},{1,4},{2,7},{3,6},{4,1},{5,0},{6,3},{7,2},{8,13},{9,12},{10,... | collective-permute-start | bytes 393224 | tf_op jit(solution)/shard_map/ppermute | solution.py:339
  38.5 3.5 %collective-permute-done.12.refs_2_ = bf16[2,16,16,128]{3,2,1,0:T(8,128)(2,1)S(1)} collective-permute-done((bf16[2,16,16,128]{3,2,1,0:T(8,128)(2,1)S(1)}, bf16[2,16,16,128]{3,2,1,0:T(8,128)(2,1)S(1)}, u32[]{:S(2)}, u32[]{:S(2)}) %collective-permute-start.12) | collective-permute-done | bytes 131104 | tf_op jit(solution)/shard_map/ppermute | solution.py:339
  42.0 1.6 %collective-permute-done.13.refs_3_ = bf16[2,16,16,128]{3,2,1,0:T(8,128)(2,1)S(1)} collective-permute-done((bf16[2,16,16,128]{3,2,1,0:T(8,128)(2,1)S(1)}, bf16[2,16,16,128]{3,2,1,0:T(8,128)(2,1)S(1)}, u32[]{:S(2)}, u32[]{:S(2)}) %collective-permute-start.13) | collective-permute-done | bytes 131104 | tf_op jit(solution)/shard_map/ppermute | solution.py:339
  44.6 1.5 %collective-permute-done.15.got_ref.refs_1_ = bf16[8,8,16,128]{3,2,1,0:T(8,128)(2,1)S(1)} collective-permute-done((bf16[8,8,16,128]{3,2,1,0:T(8,128)(2,1)S(1)}, bf16[8,8,16,128]{3,2,1,0:T(8,128)(2,1)S(1)}, u32[]{:S(2)}, u32[]{:S(2)}) %collective-permute-start.15) | collective-permute-done | bytes 262176 | tf_op jit(solution)/shard_map/ppermute | solution.py:339
  46.1 1.8 %collective-permute-start.16 = (bf16[2,8,16,128]{3,2,1,0:T(8,128)(2,1)S(1)}, bf16[2,8,16,128]{3,2,1,0:T(8,128)(2,1)S(1)}, u32[]{:S(2)}, u32[]{:S(2)}) collective-permute-start(bf16[2,8,16,128]{3,2,1,0:T(8,128)(2,1)S(1)} %get-tuple-element.92), channel_id=1, source_target_pairs={{0,13},{1,12},{2,15},{3,14},{4,9},{5,8},{6,11},{7,10},{8,5},{9,4},... | collective-permute-start | bytes 196616 | tf_op jit(solution)/shard_map/ppermute | solution.py:339
  48.0 2.5 %collective-permute-start.17 = (bf16[2,8,16,128]{3,2,1,0:T(8,128)(2,1)S(1)}, bf16[2,8,16,128]{3,2,1,0:T(8,128)(2,1)S(1)}, u32[]{:S(2)}, u32[]{:S(2)}) collective-permute-start(bf16[2,8,16,128]{3,2,1,0:T(8,128)(2,1)S(1)} %get-tuple-element.93), channel_id=1, source_target_pairs={{0,12},{1,13},{2,14},{3,15},{4,8},{5,9},{6,10},{7,11},{8,4},{9,5},... | collective-permute-start | bytes 196616 | tf_op jit(solution)/shard_map/ppermute | solution.py:339
  50.5 2.8 %collective-permute-start.19 = (bf16[2,8,16,128]{3,2,1,0:T(8,128)(2,1)S(1)}, bf16[2,8,16,128]{3,2,1,0:T(8,128)(2,1)S(1)}, u32[]{:S(2)}, u32[]{:S(2)}) collective-permute-start(bf16[2,8,16,128]{3,2,1,0:T(8,128)(2,1)S(1)} %get-tuple-element.95), channel_id=1, source_target_pairs={{0,9},{1,8},{2,11},{3,10},{4,13},{5,12},{6,15},{7,14},{8,1},{9,0},... | collective-permute-start | bytes 196616 | tf_op jit(solution)/shard_map/ppermute | solution.py:339
  53.9 2.5 %collective-permute-start.21 = (bf16[2,8,16,128]{3,2,1,0:T(8,128)(2,1)S(1)}, bf16[2,8,16,128]{3,2,1,0:T(8,128)(2,1)S(1)}, u32[]{:S(2)}, u32[]{:S(2)}) collective-permute-start(bf16[2,8,16,128]{3,2,1,0:T(8,128)(2,1)S(1)} %get-tuple-element.97), channel_id=1, source_target_pairs={{0,4},{1,5},{2,6},{3,7},{4,0},{5,1},{6,2},{7,3},{8,12},{9,13},{10,... | collective-permute-start | bytes 196616 | tf_op jit(solution)/shard_map/ppermute | solution.py:339
  57.4 3.6 %collective-permute-done.19.refs_5_ = bf16[2,8,16,128]{3,2,1,0:T(8,128)(2,1)S(1)} collective-permute-done((bf16[2,8,16,128]{3,2,1,0:T(8,128)(2,1)S(1)}, bf16[2,8,16,128]{3,2,1,0:T(8,128)(2,1)S(1)}, u32[]{:S(2)}, u32[]{:S(2)}) %collective-permute-start.19) | collective-permute-done | bytes 65568 | tf_op jit(solution)/shard_map/ppermute | solution.py:339
  61.1 1.5 %shard_map.93 = f32[1024,128]{1,0:T(8,128)} custom-call(f32[128,1024]{1,0:T(8,128)S(1)} %get-tuple-element.78.middle_ref, f32[128,1024]{1,0:T(8,128)S(1)} %shard_map.88.gating_ref, bf16[128,128]{1,0:T(8,128)(2,1)S(1)} %copy-done.1, bf16[8,8,16,128]{3,2,1,0:T(8,128)(2,1)S(1)} %get-tuple-element.90.keep_ref.refs_0_, ...), custom_call_target="tpu_custom_call" | custom-call | bytes 2588672 | tf_op jit(solution)/shard_map/pallas_call | solution.py:316
  (44 shorter events, 10.1 us)
Async XLA Ops:
  2.1 9.9 %collective-permute-start.3 = (bf16[2,8,16,128]{3,2,1,0:T(8,128)(2,1)S(1)}, bf16[2,8,16,128]{3,2,1,0:T(8,128)(2,1)S(1)}, u32[]{:S(2)}, u32[]{:S(2)}) collective-permute-start(bf16[2,8,16,128]{3,2,1,0:T(8,128)(2,1)S(1)} %get-tuple-element.58), channel_id=1, source_target_pairs={{0,8},{1,9},{2,10},{3,11},{4,12},{5,13},{6,14},{7,15},{8,0},{9,1},... | collective-permute-start | bytes 196616 | tf_op jit(solution)/shard_map/ppermute | solution.py:339
  6.2 8.7 %collective-permute-start.4 = (bf16[2,8,16,128]{3,2,1,0:T(8,128)(2,1)S(1)}, bf16[2,8,16,128]{3,2,1,0:T(8,128)(2,1)S(1)}, u32[]{:S(2)}, u32[]{:S(2)}) collective-permute-start(bf16[2,8,16,128]{3,2,1,0:T(8,128)(2,1)S(1)} %get-tuple-element.59), channel_id=1, source_target_pairs={{0,13},{1,12},{2,15},{3,14},{4,9},{5,8},{6,11},{7,10},{8,5},{9,4},... | collective-permute-start | bytes 196616 | tf_op jit(solution)/shard_map/ppermute | solution.py:339
  8.5 13.7 %collective-permute-start = (bf16[2,2,8,16,128]{4,3,2,1,0:T(8,128)(2,1)S(1)}, bf16[2,2,8,16,128]{4,3,2,1,0:T(8,128)(2,1)S(1)}, u32[]{:S(2)}, u32[]{:S(2)}) collective-permute-start(bf16[2,2,8,16,128]{4,3,2,1,0:T(8,128)(2,1)S(1)} %get-tuple-element.55), channel_id=1, source_target_pairs={{0,5},{1,4},{2,7},{3,6},{4,1},{5,0},{6,3},{7,2},{8,13},{9,12},{10,... | collective-permute-start | bytes 393224 | tf_op jit(solution)/shard_map/ppermute | solution.py:339
  8.7 13.5 %collective-permute-start.1 = (bf16[2,2,8,16,128]{4,3,2,1,0:T(8,128)(2,1)S(1)}, bf16[2,2,8,16,128]{4,3,2,1,0:T(8,128)(2,1)S(1)}, u32[]{:S(2)}, u32[]{:S(2)}) collective-permute-start(bf16[2,2,8,16,128]{4,3,2,1,0:T(8,128)(2,1)S(1)} %get-tuple-element.56), channel_id=1, source_target_pairs={{0,4},{1,5},{2,6},{3,7},{4,0},{5,1},{6,2},{7,3},{8,12},{9,13},{10,... | collective-permute-start | bytes 393224 | tf_op jit(solution)/shard_map/ppermute | solution.py:339
  10.4 11.7 %collective-permute-start.2 = (bf16[2,2,8,16,128]{4,3,2,1,0:T(8,128)(2,1)S(1)}, bf16[2,2,8,16,128]{4,3,2,1,0:T(8,128)(2,1)S(1)}, u32[]{:S(2)}, u32[]{:S(2)}) collective-permute-start(bf16[2,2,8,16,128]{4,3,2,1,0:T(8,128)(2,1)S(1)} %get-tuple-element.57), channel_id=1, source_target_pairs={{0,1},{1,0},{2,3},{3,2},{4,5},{5,4},{6,7},{7,6},{8,9},{9,8},{10,11... | collective-permute-start | bytes 393224 | tf_op jit(solution)/shard_map/ppermute | solution.py:339
  11.9 8.3 %collective-permute-start.5 = (bf16[2,8,16,128]{3,2,1,0:T(8,128)(2,1)S(1)}, bf16[2,8,16,128]{3,2,1,0:T(8,128)(2,1)S(1)}, u32[]{:S(2)}, u32[]{:S(2)}) collective-permute-start(bf16[2,8,16,128]{3,2,1,0:T(8,128)(2,1)S(1)} %get-tuple-element.60), channel_id=1, source_target_pairs={{0,12},{1,13},{2,14},{3,15},{4,8},{5,9},{6,10},{7,11},{8,4},{9,5},... | collective-permute-start | bytes 196616 | tf_op jit(solution)/shard_map/ppermute | solution.py:339
  14.8 7.3 %collective-permute-start.6 = (bf16[2,8,16,128]{3,2,1,0:T(8,128)(2,1)S(1)}, bf16[2,8,16,128]{3,2,1,0:T(8,128)(2,1)S(1)}, u32[]{:S(2)}, u32[]{:S(2)}) collective-permute-start(bf16[2,8,16,128]{3,2,1,0:T(8,128)(2,1)S(1)} %get-tuple-element.61), channel_id=1, source_target_pairs={{0,9},{1,8},{2,11},{3,10},{4,13},{5,12},{6,15},{7,14},{8,1},{9,0},... | collective-permute-start | bytes 196616 | tf_op jit(solution)/shard_map/ppermute | solution.py:339
  22.3 2.0 %collective-permute-start.7 = (bf16[8,2,8,16,128]{4,3,2,1,0:T(8,128)(2,1)S(1)}, bf16[8,2,8,16,128]{4,3,2,1,0:T(8,128)(2,1)S(1)}, u32[]{:S(2)}, u32[]{:S(2)}) collective-permute-start(bf16[8,2,8,16,128]{4,3,2,1,0:T(8,128)(2,1)S(1)} %shard_map.85), channel_id=1, source_target_pairs={{0,2},{1,3},{2,0},{3,1},{4,6},{5,7},{6,4},{7,5},{8,10},{9,11},{10,... | collective-permute-start | bytes 1572872 | tf_op jit(solution)/shard_map/ppermute | solution.py:339
  25.1 4.3 %collective-permute-start.10 = (bf16[2,8,16,128]{3,2,1,0:T(8,128)(2,1)S(1)}, bf16[2,8,16,128]{3,2,1,0:T(8,128)(2,1)S(1)}, u32[]{:S(2)}, u32[]{:S(2)}) collective-permute-start(bf16[2,8,16,128]{3,2,1,0:T(8,128)(2,1)S(1)} %get-tuple-element.77), channel_id=1, source_target_pairs={{0,1},{1,0},{2,3},{3,2},{4,5},{5,4},{6,7},{7,6},{8,9},{9,8},{10,11... | collective-permute-start | bytes 196616 | tf_op jit(solution)/shard_map/ppermute | solution.py:339
  26.2 5.5 %collective-permute-start.8 = (bf16[2,8,16,128]{3,2,1,0:T(8,128)(2,1)S(1)}, bf16[2,8,16,128]{3,2,1,0:T(8,128)(2,1)S(1)}, u32[]{:S(2)}, u32[]{:S(2)}) collective-permute-start(bf16[2,8,16,128]{3,2,1,0:T(8,128)(2,1)S(1)} %get-tuple-element.75), channel_id=1, source_target_pairs={{0,5},{1,4},{2,7},{3,6},{4,1},{5,0},{6,3},{7,2},{8,13},{9,12},{10,... | collective-permute-start | bytes 196616 | tf_op jit(solution)/shard_map/ppermute | solution.py:339
  26.5 5.4 %collective-permute-start.9 = (bf16[2,8,16,128]{3,2,1,0:T(8,128)(2,1)S(1)}, bf16[2,8,16,128]{3,2,1,0:T(8,128)(2,1)S(1)}, u32[]{:S(2)}, u32[]{:S(2)}) collective-permute-start(bf16[2,8,16,128]{3,2,1,0:T(8,128)(2,1)S(1)} %get-tuple-element.76), channel_id=1, source_target_pairs={{0,4},{1,5},{2,6},{3,7},{4,0},{5,1},{6,2},{7,3},{8,12},{9,13},{10,... | collective-permute-start | bytes 196616 | tf_op jit(solution)/shard_map/ppermute | solution.py:339
  33.0 1.6 %collective-permute-start.11 = (bf16[4,16,16,128]{3,2,1,0:T(8,128)(2,1)S(1)}, bf16[4,16,16,128]{3,2,1,0:T(8,128)(2,1)S(1)}, u32[]{:S(2)}, u32[]{:S(2)}) collective-permute-start(bf16[4,16,16,128]{3,2,1,0:T(8,128)(2,1)S(1)} %get-tuple-element.80), channel_id=1, source_target_pairs={{0,2},{1,3},{2,0},{3,1},{4,6},{5,7},{6,4},{7,5},{8,10},{9,11},{10,... | collective-permute-start | bytes 786440 | tf_op jit(solution)/shard_map/ppermute | solution.py:339
  34.7 7.3 %collective-permute-start.12 = (bf16[2,16,16,128]{3,2,1,0:T(8,128)(2,1)S(1)}, bf16[2,16,16,128]{3,2,1,0:T(8,128)(2,1)S(1)}, u32[]{:S(2)}, u32[]{:S(2)}) collective-permute-start(bf16[2,16,16,128]{3,2,1,0:T(8,128)(2,1)S(1)} %get-tuple-element.81), channel_id=1, source_target_pairs={{0,5},{1,4},{2,7},{3,6},{4,1},{5,0},{6,3},{7,2},{8,13},{9,12},{10,... | collective-permute-start | bytes 393224 | tf_op jit(solution)/shard_map/ppermute | solution.py:339
  36.2 7.3 %collective-permute-start.13 = (bf16[2,16,16,128]{3,2,1,0:T(8,128)(2,1)S(1)}, bf16[2,16,16,128]{3,2,1,0:T(8,128)(2,1)S(1)}, u32[]{:S(2)}, u32[]{:S(2)}) collective-permute-start(bf16[2,16,16,128]{3,2,1,0:T(8,128)(2,1)S(1)} %get-tuple-element.82), channel_id=1, source_target_pairs={{0,4},{1,5},{2,6},{3,7},{4,0},{5,1},{6,2},{7,3},{8,12},{9,13},{10,... | collective-permute-start | bytes 393224 | tf_op jit(solution)/shard_map/ppermute | solution.py:339
  37.2 6.8 %collective-permute-start.14 = (bf16[2,16,16,128]{3,2,1,0:T(8,128)(2,1)S(1)}, bf16[2,16,16,128]{3,2,1,0:T(8,128)(2,1)S(1)}, u32[]{:S(2)}, u32[]{:S(2)}) collective-permute-start(bf16[2,16,16,128]{3,2,1,0:T(8,128)(2,1)S(1)} %get-tuple-element.83), channel_id=1, source_target_pairs={{0,1},{1,0},{2,3},{3,2},{4,5},{5,4},{6,7},{7,6},{8,9},{9,8},{10,11... | collective-permute-start | bytes 393224 | tf_op jit(solution)/shard_map/ppermute | solution.py:339
  44.5 1.6 %collective-permute-start.15 = (bf16[8,8,16,128]{3,2,1,0:T(8,128)(2,1)S(1)}, bf16[8,8,16,128]{3,2,1,0:T(8,128)(2,1)S(1)}, u32[]{:S(2)}, u32[]{:S(2)}) collective-permute-start(bf16[8,8,16,128]{3,2,1,0:T(8,128)(2,1)S(1)} %get-tuple-element.91), channel_id=1, source_target_pairs={{0,2},{1,3},{2,0},{3,1},{4,6},{5,7},{6,4},{7,5},{8,10},{9,11},{10,... | collective-permute-start | bytes 786440 | tf_op jit(solution)/shard_map/ppermute | solution.py:339
  46.1 15.0 %copy-start.1 = (bf16[128,128]{1,0:T(8,128)(2,1)S(1)}, bf16[128,128]{1,0:T(8,128)(2,1)}, u32[]{:S(2)}) copy-start(bf16[128,128]{1,0:T(8,128)(2,1)} %final_ref.3) | copy-start | bytes 98308
  46.1 7.7 %collective-permute-start.16 = (bf16[2,8,16,128]{3,2,1,0:T(8,128)(2,1)S(1)}, bf16[2,8,16,128]{3,2,1,0:T(8,128)(2,1)S(1)}, u32[]{:S(2)}, u32[]{:S(2)}) collective-permute-start(bf16[2,8,16,128]{3,2,1,0:T(8,128)(2,1)S(1)} %get-tuple-element.92), channel_id=1, source_target_pairs={{0,13},{1,12},{2,15},{3,14},{4,9},{5,8},{6,11},{7,10},{8,5},{9,4},... | collective-permute-start | bytes 196616 | tf_op jit(solution)/shard_map/ppermute | solution.py:339
  48.0 8.4 %collective-permute-start.17 = (bf16[2,8,16,128]{3,2,1,0:T(8,128)(2,1)S(1)}, bf16[2,8,16,128]{3,2,1,0:T(8,128)(2,1)S(1)}, u32[]{:S(2)}, u32[]{:S(2)}) collective-permute-start(bf16[2,8,16,128]{3,2,1,0:T(8,128)(2,1)S(1)} %get-tuple-element.93), channel_id=1, source_target_pairs={{0,12},{1,13},{2,14},{3,15},{4,8},{5,9},{6,10},{7,11},{8,4},{9,5},... | collective-permute-start | bytes 196616 | tf_op jit(solution)/shard_map/ppermute | solution.py:339
  50.5 6.9 %collective-permute-start.18 = (bf16[2,8,16,128]{3,2,1,0:T(8,128)(2,1)S(1)}, bf16[2,8,16,128]{3,2,1,0:T(8,128)(2,1)S(1)}, u32[]{:S(2)}, u32[]{:S(2)}) collective-permute-start(bf16[2,8,16,128]{3,2,1,0:T(8,128)(2,1)S(1)} %get-tuple-element.94), channel_id=1, source_target_pairs={{0,5},{1,4},{2,7},{3,6},{4,1},{5,0},{6,3},{7,2},{8,13},{9,12},{10,... | collective-permute-start | bytes 196616 | tf_op jit(solution)/shard_map/ppermute | solution.py:339
  50.5 10.5 %collective-permute-start.19 = (bf16[2,8,16,128]{3,2,1,0:T(8,128)(2,1)S(1)}, bf16[2,8,16,128]{3,2,1,0:T(8,128)(2,1)S(1)}, u32[]{:S(2)}, u32[]{:S(2)}) collective-permute-start(bf16[2,8,16,128]{3,2,1,0:T(8,128)(2,1)S(1)} %get-tuple-element.95), channel_id=1, source_target_pairs={{0,9},{1,8},{2,11},{3,10},{4,13},{5,12},{6,15},{7,14},{8,1},{9,0},... | collective-permute-start | bytes 196616 | tf_op jit(solution)/shard_map/ppermute | solution.py:339
  53.2 7.8 %collective-permute-start.20 = (bf16[2,8,16,128]{3,2,1,0:T(8,128)(2,1)S(1)}, bf16[2,8,16,128]{3,2,1,0:T(8,128)(2,1)S(1)}, u32[]{:S(2)}, u32[]{:S(2)}) collective-permute-start(bf16[2,8,16,128]{3,2,1,0:T(8,128)(2,1)S(1)} %get-tuple-element.96), channel_id=1, source_target_pairs={{0,8},{1,9},{2,10},{3,11},{4,12},{5,13},{6,14},{7,15},{8,0},{9,1},... | collective-permute-start | bytes 196616 | tf_op jit(solution)/shard_map/ppermute | solution.py:339
  53.9 7.2 %collective-permute-start.21 = (bf16[2,8,16,128]{3,2,1,0:T(8,128)(2,1)S(1)}, bf16[2,8,16,128]{3,2,1,0:T(8,128)(2,1)S(1)}, u32[]{:S(2)}, u32[]{:S(2)}) collective-permute-start(bf16[2,8,16,128]{3,2,1,0:T(8,128)(2,1)S(1)} %get-tuple-element.97), channel_id=1, source_target_pairs={{0,4},{1,5},{2,6},{3,7},{4,0},{5,1},{6,2},{7,3},{8,12},{9,13},{10,... | collective-permute-start | bytes 196616 | tf_op jit(solution)/shard_map/ppermute | solution.py:339
  56.3 4.8 %collective-permute-start.22 = (bf16[2,8,16,128]{3,2,1,0:T(8,128)(2,1)S(1)}, bf16[2,8,16,128]{3,2,1,0:T(8,128)(2,1)S(1)}, u32[]{:S(2)}, u32[]{:S(2)}) collective-permute-start(bf16[2,8,16,128]{3,2,1,0:T(8,128)(2,1)S(1)} %get-tuple-element.98), channel_id=1, source_target_pairs={{0,1},{1,0},{2,3},{3,2},{4,5},{5,4},{6,7},{7,6},{8,9},{9,8},{10,11... | collective-permute-start | bytes 196616 | tf_op jit(solution)/shard_map/ppermute | solution.py:339
  (4 other events, 13.9 us)

commit v11 on v10

--- a/solution.py
+++ b/solution.py
@@ -381,7 +381,7 @@
     pair_t, normed, live = outs[2 * CHIPS :]
     came = exchange_panels(outs[:CHIPS], outs[CHIPS : 2 * CHIPS])
     (weights,) = call(second_weights_kernel, [shape(weights, BF16)], [wide])(in_proj.reshape(-1, hidden))
-    gating, weights, came = lax.optimization_barrier((gate(normed, out_gate)[0], weights, came))
+    (gating,) = gate(normed, out_gate)
 
     scratch = [scratch_tiles(CHIPS, 2 * pairs), scratch_tiles(devices, 2 * pairs), scratch_tiles(CHIPS, 2 * pairs)]
     own, *others = call(functools.partial(outgoing_kernel, cols), per_chip, scratch)(*came)

time: 62.9 us -> 62.9 us (level)
  waiting for transfers between devices: 20.7 us -> 21.5 us
  local copies, waits for them, and re-layouts: 1.29 us -> 0.53 us
    unnamed x10, local copies, waits for them, and re-layouts: 1.29 us -> 0.53 us
    ppermute x23, waiting for transfers between devices: 20.7 us -> 21.5 us  [swap(): return lax.ppermute(values, axes, [(d, d ^ step) for d in range(devices)])]
  transfers between devices with their start and end apart: 23 -> 23, of which waited for: 13 -> 12; matrix products, arithmetic and copies ran while one was open for 0% -> 0% of each run, Pallas kernels for 2% -> 2%
where the time goes in v11:
time: 62.9 us; the launch traced here: 62.7 us
  starting transfers between devices  33.1 us (53%)
  waiting for transfers between devices  21.5 us (34%)
  Pallas kernels  7.44 us (12%)
    ppermute x23, starting transfers between devices, swap(): return lax.ppermute(values, axes, [(d, d ^ step) for d in range(devices)])  33.1 us
    ppermute x23, waiting for transfers between devices, swap(): return lax.ppermute(values, axes, [(d, d ^ step) for d in range(devices)])  21.5 us
    pallas_call x12, Pallas kernels, run(): pl.pallas_call(kernel, out_shape=tuple(out_shape), in_specs=[hbm] * far_a...  7.44 us
  transfers between devices with their start and end apart: 23, of which 12 were waited for; matrix products, arithmetic and copies ran while one was open for 0% of the time, Pallas kernels for 2%

profile of v11, /device:TPU:0, one launch (start us, length us, event | category | flops | bytes accessed | tf_op | source)
XLA Modules:
  0.0 62.7 jit_solution(14211393793594345704)
XLA Ops:
  0.0 2.1 %shard_map.82 = (bf16[2,2,8,16,128]{4,3,2,1,0:T(8,128)(2,1)S(1)}, bf16[2,2,8,16,128]{4,3,2,1,0:T(8,128)(2,1)S(1)}, bf16[2,2,8,16,128]{4,3,2,1,0:T(8,128)(2,1)S(1...) custom-call(f32[1024,128]{1,0:T(8,128)} %bitcast.6, ...), custom_call_target="tpu_custom_call" | custom-call | bytes 2236928 | tf_op jit(solution)/shard_map/pallas_call | solution.py:316
  2.1 4.1 %collective-permute-start.3 = (bf16[2,8,16,128]{3,2,1,0:T(8,128)(2,1)S(1)}, bf16[2,8,16,128]{3,2,1,0:T(8,128)(2,1)S(1)}, u32[]{:S(2)}, u32[]{:S(2)}) collective-permute-start(bf16[2,8,16,128]{3,2,1,0:T(8,128)(2,1)S(1)} %get-tuple-element.48), channel_id=1, source_target_pairs={{0,8},{1,9},{2,10},{3,11},{4,12},{5,13},{6,14},{7,15},{8,0},{9,1},... | collective-permute-start | bytes 196616 | tf_op jit(solution)/shard_map/ppermute | solution.py:339
  6.2 2.3 %collective-permute-start.4 = (bf16[2,8,16,128]{3,2,1,0:T(8,128)(2,1)S(1)}, bf16[2,8,16,128]{3,2,1,0:T(8,128)(2,1)S(1)}, u32[]{:S(2)}, u32[]{:S(2)}) collective-permute-start(bf16[2,8,16,128]{3,2,1,0:T(8,128)(2,1)S(1)} %get-tuple-element.49), channel_id=1, source_target_pairs={{0,13},{1,12},{2,15},{3,14},{4,9},{5,8},{6,11},{7,10},{8,5},{9,4},... | collective-permute-start | bytes 196616 | tf_op jit(solution)/shard_map/ppermute | solution.py:339
  8.7 1.8 %collective-permute-start.1 = (bf16[2,2,8,16,128]{4,3,2,1,0:T(8,128)(2,1)S(1)}, bf16[2,2,8,16,128]{4,3,2,1,0:T(8,128)(2,1)S(1)}, u32[]{:S(2)}, u32[]{:S(2)}) collective-permute-start(bf16[2,2,8,16,128]{4,3,2,1,0:T(8,128)(2,1)S(1)} %get-tuple-element.46), channel_id=1, source_target_pairs={{0,4},{1,5},{2,6},{3,7},{4,0},{5,1},{6,2},{7,3},{8,12},{9,13},{10,... | collective-permute-start | bytes 393224 | tf_op jit(solution)/shard_map/ppermute | solution.py:339
  10.4 1.5 %collective-permute-start.2 = (bf16[2,2,8,16,128]{4,3,2,1,0:T(8,128)(2,1)S(1)}, bf16[2,2,8,16,128]{4,3,2,1,0:T(8,128)(2,1)S(1)}, u32[]{:S(2)}, u32[]{:S(2)}) collective-permute-start(bf16[2,2,8,16,128]{4,3,2,1,0:T(8,128)(2,1)S(1)} %get-tuple-element.47), channel_id=1, source_target_pairs={{0,1},{1,0},{2,3},{3,2},{4,5},{5,4},{6,7},{7,6},{8,9},{9,8},{10,11... | collective-permute-start | bytes 393224 | tf_op jit(solution)/shard_map/ppermute | solution.py:339
  11.9 2.9 %collective-permute-start.5 = (bf16[2,8,16,128]{3,2,1,0:T(8,128)(2,1)S(1)}, bf16[2,8,16,128]{3,2,1,0:T(8,128)(2,1)S(1)}, u32[]{:S(2)}, u32[]{:S(2)}) collective-permute-start(bf16[2,8,16,128]{3,2,1,0:T(8,128)(2,1)S(1)} %get-tuple-element.50), channel_id=1, source_target_pairs={{0,12},{1,13},{2,14},{3,15},{4,8},{5,9},{6,10},{7,11},{8,4},{9,5},... | collective-permute-start | bytes 196616 | tf_op jit(solution)/shard_map/ppermute | solution.py:339
  14.8 1.8 %collective-permute-start.6 = (bf16[2,8,16,128]{3,2,1,0:T(8,128)(2,1)S(1)}, bf16[2,8,16,128]{3,2,1,0:T(8,128)(2,1)S(1)}, u32[]{:S(2)}, u32[]{:S(2)}) collective-permute-start(bf16[2,8,16,128]{3,2,1,0:T(8,128)(2,1)S(1)} %get-tuple-element.51), channel_id=1, source_target_pairs={{0,9},{1,8},{2,11},{3,10},{4,13},{5,12},{6,15},{7,14},{8,1},{9,0},... | collective-permute-start | bytes 196616 | tf_op jit(solution)/shard_map/ppermute | solution.py:339
  16.7 3.6 %collective-permute-done.5.refs_6_ = bf16[2,8,16,128]{3,2,1,0:T(8,128)(2,1)S(1)} collective-permute-done((bf16[2,8,16,128]{3,2,1,0:T(8,128)(2,1)S(1)}, bf16[2,8,16,128]{3,2,1,0:T(8,128)(2,1)S(1)}, u32[]{:S(2)}, u32[]{:S(2)}) %collective-permute-start.5) | collective-permute-done | bytes 65568 | tf_op jit(solution)/shard_map/ppermute | solution.py:339
  20.3 1.9 %collective-permute-done.6.refs_7_ = bf16[2,8,16,128]{3,2,1,0:T(8,128)(2,1)S(1)} collective-permute-done((bf16[2,8,16,128]{3,2,1,0:T(8,128)(2,1)S(1)}, bf16[2,8,16,128]{3,2,1,0:T(8,128)(2,1)S(1)}, u32[]{:S(2)}, u32[]{:S(2)}) %collective-permute-start.6) | collective-permute-done | bytes 65568 | tf_op jit(solution)/shard_map/ppermute | solution.py:339
  22.3 1.9 %collective-permute-done.7.refs_8_ = bf16[8,2,8,16,128]{4,3,2,1,0:T(8,128)(2,1)S(1)} collective-permute-done((bf16[8,2,8,16,128]{4,3,2,1,0:T(8,128)(2,1)S(1)}, bf16[8,2,8,16,128]{4,3,2,1,0:T(8,128)(2,1)S(1)}, u32[]{:S(2)}, u32[]{:S(2)}) %collective-permute-start.7) | collective-permute-done | bytes 524320 | tf_op jit(solution)/shard_map/ppermute | solution.py:339
  25.1 1.1 %collective-permute-start.10 = (bf16[2,8,16,128]{3,2,1,0:T(8,128)(2,1)S(1)}, bf16[2,8,16,128]{3,2,1,0:T(8,128)(2,1)S(1)}, u32[]{:S(2)}, u32[]{:S(2)}) collective-permute-start(bf16[2,8,16,128]{3,2,1,0:T(8,128)(2,1)S(1)} %get-tuple-element.55), channel_id=1, source_target_pairs={{0,1},{1,0},{2,3},{3,2},{4,5},{5,4},{6,7},{7,6},{8,9},{9,8},{10,11... | collective-permute-start | bytes 196616 | tf_op jit(solution)/shard_map/ppermute | solution.py:339
  26.5 2.2 %collective-permute-start.9 = (bf16[2,8,16,128]{3,2,1,0:T(8,128)(2,1)S(1)}, bf16[2,8,16,128]{3,2,1,0:T(8,128)(2,1)S(1)}, u32[]{:S(2)}, u32[]{:S(2)}) collective-permute-start(bf16[2,8,16,128]{3,2,1,0:T(8,128)(2,1)S(1)} %get-tuple-element.54), channel_id=1, source_target_pairs={{0,4},{1,5},{2,6},{3,7},{4,0},{5,1},{6,2},{7,3},{8,12},{9,13},{10,... | collective-permute-start | bytes 196616 | tf_op jit(solution)/shard_map/ppermute | solution.py:339
  29.7 1.9 %collective-permute-done.8.refs_1_ = bf16[2,8,16,128]{3,2,1,0:T(8,128)(2,1)S(1)} collective-permute-done((bf16[2,8,16,128]{3,2,1,0:T(8,128)(2,1)S(1)}, bf16[2,8,16,128]{3,2,1,0:T(8,128)(2,1)S(1)}, u32[]{:S(2)}, u32[]{:S(2)}) %collective-permute-start.8) | collective-permute-done | bytes 65568 | tf_op jit(solution)/shard_map/ppermute | solution.py:339
  31.9 1.2 %shard_map.87 = (bf16[4,16,16,128]{3,2,1,0:T(8,128)(2,1)S(1)}, f32[128,1024]{1,0:T(8,128)S(1)}, bf16[128,1024]{1,0:T(8,128)(2,1)S(1)}) custom-call(f32[16,128]{1,0:T(8,128)S(1)} %get-tuple-element.41.live_ref, bf16[128,512]{1,0:T(8,128)(2,1)S(1)} %shard_map.83.weights, bf16[128,128]{1,0:T(8,128)(2,1)S(1)} %copy-done.3, ...), custom_call_target="tpu_custom_call" | custom-call | bytes 2531328 | tf_op jit(solution)/shard_map/pallas_call | solution.py:316
  34.7 1.6 %collective-permute-start.12 = (bf16[2,16,16,128]{3,2,1,0:T(8,128)(2,1)S(1)}, bf16[2,16,16,128]{3,2,1,0:T(8,128)(2,1)S(1)}, u32[]{:S(2)}, u32[]{:S(2)}) collective-permute-start(bf16[2,16,16,128]{3,2,1,0:T(8,128)(2,1)S(1)} %get-tuple-element.59), channel_id=1, source_target_pairs={{0,5},{1,4},{2,7},{3,6},{4,1},{5,0},{6,3},{7,2},{8,13},{9,12},{10,... | collective-permute-start | bytes 393224 | tf_op jit(solution)/shard_map/ppermute | solution.py:339
  38.5 3.5 %collective-permute-done.12.refs_2_ = bf16[2,16,16,128]{3,2,1,0:T(8,128)(2,1)S(1)} collective-permute-done((bf16[2,16,16,128]{3,2,1,0:T(8,128)(2,1)S(1)}, bf16[2,16,16,128]{3,2,1,0:T(8,128)(2,1)S(1)}, u32[]{:S(2)}, u32[]{:S(2)}) %collective-permute-start.12) | collective-permute-done | bytes 131104 | tf_op jit(solution)/shard_map/ppermute | solution.py:339
  42.0 1.6 %collective-permute-done.13.refs_3_ = bf16[2,16,16,128]{3,2,1,0:T(8,128)(2,1)S(1)} collective-permute-done((bf16[2,16,16,128]{3,2,1,0:T(8,128)(2,1)S(1)}, bf16[2,16,16,128]{3,2,1,0:T(8,128)(2,1)S(1)}, u32[]{:S(2)}, u32[]{:S(2)}) %collective-permute-start.13) | collective-permute-done | bytes 131104 | tf_op jit(solution)/shard_map/ppermute | solution.py:339
  44.6 1.5 %collective-permute-done.15.got_ref.refs_1_ = bf16[8,8,16,128]{3,2,1,0:T(8,128)(2,1)S(1)} collective-permute-done((bf16[8,8,16,128]{3,2,1,0:T(8,128)(2,1)S(1)}, bf16[8,8,16,128]{3,2,1,0:T(8,128)(2,1)S(1)}, u32[]{:S(2)}, u32[]{:S(2)}) %collective-permute-start.15) | collective-permute-done | bytes 262176 | tf_op jit(solution)/shard_map/ppermute | solution.py:339
  46.1 1.8 %collective-permute-start.16 = (bf16[2,8,16,128]{3,2,1,0:T(8,128)(2,1)S(1)}, bf16[2,8,16,128]{3,2,1,0:T(8,128)(2,1)S(1)}, u32[]{:S(2)}, u32[]{:S(2)}) collective-permute-start(bf16[2,8,16,128]{3,2,1,0:T(8,128)(2,1)S(1)} %get-tuple-element.70), channel_id=1, source_target_pairs={{0,13},{1,12},{2,15},{3,14},{4,9},{5,8},{6,11},{7,10},{8,5},{9,4},... | collective-permute-start | bytes 196616 | tf_op jit(solution)/shard_map/ppermute | solution.py:339
  48.0 2.5 %collective-permute-start.17 = (bf16[2,8,16,128]{3,2,1,0:T(8,128)(2,1)S(1)}, bf16[2,8,16,128]{3,2,1,0:T(8,128)(2,1)S(1)}, u32[]{:S(2)}, u32[]{:S(2)}) collective-permute-start(bf16[2,8,16,128]{3,2,1,0:T(8,128)(2,1)S(1)} %get-tuple-element.71), channel_id=1, source_target_pairs={{0,12},{1,13},{2,14},{3,15},{4,8},{5,9},{6,10},{7,11},{8,4},{9,5},... | collective-permute-start | bytes 196616 | tf_op jit(solution)/shard_map/ppermute | solution.py:339
  50.5 2.8 %collective-permute-start.19 = (bf16[2,8,16,128]{3,2,1,0:T(8,128)(2,1)S(1)}, bf16[2,8,16,128]{3,2,1,0:T(8,128)(2,1)S(1)}, u32[]{:S(2)}, u32[]{:S(2)}) collective-permute-start(bf16[2,8,16,128]{3,2,1,0:T(8,128)(2,1)S(1)} %get-tuple-element.73), channel_id=1, source_target_pairs={{0,9},{1,8},{2,11},{3,10},{4,13},{5,12},{6,15},{7,14},{8,1},{9,0},... | collective-permute-start | bytes 196616 | tf_op jit(solution)/shard_map/ppermute | solution.py:339
  53.9 2.5 %collective-permute-start.21 = (bf16[2,8,16,128]{3,2,1,0:T(8,128)(2,1)S(1)}, bf16[2,8,16,128]{3,2,1,0:T(8,128)(2,1)S(1)}, u32[]{:S(2)}, u32[]{:S(2)}) collective-permute-start(bf16[2,8,16,128]{3,2,1,0:T(8,128)(2,1)S(1)} %get-tuple-element.75), channel_id=1, source_target_pairs={{0,4},{1,5},{2,6},{3,7},{4,0},{5,1},{6,2},{7,3},{8,12},{9,13},{10,... | collective-permute-start | bytes 196616 | tf_op jit(solution)/shard_map/ppermute | solution.py:339
  57.4 3.6 %collective-permute-done.19.refs_5_ = bf16[2,8,16,128]{3,2,1,0:T(8,128)(2,1)S(1)} collective-permute-done((bf16[2,8,16,128]{3,2,1,0:T(8,128)(2,1)S(1)}, bf16[2,8,16,128]{3,2,1,0:T(8,128)(2,1)S(1)}, u32[]{:S(2)}, u32[]{:S(2)}) %collective-permute-start.19) | collective-permute-done | bytes 65568 | tf_op jit(solution)/shard_map/ppermute | solution.py:339
  61.1 1.5 %shard_map.93 = f32[1024,128]{1,0:T(8,128)} custom-call(f32[128,1024]{1,0:T(8,128)S(1)} %get-tuple-element.56.middle_ref, f32[128,1024]{1,0:T(8,128)S(1)} %shard_map.88.gating_ref, bf16[128,128]{1,0:T(8,128)(2,1)S(1)} %copy-done.1, bf16[8,8,16,128]{3,2,1,0:T(8,128)(2,1)S(1)} %get-tuple-element.68.keep_ref.refs_0_, ...), custom_call_target="tpu_custom_call" | custom-call | bytes 2588672 | tf_op jit(solution)/shard_map/pallas_call | solution.py:316
  (44 shorter events, 9.5 us)
Async XLA Ops:
  2.1 9.9 %collective-permute-start.3 = (bf16[2,8,16,128]{3,2,1,0:T(8,128)(2,1)S(1)}, bf16[2,8,16,128]{3,2,1,0:T(8,128)(2,1)S(1)}, u32[]{:S(2)}, u32[]{:S(2)}) collective-permute-start(bf16[2,8,16,128]{3,2,1,0:T(8,128)(2,1)S(1)} %get-tuple-element.48), channel_id=1, source_target_pairs={{0,8},{1,9},{2,10},{3,11},{4,12},{5,13},{6,14},{7,15},{8,0},{9,1},... | collective-permute-start | bytes 196616 | tf_op jit(solution)/shard_map/ppermute | solution.py:339
  6.2 8.7 %collective-permute-start.4 = (bf16[2,8,16,128]{3,2,1,0:T(8,128)(2,1)S(1)}, bf16[2,8,16,128]{3,2,1,0:T(8,128)(2,1)S(1)}, u32[]{:S(2)}, u32[]{:S(2)}) collective-permute-start(bf16[2,8,16,128]{3,2,1,0:T(8,128)(2,1)S(1)} %get-tuple-element.49), channel_id=1, source_target_pairs={{0,13},{1,12},{2,15},{3,14},{4,9},{5,8},{6,11},{7,10},{8,5},{9,4},... | collective-permute-start | bytes 196616 | tf_op jit(solution)/shard_map/ppermute | solution.py:339
  8.5 13.7 %collective-permute-start = (bf16[2,2,8,16,128]{4,3,2,1,0:T(8,128)(2,1)S(1)}, bf16[2,2,8,16,128]{4,3,2,1,0:T(8,128)(2,1)S(1)}, u32[]{:S(2)}, u32[]{:S(2)}) collective-permute-start(bf16[2,2,8,16,128]{4,3,2,1,0:T(8,128)(2,1)S(1)} %get-tuple-element.45), channel_id=1, source_target_pairs={{0,5},{1,4},{2,7},{3,6},{4,1},{5,0},{6,3},{7,2},{8,13},{9,12},{10,... | collective-permute-start | bytes 393224 | tf_op jit(solution)/shard_map/ppermute | solution.py:339
  8.7 13.5 %collective-permute-start.1 = (bf16[2,2,8,16,128]{4,3,2,1,0:T(8,128)(2,1)S(1)}, bf16[2,2,8,16,128]{4,3,2,1,0:T(8,128)(2,1)S(1)}, u32[]{:S(2)}, u32[]{:S(2)}) collective-permute-start(bf16[2,2,8,16,128]{4,3,2,1,0:T(8,128)(2,1)S(1)} %get-tuple-element.46), channel_id=1, source_target_pairs={{0,4},{1,5},{2,6},{3,7},{4,0},{5,1},{6,2},{7,3},{8,12},{9,13},{10,... | collective-permute-start | bytes 393224 | tf_op jit(solution)/shard_map/ppermute | solution.py:339
  10.4 11.7 %collective-permute-start.2 = (bf16[2,2,8,16,128]{4,3,2,1,0:T(8,128)(2,1)S(1)}, bf16[2,2,8,16,128]{4,3,2,1,0:T(8,128)(2,1)S(1)}, u32[]{:S(2)}, u32[]{:S(2)}) collective-permute-start(bf16[2,2,8,16,128]{4,3,2,1,0:T(8,128)(2,1)S(1)} %get-tuple-element.47), channel_id=1, source_target_pairs={{0,1},{1,0},{2,3},{3,2},{4,5},{5,4},{6,7},{7,6},{8,9},{9,8},{10,11... | collective-permute-start | bytes 393224 | tf_op jit(solution)/shard_map/ppermute | solution.py:339
  11.9 8.3 %collective-permute-start.5 = (bf16[2,8,16,128]{3,2,1,0:T(8,128)(2,1)S(1)}, bf16[2,8,16,128]{3,2,1,0:T(8,128)(2,1)S(1)}, u32[]{:S(2)}, u32[]{:S(2)}) collective-permute-start(bf16[2,8,16,128]{3,2,1,0:T(8,128)(2,1)S(1)} %get-tuple-element.50), channel_id=1, source_target_pairs={{0,12},{1,13},{2,14},{3,15},{4,8},{5,9},{6,10},{7,11},{8,4},{9,5},... | collective-permute-start | bytes 196616 | tf_op jit(solution)/shard_map/ppermute | solution.py:339
  14.8 7.3 %collective-permute-start.6 = (bf16[2,8,16,128]{3,2,1,0:T(8,128)(2,1)S(1)}, bf16[2,8,16,128]{3,2,1,0:T(8,128)(2,1)S(1)}, u32[]{:S(2)}, u32[]{:S(2)}) collective-permute-start(bf16[2,8,16,128]{3,2,1,0:T(8,128)(2,1)S(1)} %get-tuple-element.51), channel_id=1, source_target_pairs={{0,9},{1,8},{2,11},{3,10},{4,13},{5,12},{6,15},{7,14},{8,1},{9,0},... | collective-permute-start | bytes 196616 | tf_op jit(solution)/shard_map/ppermute | solution.py:339
  22.3 2.0 %collective-permute-start.7 = (bf16[8,2,8,16,128]{4,3,2,1,0:T(8,128)(2,1)S(1)}, bf16[8,2,8,16,128]{4,3,2,1,0:T(8,128)(2,1)S(1)}, u32[]{:S(2)}, u32[]{:S(2)}) collective-permute-start(bf16[8,2,8,16,128]{4,3,2,1,0:T(8,128)(2,1)S(1)} %shard_map.85), channel_id=1, source_target_pairs={{0,2},{1,3},{2,0},{3,1},{4,6},{5,7},{6,4},{7,5},{8,10},{9,11},{10,... | collective-permute-start | bytes 1572872 | tf_op jit(solution)/shard_map/ppermute | solution.py:339
  25.1 4.6 %collective-permute-start.10 = (bf16[2,8,16,128]{3,2,1,0:T(8,128)(2,1)S(1)}, bf16[2,8,16,128]{3,2,1,0:T(8,128)(2,1)S(1)}, u32[]{:S(2)}, u32[]{:S(2)}) collective-permute-start(bf16[2,8,16,128]{3,2,1,0:T(8,128)(2,1)S(1)} %get-tuple-element.55), channel_id=1, source_target_pairs={{0,1},{1,0},{2,3},{3,2},{4,5},{5,4},{6,7},{7,6},{8,9},{9,8},{10,11... | collective-permute-start | bytes 196616 | tf_op jit(solution)/shard_map/ppermute | solution.py:339
  26.2 5.5 %collective-permute-start.8 = (bf16[2,8,16,128]{3,2,1,0:T(8,128)(2,1)S(1)}, bf16[2,8,16,128]{3,2,1,0:T(8,128)(2,1)S(1)}, u32[]{:S(2)}, u32[]{:S(2)}) collective-permute-start(bf16[2,8,16,128]{3,2,1,0:T(8,128)(2,1)S(1)} %get-tuple-element.53), channel_id=1, source_target_pairs={{0,5},{1,4},{2,7},{3,6},{4,1},{5,0},{6,3},{7,2},{8,13},{9,12},{10,... | collective-permute-start | bytes 196616 | tf_op jit(solution)/shard_map/ppermute | solution.py:339
  26.5 5.4 %collective-permute-start.9 = (bf16[2,8,16,128]{3,2,1,0:T(8,128)(2,1)S(1)}, bf16[2,8,16,128]{3,2,1,0:T(8,128)(2,1)S(1)}, u32[]{:S(2)}, u32[]{:S(2)}) collective-permute-start(bf16[2,8,16,128]{3,2,1,0:T(8,128)(2,1)S(1)} %get-tuple-element.54), channel_id=1, source_target_pairs={{0,4},{1,5},{2,6},{3,7},{4,0},{5,1},{6,2},{7,3},{8,12},{9,13},{10,... | collective-permute-start | bytes 196616 | tf_op jit(solution)/shard_map/ppermute | solution.py:339
  33.0 1.6 %collective-permute-start.11 = (bf16[4,16,16,128]{3,2,1,0:T(8,128)(2,1)S(1)}, bf16[4,16,16,128]{3,2,1,0:T(8,128)(2,1)S(1)}, u32[]{:S(2)}, u32[]{:S(2)}) collective-permute-start(bf16[4,16,16,128]{3,2,1,0:T(8,128)(2,1)S(1)} %get-tuple-element.58), channel_id=1, source_target_pairs={{0,2},{1,3},{2,0},{3,1},{4,6},{5,7},{6,4},{7,5},{8,10},{9,11},{10,... | collective-permute-start | bytes 786440 | tf_op jit(solution)/shard_map/ppermute | solution.py:339
  34.7 7.3 %collective-permute-start.12 = (bf16[2,16,16,128]{3,2,1,0:T(8,128)(2,1)S(1)}, bf16[2,16,16,128]{3,2,1,0:T(8,128)(2,1)S(1)}, u32[]{:S(2)}, u32[]{:S(2)}) collective-permute-start(bf16[2,16,16,128]{3,2,1,0:T(8,128)(2,1)S(1)} %get-tuple-element.59), channel_id=1, source_target_pairs={{0,5},{1,4},{2,7},{3,6},{4,1},{5,0},{6,3},{7,2},{8,13},{9,12},{10,... | collective-permute-start | bytes 393224 | tf_op jit(solution)/shard_map/ppermute | solution.py:339
  36.2 7.3 %collective-permute-start.13 = (bf16[2,16,16,128]{3,2,1,0:T(8,128)(2,1)S(1)}, bf16[2,16,16,128]{3,2,1,0:T(8,128)(2,1)S(1)}, u32[]{:S(2)}, u32[]{:S(2)}) collective-permute-start(bf16[2,16,16,128]{3,2,1,0:T(8,128)(2,1)S(1)} %get-tuple-element.60), channel_id=1, source_target_pairs={{0,4},{1,5},{2,6},{3,7},{4,0},{5,1},{6,2},{7,3},{8,12},{9,13},{10,... | collective-permute-start | bytes 393224 | tf_op jit(solution)/shard_map/ppermute | solution.py:339
  37.2 6.8 %collective-permute-start.14 = (bf16[2,16,16,128]{3,2,1,0:T(8,128)(2,1)S(1)}, bf16[2,16,16,128]{3,2,1,0:T(8,128)(2,1)S(1)}, u32[]{:S(2)}, u32[]{:S(2)}) collective-permute-start(bf16[2,16,16,128]{3,2,1,0:T(8,128)(2,1)S(1)} %get-tuple-element.61), channel_id=1, source_target_pairs={{0,1},{1,0},{2,3},{3,2},{4,5},{5,4},{6,7},{7,6},{8,9},{9,8},{10,11... | collective-permute-start | bytes 393224 | tf_op jit(solution)/shard_map/ppermute | solution.py:339
  44.5 1.6 %collective-permute-start.15 = (bf16[8,8,16,128]{3,2,1,0:T(8,128)(2,1)S(1)}, bf16[8,8,16,128]{3,2,1,0:T(8,128)(2,1)S(1)}, u32[]{:S(2)}, u32[]{:S(2)}) collective-permute-start(bf16[8,8,16,128]{3,2,1,0:T(8,128)(2,1)S(1)} %get-tuple-element.69), channel_id=1, source_target_pairs={{0,2},{1,3},{2,0},{3,1},{4,6},{5,7},{6,4},{7,5},{8,10},{9,11},{10,... | collective-permute-start | bytes 786440 | tf_op jit(solution)/shard_map/ppermute | solution.py:339
  46.1 15.0 %copy-start.1 = (bf16[128,128]{1,0:T(8,128)(2,1)S(1)}, bf16[128,128]{1,0:T(8,128)(2,1)}, u32[]{:S(2)}) copy-start(bf16[128,128]{1,0:T(8,128)(2,1)} %final_ref.3) | copy-start | bytes 98308
  46.1 7.7 %collective-permute-start.16 = (bf16[2,8,16,128]{3,2,1,0:T(8,128)(2,1)S(1)}, bf16[2,8,16,128]{3,2,1,0:T(8,128)(2,1)S(1)}, u32[]{:S(2)}, u32[]{:S(2)}) collective-permute-start(bf16[2,8,16,128]{3,2,1,0:T(8,128)(2,1)S(1)} %get-tuple-element.70), channel_id=1, source_target_pairs={{0,13},{1,12},{2,15},{3,14},{4,9},{5,8},{6,11},{7,10},{8,5},{9,4},... | collective-permute-start | bytes 196616 | tf_op jit(solution)/shard_map/ppermute | solution.py:339
  48.0 8.4 %collective-permute-start.17 = (bf16[2,8,16,128]{3,2,1,0:T(8,128)(2,1)S(1)}, bf16[2,8,16,128]{3,2,1,0:T(8,128)(2,1)S(1)}, u32[]{:S(2)}, u32[]{:S(2)}) collective-permute-start(bf16[2,8,16,128]{3,2,1,0:T(8,128)(2,1)S(1)} %get-tuple-element.71), channel_id=1, source_target_pairs={{0,12},{1,13},{2,14},{3,15},{4,8},{5,9},{6,10},{7,11},{8,4},{9,5},... | collective-permute-start | bytes 196616 | tf_op jit(solution)/shard_map/ppermute | solution.py:339
  50.5 6.9 %collective-permute-start.18 = (bf16[2,8,16,128]{3,2,1,0:T(8,128)(2,1)S(1)}, bf16[2,8,16,128]{3,2,1,0:T(8,128)(2,1)S(1)}, u32[]{:S(2)}, u32[]{:S(2)}) collective-permute-start(bf16[2,8,16,128]{3,2,1,0:T(8,128)(2,1)S(1)} %get-tuple-element.72), channel_id=1, source_target_pairs={{0,5},{1,4},{2,7},{3,6},{4,1},{5,0},{6,3},{7,2},{8,13},{9,12},{10,... | collective-permute-start | bytes 196616 | tf_op jit(solution)/shard_map/ppermute | solution.py:339
  50.5 10.5 %collective-permute-start.19 = (bf16[2,8,16,128]{3,2,1,0:T(8,128)(2,1)S(1)}, bf16[2,8,16,128]{3,2,1,0:T(8,128)(2,1)S(1)}, u32[]{:S(2)}, u32[]{:S(2)}) collective-permute-start(bf16[2,8,16,128]{3,2,1,0:T(8,128)(2,1)S(1)} %get-tuple-element.73), channel_id=1, source_target_pairs={{0,9},{1,8},{2,11},{3,10},{4,13},{5,12},{6,15},{7,14},{8,1},{9,0},... | collective-permute-start | bytes 196616 | tf_op jit(solution)/shard_map/ppermute | solution.py:339
  53.3 7.8 %collective-permute-start.20 = (bf16[2,8,16,128]{3,2,1,0:T(8,128)(2,1)S(1)}, bf16[2,8,16,128]{3,2,1,0:T(8,128)(2,1)S(1)}, u32[]{:S(2)}, u32[]{:S(2)}) collective-permute-start(bf16[2,8,16,128]{3,2,1,0:T(8,128)(2,1)S(1)} %get-tuple-element.74), channel_id=1, source_target_pairs={{0,8},{1,9},{2,10},{3,11},{4,12},{5,13},{6,14},{7,15},{8,0},{9,1},... | collective-permute-start | bytes 196616 | tf_op jit(solution)/shard_map/ppermute | solution.py:339
  53.9 7.2 %collective-permute-start.21 = (bf16[2,8,16,128]{3,2,1,0:T(8,128)(2,1)S(1)}, bf16[2,8,16,128]{3,2,1,0:T(8,128)(2,1)S(1)}, u32[]{:S(2)}, u32[]{:S(2)}) collective-permute-start(bf16[2,8,16,128]{3,2,1,0:T(8,128)(2,1)S(1)} %get-tuple-element.75), channel_id=1, source_target_pairs={{0,4},{1,5},{2,6},{3,7},{4,0},{5,1},{6,2},{7,3},{8,12},{9,13},{10,... | collective-permute-start | bytes 196616 | tf_op jit(solution)/shard_map/ppermute | solution.py:339
  56.3 4.8 %collective-permute-start.22 = (bf16[2,8,16,128]{3,2,1,0:T(8,128)(2,1)S(1)}, bf16[2,8,16,128]{3,2,1,0:T(8,128)(2,1)S(1)}, u32[]{:S(2)}, u32[]{:S(2)}) collective-permute-start(bf16[2,8,16,128]{3,2,1,0:T(8,128)(2,1)S(1)} %get-tuple-element.76), channel_id=1, source_target_pairs={{0,1},{1,0},{2,3},{3,2},{4,5},{5,4},{6,7},{7,6},{8,9},{9,8},{10,11... | collective-permute-start | bytes 196616 | tf_op jit(solution)/shard_map/ppermute | solution.py:339
  (4 other events, 14.2 us)
